TPU v7x, 128 devices: a whole 4x4x4 slice. The times are simulated.
128 devices in a mesh: seq: 32 (over z, y, core), mp: 4 (over x).
Axes of the slice: x: 4, y: 4, z: 4, core: 2. Of those that a mesh axis runs over, the one named last changes fastest.
Arguments:
- tokens: bfloat16 [4096, 2048], P('seq'), may hold values from -6 to 6
- cotangent: bfloat16 [4096, 2048], P('seq'), may hold values from -6 to 6
- resets: int32 [4096], P('seq'), may hold values from 0 to 1, as said below
- norm1_gain: bfloat16 [2048], P('seq'), may hold values from 0.5 to 1.5
- in_weight: bfloat16 [2048, 3, 2048], P('seq', None, 'mp'), may hold values from -0.125 to 0.125
- conv_weight: float32 [3, 3, 2048], P(None, None, 'mp'), may hold values from -3 to 3
- pole_decay: float32 [16, 2048], P(None, 'mp'), may hold values from 7.3242187e-06 to 0.04
- pole_angle: float32 [16, 2048], P(None, 'mp'), may hold values from -3.140625 to 3.140625
- residue_re: float32 [16, 2048], P(None, 'mp'), may hold values from -2 to 2
- residue_im: float32 [16, 2048], P(None, 'mp'), may hold values from -2 to 2
- out_weight: bfloat16 [2048, 2048], P('seq', 'mp'), may hold values from -0.125 to 0.125
- norm2_gain: bfloat16 [2048], P('seq'), may hold values from 0.5 to 1.5
- gate_weight: bfloat16 [2048, 5632], P('seq', 'mp'), may hold values from -0.125 to 0.125
- up_weight: bfloat16 [2048, 5632], P('seq', 'mp'), may hold values from -0.125 to 0.125
- down_weight: bfloat16 [2048, 5632], P('seq', 'mp'), may hold values from -0.078125 to 0.078125
Outputs:
- block_out: bfloat16 [4096, 2048], P('seq')
- grad_tokens: bfloat16 [4096, 2048], P('seq')
- grad_norm1_gain: float32 [2048], P('seq')
- grad_in_weight: float32 [2048, 3, 2048], P('seq', None, 'mp')
- grad_conv_weight: float32 [3, 3, 2048], P(None, None, 'mp')
- grad_pole_decay: float32 [16, 2048], P(None, 'mp')
- grad_pole_angle: float32 [16, 2048], P(None, 'mp')
- grad_residue_re: float32 [16, 2048], P(None, 'mp')
- grad_residue_im: float32 [16, 2048], P(None, 'mp')
- grad_out_weight: float32 [2048, 2048], P('seq', 'mp')
- grad_norm2_gain: float32 [2048], P('seq')
- grad_gate_weight: float32 [2048, 5632], P('seq', 'mp')
- grad_up_weight: float32 [2048, 5632], P('seq', 'mp')
- grad_down_weight: float32 [2048, 5632], P('seq', 'mp')
Inputs may be any that keep to these rules, and one draw needn't show every extreme that they name: resets[0] is 1. One document begins among the first 64 tokens and its successor begins among the last 64 tokens, with no reset in between; further resets fall only before or after that document.
All inputs are finite; a program needn't handle non-finite values.
Results may differ from a plain program's by a relative error of at most 0.025.
Values may be sent and summed in bfloat16 or wider, within the bound.
A program may use at most 192 MiB of HBM per device.

v0:
```python
import jax
import jax.numpy as jnp
from jax import lax
from jax.sharding import PartitionSpec as P

EPSILON = 1e-05


def passed_along(value, axis, steps):
    count = lax.axis_size(axis)
    first, last = (max(0, -steps), min(count, count - steps))
    return lax.ppermute(value, axis, [(source, source + steps) for source in range(first, last)])


def entering_2(part, axis, combine, identity, reverse):
    count = lax.axis_size(axis)
    place = lax.axis_index(axis)
    ahead = count - 1 - place if reverse else place
    gathered = jax.tree.map(lambda a: lax.all_gather(a, axis), part)
    state = jax.tree.map(lambda a, e: jnp.zeros_like(a) + jnp.asarray(e, a.dtype), part, identity)

    def one(step, state):
        source = count - 1 - step if reverse else step
        return combine(
            state, jax.tree.map(lambda a: lax.dynamic_index_in_dim(a, source, 0, False), gathered)
        )

    return lax.fori_loop(0, ahead, one, state)


def chain_combine(first, second):
    ar, ai, sr, si = first
    br, bi, tr, ti = second
    return (ar * br - ai * bi, ar * bi + ai * br, br * sr - bi * si + tr, br * si + bi * sr + ti)


def chain_unit(shape, lead):
    zeros = jnp.zeros(lead + shape, jnp.float32)
    return (jnp.ones(lead + shape, jnp.float32), zeros, zeros, zeros)


def pole_powers(decay, angle, counts):
    magnitude = jnp.exp(-decay[None] * counts[:, None, None])
    phase = angle[None] * counts[:, None, None]
    return (magnitude * jnp.cos(phase), magnitude * jnp.sin(phase))


def chain_factor(decay, angle, flags):
    length = flags.shape[0]
    whole = jnp.where(jnp.sum(flags) == 0, 1.0, 0.0)
    power_real, power_imag = pole_powers(decay, angle, jnp.full((1,), length, jnp.float32))
    return (whole * power_real[0], whole * power_imag[0])


def base_conv(signal, decay, angle, res_real, res_imag, flags):
    length, width = signal.shape
    block = min(64, length)
    blocks = length // block
    gain_in = jnp.sqrt(-jnp.expm1(-2.0 * decay))
    power_real, power_imag = pole_powers(decay, angle, jnp.arange(block + 1, dtype=jnp.float32))
    kernel_rows = jnp.sum(
        gain_in * (res_real * power_real[:block] - res_imag * power_imag[:block]), axis=1
    )
    offsets = jnp.arange(block)[:, None] - jnp.arange(block)[None, :]
    kernel = jnp.take(kernel_rows, jnp.clip(offsets, 0, block - 1), axis=0)
    lower = offsets >= 0
    reverse_real = power_real[:block][::-1]
    reverse_imag = power_imag[:block][::-1]

    def one_block(carry, pieces):
        state_real, state_imag = carry
        values, marks = pieces
        counts = jnp.cumsum(marks)
        same = jnp.where(lower & (counts[:, None] == counts[None, :]), 1.0, 0.0)
        inner = jnp.einsum("tjc,jc->tc", kernel * same[:, :, None], values)
        fresh = jnp.where(counts == 0, 1.0, 0.0)
        carried_real = power_real[1:] * state_real - power_imag[1:] * state_imag
        carried_imag = power_real[1:] * state_imag + power_imag[1:] * state_real
        outside = fresh[:, None] * jnp.sum(
            res_real * carried_real - res_imag * carried_imag, axis=1
        )
        tail = jnp.where(counts == counts[-1], 1.0, 0.0)
        whole = jnp.where(counts[-1] == 0, 1.0, 0.0)
        weighted = gain_in * values[:, None, :] * tail[:, None, None]
        end_real = whole * carried_real[-1] + jnp.sum(reverse_real * weighted, axis=0)
        end_imag = whole * carried_imag[-1] + jnp.sum(reverse_imag * weighted, axis=0)
        return ((end_real, end_imag), inner + outside)

    zero = jnp.zeros(decay.shape, jnp.float32)
    final, outputs = lax.scan(
        one_block,
        (zero, zero),
        (signal.reshape(blocks, block, width), flags.reshape(blocks, block)),
    )
    return (outputs.reshape(length, width), final[0], final[1])


def carried_conv(state_real, state_imag, decay, angle, res_real, res_imag, flags):
    length = flags.shape[0]
    power_real, power_imag = pole_powers(decay, angle, jnp.arange(1, length + 1, dtype=jnp.float32))
    fresh = jnp.where(jnp.cumsum(flags) == 0, 1.0, 0.0)
    carried_real = power_real * state_real - power_imag * state_imag
    carried_imag = power_real * state_imag + power_imag * state_real
    outputs = fresh[:, None] * jnp.sum(res_real * carried_real - res_imag * carried_imag, axis=1)
    factor_real, factor_imag = chain_factor(decay, angle, flags)
    end_real = factor_real * state_real - factor_imag * state_imag
    end_imag = factor_real * state_imag + factor_imag * state_real
    return (outputs, end_real, end_imag)


def on_device(
    tokens,
    cotangent,
    resets,
    norm1_gain,
    in_weight,
    conv_weight,
    pole_decay,
    pole_angle,
    residue_re,
    residue_im,
    out_weight,
    norm2_gain,
    gate_weight,
    up_weight,
    down_weight,
):
    gain_one, weight_in, weight_out, gain_two, weight_gate, weight_up, weight_down = (
        lax.all_gather(norm1_gain, "seq", axis=0, tiled=True),
        lax.all_gather(in_weight, "seq", axis=0, tiled=True),
        lax.all_gather(out_weight, "seq", axis=0, tiled=True),
        lax.all_gather(norm2_gain, "seq", axis=0, tiled=True),
        lax.all_gather(gate_weight, "seq", axis=0, tiled=True),
        lax.all_gather(up_weight, "seq", axis=0, tiled=True),
        lax.all_gather(down_weight, "seq", axis=0, tiled=True),
    )
    length = tokens.shape[0]
    keep = 1.0 - resets.astype(jnp.float32)
    far = keep * jnp.concatenate([jnp.ones((1,), jnp.float32), keep[:-1]])

    def short_conv(rows, taps):
        return (
            taps[0][None] * rows[2:]
            + keep[:, None, None] * taps[1][None] * rows[1:-1]
            + far[:, None, None] * taps[2][None] * rows[:-2]
        )

    stream = tokens.astype(jnp.float32)
    scale_one = lax.rsqrt(jnp.mean(stream * stream, axis=-1, keepdims=True) + EPSILON)
    unit_one = stream * scale_one
    normed_one = (unit_one * gain_one.astype(jnp.float32)).astype(jnp.bfloat16)
    projected = jnp.einsum(
        "td,dbc->tbc", normed_one, weight_in, preferred_element_type=jnp.float32
    ).astype(jnp.bfloat16)
    edge_scale = jnp.stack([keep[length - 1], jnp.ones((), jnp.float32)])
    edge_rows = (projected[length - 2 :].astype(jnp.float32) * edge_scale[:, None, None]).astype(
        jnp.bfloat16
    )
    before = passed_along(edge_rows, "seq", 1)
    extended = jnp.concatenate([before, projected], 0).astype(jnp.float32)
    mixed = short_conv(extended, conv_weight)
    signal = mixed[:, 1] * mixed[:, 2]
    local_out, start_real, start_imag = base_conv(
        signal, pole_decay, pole_angle, residue_re, residue_im, resets
    )
    factor_real, factor_imag = chain_factor(pole_decay, pole_angle, resets)
    entering = entering_2(
        (factor_real, factor_imag, start_real, start_imag),
        "seq",
        chain_combine,
        chain_unit(pole_decay.shape, ()),
        False,
    )
    enter_real, enter_imag = (entering[2], entering[3])

    def carried_part(state_real, state_imag, decay, angle, res_real, res_imag):
        return carried_conv(state_real, state_imag, decay, angle, res_real, res_imag, resets)

    carried_values, carried_pull = jax.vjp(
        carried_part, enter_real, enter_imag, pole_decay, pole_angle, residue_re, residue_im
    )
    long_out = local_out + carried_values[0]
    gated = (mixed[:, 0] * long_out).astype(jnp.bfloat16)
    mixer_part = jnp.einsum("tc,dc->td", gated, weight_out, preferred_element_type=jnp.float32)
    mixer = lax.psum(mixer_part.astype(jnp.bfloat16), "mp").astype(jnp.float32)
    hidden_stream = stream + mixer
    scale_two = lax.rsqrt(jnp.mean(hidden_stream * hidden_stream, axis=-1, keepdims=True) + EPSILON)
    unit_two = hidden_stream * scale_two
    normed_two = (unit_two * gain_two.astype(jnp.float32)).astype(jnp.bfloat16)
    gate = jnp.dot(normed_two, weight_gate, preferred_element_type=jnp.float32)
    upper = jnp.dot(normed_two, weight_up, preferred_element_type=jnp.float32)
    sigma = jax.nn.sigmoid(gate)
    swish = gate * sigma
    activated = (swish * upper).astype(jnp.bfloat16)
    ffn_part = jnp.einsum("tf,df->td", activated, weight_down, preferred_element_type=jnp.float32)
    ffn = lax.psum(ffn_part.astype(jnp.bfloat16), "mp").astype(jnp.float32)
    block_out = (hidden_stream + ffn).astype(jnp.bfloat16)
    gain_one, weight_in, weight_out, gain_two, weight_gate, weight_up, weight_down = (
        lax.all_gather(norm1_gain, "seq", axis=0, tiled=True),
        lax.all_gather(in_weight, "seq", axis=0, tiled=True),
        lax.all_gather(out_weight, "seq", axis=0, tiled=True),
        lax.all_gather(norm2_gain, "seq", axis=0, tiled=True),
        lax.all_gather(gate_weight, "seq", axis=0, tiled=True),
        lax.all_gather(up_weight, "seq", axis=0, tiled=True),
        lax.all_gather(down_weight, "seq", axis=0, tiled=True),
    )
    grad_top = cotangent.astype(jnp.float32)
    grad_down = jnp.einsum("td,tf->df", cotangent, activated, preferred_element_type=jnp.float32)
    grad_act = jnp.einsum("td,df->tf", cotangent, weight_down, preferred_element_type=jnp.float32)
    grad_gate = (grad_act * upper * sigma * (1.0 + gate * (1.0 - sigma))).astype(jnp.bfloat16)
    grad_upper = (grad_act * swish).astype(jnp.bfloat16)
    grad_wgate = jnp.einsum("td,tf->df", normed_two, grad_gate, preferred_element_type=jnp.float32)
    grad_wup = jnp.einsum("td,tf->df", normed_two, grad_upper, preferred_element_type=jnp.float32)
    back_two_part = jnp.einsum(
        "tf,df->td", grad_gate, weight_gate, preferred_element_type=jnp.float32
    ) + jnp.einsum("tf,df->td", grad_upper, weight_up, preferred_element_type=jnp.float32)
    back_two = lax.psum(back_two_part.astype(jnp.bfloat16), "mp").astype(jnp.float32)
    scaled_two = back_two * gain_two.astype(jnp.float32)
    grad_gain_two = jnp.sum(back_two * unit_two, axis=0)
    grad_hidden = grad_top + scale_two * (
        scaled_two - unit_two * jnp.mean(scaled_two * unit_two, axis=-1, keepdims=True)
    )
    grad_hidden_low = grad_hidden.astype(jnp.bfloat16)
    grad_wout = jnp.einsum("td,tc->dc", grad_hidden_low, gated, preferred_element_type=jnp.float32)
    grad_gated = jnp.einsum(
        "td,dc->tc", grad_hidden_low, weight_out, preferred_element_type=jnp.float32
    )
    grad_first = grad_gated * long_out
    grad_long = grad_gated * mixed[:, 0]
    zero_state = jnp.zeros_like(enter_real)
    first_part = carried_pull((grad_long, zero_state, zero_state))
    arriving = entering_2(
        (factor_real, -factor_imag, first_part[0], first_part[1]),
        "seq",
        chain_combine,
        chain_unit(pole_decay.shape, ()),
        True,
    )
    arrive_real, arrive_imag = (arriving[2], arriving[3])
    second_part = carried_pull((jnp.zeros_like(grad_long), arrive_real, arrive_imag))

    def local_part(values, decay, angle, res_real, res_imag):
        return base_conv(values, decay, angle, res_real, res_imag, resets)

    _, local_pull = jax.vjp(local_part, signal, pole_decay, pole_angle, residue_re, residue_im)
    local_grads = local_pull((grad_long, arrive_real, arrive_imag))
    grad_signal = local_grads[0]
    grad_poles = tuple(
        (
            local_grads[index + 1] + first_part[index + 2] + second_part[index + 2]
            for index in range(4)
        )
    )
    grad_mixed = jnp.stack(
        [grad_first, grad_signal * mixed[:, 2], grad_signal * mixed[:, 1]], axis=1
    )
    _, conv_pull = jax.vjp(short_conv, extended, conv_weight)
    grad_extended, grad_taps = conv_pull(grad_mixed)
    returned = passed_along(grad_extended[:2], "seq", -1)
    returned = returned * edge_scale[:, None, None]
    grad_proj = grad_extended[2:] + jnp.concatenate(
        [jnp.zeros((length - 2,) + returned.shape[1:], jnp.float32), returned], 0
    )
    grad_proj_low = grad_proj.astype(jnp.bfloat16)
    grad_win = jnp.einsum(
        "td,tbc->dbc", normed_one, grad_proj_low, preferred_element_type=jnp.float32
    )
    back_one_part = jnp.einsum(
        "tbc,dbc->td", grad_proj_low, weight_in, preferred_element_type=jnp.float32
    )
    back_one = lax.psum(back_one_part.astype(jnp.bfloat16), "mp").astype(jnp.float32)
    scaled_one = back_one * gain_one.astype(jnp.float32)
    grad_gain_one = jnp.sum(back_one * unit_one, axis=0)
    grad_stream = grad_hidden + scale_one * (
        scaled_one - unit_one * jnp.mean(scaled_one * unit_one, axis=-1, keepdims=True)
    )
    shares = (
        lax.psum_scatter(
            grad_gain_one.astype(jnp.bfloat16), "seq", scatter_dimension=0, tiled=True
        ).astype(jnp.float32),
        lax.psum_scatter(
            grad_win.astype(jnp.bfloat16), "seq", scatter_dimension=0, tiled=True
        ).astype(jnp.float32),
        lax.psum_scatter(
            grad_wout.astype(jnp.bfloat16), "seq", scatter_dimension=0, tiled=True
        ).astype(jnp.float32),
        lax.psum_scatter(
            grad_gain_two.astype(jnp.bfloat16), "seq", scatter_dimension=0, tiled=True
        ).astype(jnp.float32),
        lax.psum_scatter(
            grad_wgate.astype(jnp.bfloat16), "seq", scatter_dimension=0, tiled=True
        ).astype(jnp.float32),
        lax.psum_scatter(
            grad_wup.astype(jnp.bfloat16), "seq", scatter_dimension=0, tiled=True
        ).astype(jnp.float32),
        lax.psum_scatter(
            grad_down.astype(jnp.bfloat16), "seq", scatter_dimension=0, tiled=True
        ).astype(jnp.float32),
    )
    channel = (
        lax.psum(grad_taps.astype(jnp.bfloat16), "seq").astype(jnp.float32),
        lax.psum(grad_poles[0].astype(jnp.bfloat16), "seq").astype(jnp.float32),
        lax.psum(grad_poles[1].astype(jnp.bfloat16), "seq").astype(jnp.float32),
        lax.psum(grad_poles[2].astype(jnp.bfloat16), "seq").astype(jnp.float32),
        lax.psum(grad_poles[3].astype(jnp.bfloat16), "seq").astype(jnp.float32),
    )
    return (
        block_out,
        grad_stream.astype(jnp.bfloat16),
        shares[0],
        shares[1],
        channel[0],
        channel[1],
        channel[2],
        channel[3],
        channel[4],
        shares[2],
        shares[3],
        shares[4],
        shares[5],
        shares[6],
    )


def solution(mesh):
    return jax.shard_map(
        on_device,
        mesh=mesh,
        in_specs=(
            P("seq", None),
            P("seq", None),
            P("seq"),
            P("seq"),
            P("seq", None, "mp"),
            P(None, None, "mp"),
            P(None, "mp"),
            P(None, "mp"),
            P(None, "mp"),
            P(None, "mp"),
            P("seq", "mp"),
            P("seq"),
            P("seq", "mp"),
            P("seq", "mp"),
            P("seq", "mp"),
        ),
        out_specs=(
            P("seq", None),
            P("seq", None),
            P("seq"),
            P("seq", None, "mp"),
            P(None, None, "mp"),
            P(None, "mp"),
            P(None, "mp"),
            P(None, "mp"),
            P(None, "mp"),
            P("seq", "mp"),
            P("seq"),
            P("seq", "mp"),
            P("seq", "mp"),
            P("seq", "mp"),
        ),
        check_vma=False,
    )
```

profile of v0, /device:TPU:1, one launch (start us, length us, event | category | flops | bytes accessed | tf_op | source)
XLA Modules:
  0.0 1418.8 jit_solution(14074682898061447345)
XLA Ops:
  16.7 66.4 %all-reduce.22 = (bf16[2048]{0:T(1024)(128)(2,1)S(1)}, bf16[2048]{0:T(1024)(128)(2,1)S(1)}) all-reduce(bf16[2048]{0:T(1024)(128)(2,1)S(1)} %dynamic-update-slice, bf16[2048]{0:T(1024)(128)(2,1)S(1)} %dynamic-update-slice.1), channel_id=1, replica_groups=mesh['seq'=32,'mp'=4] {'seq'}, use_global_device_ids=true, to_apply=%add.17 | all-reduce | flops 4096 | bytes 16384
  141.1 26.2 %while.128 = (s32[]{:T(128)}, f32[16,512]{1,0:T(8,128)S(1)}, f32[16,512]{1,0:T(8,128)S(1)}, f32[2,64,512]{2,1,0:T(8,128)}, s32[2,64]{1,0:T(2,128)S(1)}, /*index=...) while((s32[]{:T(128)}, f32[16,512]{1,0:T(8,128)S(1)}, ...), condition=%wide.region_7.8_spmd.clone, body=%wide.region_2.7_spmd.clone.sunk | while | flops 14737605 | bytes 58527808 | solution.py:90
  169.6 40.9 %all-gather.34.cloned.1.call-done = f32[512,512]{1,0:T(8,128)} async-done(((f32[16,512]{1,0:T(8,128)}), f32[512,512]{1,0:T(8,128)}) %all-gather.34.cloned.1.call-update) | async-done | bytes 1048592 | tf_op jit(solution)/shard_map/all_gather | solution.py:19
  210.6 44.8 %all-gather.36.cloned.1.call-done = f32[512,512]{1,0:T(8,128)} async-done(((f32[16,512]{1,0:T(8,128)}), f32[512,512]{1,0:T(8,128)}) %all-gather.36.cloned.1.call-update) | async-done | bytes 1048592 | tf_op jit(solution)/shard_map/all_gather | solution.py:19
  277.4 23.4 %all-gather.22.cloned.1.call-done = bf16[2048,512]{1,0:T(8,128)(2,1)} async-done(((bf16[64,512]{1,0:T(8,128)(2,1)}), bf16[2048,512]{1,0:T(8,128)(2,1)}) %all-gather.22.cloned.1.call-update) | async-done | bytes 2097168 | tf_op jit(solution)/shard_map/all_gather | solution.py:131
  306.1 39.3 %all-reduce.29.cloned.1.call-done = bf16[128,2048]{1,0:T(8,128)(2,1)} async-done(((bf16[128,2048]{1,0:T(8,128)(2,1)}), bf16[128,2048]{1,0:T(8,128)(2,1)}) %all-reduce.29.cloned.1.call-update) | async-done | bytes 524304 | tf_op jit(solution)/shard_map/psum | solution.py:185
  348.0 51.2 %all-gather.24.cloned.1.call-done = bf16[2048,1408]{1,0:T(8,128)(2,1)} async-done(((bf16[64,1408]{1,0:T(8,128)(2,1)}), bf16[2048,1408]{1,0:T(8,128)(2,1)}) %all-gather.24.cloned.1.call-update) | async-done | bytes 5767184 | tf_op jit(solution)/shard_map/all_gather | solution.py:133
  403.7 45.2 %all-gather.26.cloned.1.call-done = bf16[2048,1408]{1,0:T(8,128)(2,1)} async-done(((bf16[64,1408]{1,0:T(8,128)(2,1)}), bf16[2048,1408]{1,0:T(8,128)(2,1)}) %all-gather.26.cloned.1.call-update) | async-done | bytes 5767184 | tf_op jit(solution)/shard_map/all_gather | solution.py:134
  453.5 45.0 %all-gather.28.cloned.1.call-done = bf16[2048,1408]{1,0:T(8,128)(2,1)} async-done(((bf16[64,1408]{1,0:T(8,128)(2,1)}), bf16[2048,1408]{1,0:T(8,128)(2,1)}) %all-gather.28.cloned.1.call-update) | async-done | bytes 5767184 | tf_op jit(solution)/shard_map/all_gather | solution.py:135
  512.6 38.3 %all-reduce.31.cloned.1.call-done = bf16[128,2048]{1,0:T(8,128)(2,1)} async-done(((bf16[128,2048]{1,0:T(8,128)(2,1)}), bf16[128,2048]{1,0:T(8,128)(2,1)}) %all-reduce.31.cloned.1.call-update) | async-done | bytes 524304 | tf_op jit(solution)/shard_map/psum | solution.py:217
  556.7 26.4 %fusion.62 = (f32[16,512]{1,0:T(8,128)}, f32[16,512]{1,0:T(8,128)}, f32[16,512]{1,0:T(8,128)}, f32[16,512]{1,0:T(8,128)}, f32[16,512]{1,0:T(8,128)S(1)}, /*index...) fusion(f32[128,512]{1,0:T(8,128)S(1)} %get-tuple-element.2253, ...), kind=kLoop, calls=%fused_computation.170 | loop fusion | flops 75399168 | bytes 1115648 | tf_op jit(solution)/shard_map/transpose(jvp())/reduce_sum | solution.py:44
  584.3 33.5 %while.130 = (s32[]{:T(128)}, f32[16,512]{1,0:T(8,128)S(1)}, f32[16,512]{1,0:T(8,128)S(1)}, f32[2,64,64,1]{2,3,1,0:T(1,128)S(1)}, f32[2,64,64,512]{3,2,1,0:T(8,1...) while((s32[]{:T(128)}, f32[16,512]{1,0:T(8,128)S(1)}, ...), condition=%wide.region_28.29_spmd.clone.clone, body=%wide.region_24.28_spmd.clone.clone.sunk | while | flops 9564485 | bytes 41636204 | solution.py:90
  624.1 20.5 %all-gather.40.cloned.1.call-done = f32[512,512]{1,0:T(8,128)} async-done(((f32[16,512]{1,0:T(8,128)}), f32[512,512]{1,0:T(8,128)}) %all-gather.40.cloned.1.call-update) | async-done | bytes 1048592 | tf_op jit(solution)/shard_map/all_gather | solution.py:19
  644.6 44.8 %all-gather.42.cloned.1.call-done = f32[512,512]{1,0:T(8,128)} async-done(((f32[16,512]{1,0:T(8,128)}), f32[512,512]{1,0:T(8,128)}) %all-gather.42.cloned.1.call-update) | async-done | bytes 1048592 | tf_op jit(solution)/shard_map/all_gather | solution.py:19
  689.4 26.0 %while.127 = (s32[]{:T(128)}, f32[16,512]{1,0:T(8,128)S(1)}, f32[16,512]{1,0:T(8,128)S(1)}, s32[]{:T(128)}, f32[32,16,512]{2,1,0:T(8,128)}, /*index=5*/f32[32,16...) while((s32[]{:T(128)}, f32[16,512]{1,0:T(8,128)S(1)}, ...), condition=%wide.region_23.24_spmd, body=%wide.region_22.23_spmd.sunk | while | flops 65542 | bytes 262311 | solution.py:28
  716.3 63.6 %while.129 = (s32[]{:T(128)}, f32[64,64,512]{2,1,0:T(8,128)}, f32[65,16,512]{2,1,0:T(8,128)}, f32[65,16,512]{2,1,0:T(8,128)}, f32[16,512]{1,0:T(8,128)S(1)}, /*i...) while((s32[]{:T(128)}, f32[64,64,512]{2,1,0:T(8,128)}, ...), condition=%wide.region_38.39_spmd.clone, body=%wide.region_29.38_spmd.clone.sunk | while | flops 34185220 | bytes 140396736 | solution.py:90
  787.7 27.0 %scatter_custom_fusion = f32[64,512]{1,0:T(8,128)S(1)} fusion(s32[4096]{0:T(1024)} %copy-done.80, f32[4096,512]{1,0:T(8,128)} %bitcast.40, f32[]{:T(128)} %constant.265.clone.1), kind=kCustom, calls=%fused_computation.287 | custom fusion | flops 2097152 | bytes 131584 | tf_op jit(solution)/shard_map/transpose(jvp(jit(_take)))/scatter-add | solution.py:65
  846.9 20.8 %all-reduce.35.cloned.1.call-done = (bf16[128,2048]{1,0:T(8,128)(2,1)}, bf16[128,2048]{1,0:T(8,128)(2,1)}) async-done(((bf16[128,2048]{1,0:T(8,128)(2,1)}, bf16[128,2048]{1,0:T(8,128)(2,1)}), (bf16[128,2048]{1,0:T(8,128)(2,1)}, bf16[128,2048]{1,0:T(8,128)(2,1)})) %all-reduce.35.cloned.1.call-update) | async-done | bytes 1048592 | tf_op jit(solution)/shard_map/psum | solution.py:196
  906.3 68.3 %all-reduce.33.cloned.1.call-done = (bf16[2048]{0:T(1024)(128)(2,1)}, bf16[3,3,512]{2,1,0:T(4,128)(2,1)}, bf16[16,512]{1,0:T(8,128)(2,1)}, bf16[16,512]{1,0:T(8,...) async-done(((bf16[2048]{0:T(1024)(128)(2,1)}, bf16[3,3,512]{2,1,0:T(4,128)(2,1)}, bf16[16,512]{1,0:T(8,128)(2,1)}, ...) | async-done | bytes 82960
  983.7 70.7 %reduce-scatter.10.cloned.1.call-done = bf16[64,512]{1,0:T(8,128)(2,1)} async-done(((bf16[2048,512]{1,0:T(8,128)(2,1)}), bf16[64,512]{1,0:T(8,128)(2,1)}) %reduce-scatter.10.cloned.1.call-update) | async-done | bytes 65552 | tf_op jit(solution)/shard_map/reduce_scatter | solution.py:284
  1055.9 86.8 %reduce-scatter.16.cloned.1.call-done = bf16[64,1408]{1,0:T(8,128)(2,1)} async-done(((bf16[2048,1408]{1,0:T(8,128)(2,1)}), bf16[64,1408]{1,0:T(8,128)(2,1)}) %reduce-scatter.16.cloned.1.call-update) | async-done | bytes 180240
  1144.7 86.9 %reduce-scatter.12.cloned.1.call-done = bf16[64,1408]{1,0:T(8,128)(2,1)} async-done(((bf16[2048,1408]{1,0:T(8,128)(2,1)}), bf16[64,1408]{1,0:T(8,128)(2,1)}) %reduce-scatter.12.cloned.1.call-update) | async-done | bytes 180240 | tf_op jit(solution)/shard_map/reduce_scatter | solution.py:290
  1233.3 86.6 %reduce-scatter.14.cloned.1.call-done = bf16[64,1408]{1,0:T(8,128)(2,1)} async-done(((bf16[2048,1408]{1,0:T(8,128)(2,1)}), bf16[64,1408]{1,0:T(8,128)(2,1)}) %reduce-scatter.14.cloned.1.call-update) | async-done | bytes 180240 | tf_op jit(solution)/shard_map/reduce_scatter | solution.py:293
  1321.6 88.2 %reduce-scatter.8.cloned.1.call-done = bf16[64,3,512]{2,0,1:T(8,128)(2,1)} async-done(((bf16[2048,3,512]{2,0,1:T(8,128)(2,1)}), bf16[64,3,512]{2,0,1:T(8,128)(2,1)}) %reduce-scatter.8.cloned.1.call-update) | async-done | bytes 196624 | tf_op jit(solution)/shard_map/reduce_scatter | solution.py:281
  (585 shorter events, 375.5 us)
Async XLA Ops:
  7.2 118.5 %all-gather.20.cloned.1.call-start = ((), (), s32[]{:S(2)}) async-start(), calls=%async_computation.5 | async-start | bytes 6488064 | tf_op jit(solution)/shard_map/all_gather | solution.py:130
  7.9 161.7 %all-gather.30.cloned.1.call-start = ((), (), s32[]{:S(2)}) async-start(), calls=%async_computation.16 | async-start | bytes 1081344 | tf_op jit(solution)/shard_map/all_gather | solution.py:19
  11.5 158.1 %all-gather.32.cloned.1.call-start = ((), (), s32[]{:S(2)}) async-start(), calls=%async_computation.17 | async-start | bytes 1081344 | tf_op jit(solution)/shard_map/all_gather | solution.py:19
  12.2 198.3 %all-gather.34.cloned.1.call-start = ((), (), s32[]{:S(2)}) async-start(), calls=%async_computation.18 | async-start | bytes 1081344 | tf_op jit(solution)/shard_map/all_gather | solution.py:19
  129.6 8.3 collective-permute-start
  168.0 87.4 %all-gather.36.cloned.1.call-start = ((), (), s32[]{:S(2)}) async-start(), calls=%async_computation.19 | async-start | bytes 1081344 | tf_op jit(solution)/shard_map/all_gather | solution.py:19
  168.6 132.2 %all-gather.22.cloned.1.call-start = ((), (), s32[]{:S(2)}) async-start(), calls=%async_computation.6 | async-start | bytes 2162688 | tf_op jit(solution)/shard_map/all_gather | solution.py:131
  169.1 176.2 %all-reduce.29.cloned.1.call-start = ((), (), s32[]{:S(2)}) async-start(), calls=%async_computation.7 | async-start | bytes 1048576 | tf_op jit(solution)/shard_map/psum | solution.py:185
  256.8 299.8 %copy-start.36 = (f32[16,512]{1,0:T(8,128)}, f32[16,512]{1,0:T(8,128)S(1)}, u32[]{:S(2)}) copy-start(f32[16,512]{1,0:T(8,128)S(1)} %get-tuple-element.1456) | copy-start | bytes 98308
  303.9 95.2 %all-gather.24.cloned.1.call-start = ((), (), s32[]{:S(2)}) async-start(), calls=%async_computation.8 | async-start | bytes 5947392 | tf_op jit(solution)/shard_map/all_gather | solution.py:133
  304.7 144.2 %all-gather.26.cloned.1.call-start = ((), (), s32[]{:S(2)}) async-start(), calls=%async_computation.9 | async-start | bytes 5947392 | tf_op jit(solution)/shard_map/all_gather | solution.py:134
  305.4 193.0 %all-gather.28.cloned.1.call-start = ((), (), s32[]{:S(2)}) async-start(), calls=%async_computation.10 | async-start | bytes 5947392 | tf_op jit(solution)/shard_map/all_gather | solution.py:135
  306.0 244.9 %all-reduce.31.cloned.1.call-start = ((), (), s32[]{:S(2)}) async-start(), calls=%async_computation.11 | async-start | bytes 1048576 | tf_op jit(solution)/shard_map/psum | solution.py:217
  511.2 112.9 %all-gather.38.cloned.1.call-start = ((), (), s32[]{:S(2)}) async-start(), calls=%async_computation.20 | async-start | bytes 1081344 | tf_op jit(solution)/shard_map/all_gather | solution.py:19
  511.8 132.8 %all-gather.40.cloned.1.call-start = ((), (), s32[]{:S(2)}) async-start(), calls=%async_computation.21 | async-start | bytes 1081344 | tf_op jit(solution)/shard_map/all_gather | solution.py:19
  583.7 105.7 %all-gather.42.cloned.1.call-start = ((), (), s32[]{:S(2)}) async-start(), calls=%async_computation.22 | async-start | bytes 1081344 | tf_op jit(solution)/shard_map/all_gather | solution.py:19
  584.3 283.4 %all-reduce.35.cloned.1.call-start = ((), (), s32[]{:S(2)}) async-start(), calls=%async_computation.25 | async-start | bytes 2097152 | tf_op jit(solution)/shard_map/psum | solution.py:196
  784.5 36.5 %collective-permute-start.1 = (f32[2,3,512]{2,0,1:T(2,128)S(1)}, f32[2,3,512]{2,0,1:T(2,128)S(1)}, u32[]{:S(2)}, u32[]{:S(2)}) collective-permute-start(f32[2,3,512]{2,0,1:T(2,128)S(1)} %pad_add_fusion.3), channel_id=1, source_target_pairs={{4,0},{8,4},{12,8},{16,12},{20,16},{24,20},{28,24},{32,28},{36,32}... | collective-permute-start | bytes 36872 | tf_op jit(solution)/shard_map/ppermute | solution.py:12
  827.0 147.5 %all-reduce.33.cloned.1.call-start = ((), (), s32[]{:S(2)}) async-start(), calls=%async_computation.24 | async-start | bytes 172032
  869.8 184.6 %reduce-scatter.10.cloned.1.call-start = ((), (), s32[]{:S(2)}) async-start(), calls=%async_computation.13 | async-start | bytes 2162688 | tf_op jit(solution)/shard_map/reduce_scatter | solution.py:284
  873.2 269.5 %reduce-scatter.16.cloned.1.call-start = ((), (), s32[]{:S(2)}) async-start(), calls=%async_computation.23 | async-start | bytes 5947392
  886.7 344.9 %reduce-scatter.12.cloned.1.call-start = ((), (), s32[]{:S(2)}) async-start(), calls=%async_computation.14 | async-start | bytes 5947392 | tf_op jit(solution)/shard_map/reduce_scatter | solution.py:290
  892.9 427.0 %reduce-scatter.14.cloned.1.call-start = ((), (), s32[]{:S(2)}) async-start(), calls=%async_computation.15 | async-start | bytes 5947392 | tf_op jit(solution)/shard_map/reduce_scatter | solution.py:293
  898.1 511.6 %reduce-scatter.8.cloned.1.call-start = ((), (), s32[]{:S(2)}) async-start(), calls=%async_computation.12 | async-start | bytes 6488064 | tf_op jit(solution)/shard_map/reduce_scatter | solution.py:281
  (130 other events, 2850.5 us)
Sparse Core Ops, SparseCore 0:
  10.3 53.1 all-gather.19
  66.3 41.5 all-gather.29
  110.8 42.1 all-gather.31
  168.1 42.4 all-gather.33
  213.2 42.0 all-gather.35
  257.5 43.1 all-gather.21
  304.1 41.2 all-reduce.28
  347.6 51.5 all-gather.23
  401.4 47.4 all-gather.25
  451.0 47.4 all-gather.27
  511.4 39.4 all-reduce.30
  553.6 45.9 all-gather.37
  602.5 42.0 all-gather.39
  647.3 42.0 all-gather.41
  827.1 40.5 all-reduce.34
  873.6 100.9 all-reduce.32
  977.9 76.4 reduce-scatter.9
  1058.0 84.6 reduce-scatter.15
  1146.9 84.6 reduce-scatter.11
  1235.2 84.6 reduce-scatter.13
  1324.1 85.5 reduce-scatter.7
where the time goes:
time: 1430 us; the launch traced here: 1420 us
  waiting for transfers between devices  907 us (63%)
  other arithmetic  288 us (20%)
  blocking collectives  66.4 us (5%)
  matrix products  66 us (5%)
  local copies, waits for them, and re-layouts  60.5 us (4%)
  between operations  18.3 us (1%)
    unnamed x23, waiting for transfers between devices  160 us
    all_gather x7, waiting for transfers between devices, entering_2(): gathered = jax.tree.map(lambda a: lax.all_gather(a, axis), part)  151 us
    reduce_scatter x1, waiting for transfers between devices, on_device(): lax.psum_scatter(grad_win.astype(jnp.bfloat16), 'seq', scatter_dimension=...  88.2 us
    reduce_scatter x1, waiting for transfers between devices, on_device(): lax.psum_scatter(grad_wgate.astype(jnp.bfloat16), 'seq', scatter_dimensio...  86.9 us
    reduce_scatter x1, waiting for transfers between devices, on_device(): lax.psum_scatter(grad_wup.astype(jnp.bfloat16), 'seq', scatter_dimension=...  86.6 us
    reduce_scatter x1, waiting for transfers between devices, on_device(): lax.psum_scatter(grad_wout.astype(jnp.bfloat16), 'seq', scatter_dimension...  70.7 us
    unnamed x1, blocking collectives  66.4 us
    all_gather x1, waiting for transfers between devices, on_device(): lax.all_gather(gate_weight, 'seq', axis=0, tiled=True)  51.2 us
  transfers between devices with their start and end apart: 23, of which 17 were waited for; matrix products, arithmetic and copies ran while one was open for 20% of the time, Pallas kernels for 0%

commit v1 on v0

v1 whole, which is shorter than its diff:
```python
import functools

import jax
import jax.numpy as jnp
from jax import lax
from jax.experimental import pallas as pl
from jax.experimental.pallas import tpu as pltpu
from jax.sharding import PartitionSpec as P

EPSILON = 1e-05
BF16, F32 = jnp.bfloat16, jnp.float32
MESH = pl.DeviceIdType.MESH
LANES_A, LANES_B = 1664, 1536
CHUNKS = (
    ((0, 384), (0, 384)),
    ((384, 128), (384, 128)),
    ((512, 768), (512, 640)),
    ((1280, 384), (1152, 384)),
)
IN, OUT, GU, DOWN = range(4)


def where():
    place = lax.axis_index("seq")
    chip = place // 2
    return chip // 4, lax.rem(chip, 4), lax.rem(place, 2), lax.axis_index("mp")


def device(z, y, c, x):
    return ((z * 4 + y) * 2 + c, x)


def rem4(a):
    return lax.rem(a + 4, 4)


def remote(src, dst, send, recv, to):
    return pltpu.make_async_remote_copy(
        src_ref=src, dst_ref=dst, send_sem=send, recv_sem=recv, device_id=to, device_id_type=MESH
    )


def nn(a, b):
    return jnp.dot(a, b, preferred_element_type=F32)


def nt(a, b):
    return lax.dot_general(a, b, (((1,), (1,)), ((), ())), preferred_element_type=F32)


def tn(a, b):
    return lax.dot_general(a, b, (((0,), (0,)), ((), ())), preferred_element_type=F32)


def loop(count, body):
    lax.fori_loop(0, count, lambda i, _: (body(i), 0)[1], 0)


def span(start, size):
    return pl.ds(pl.multiple_of(start, size), size)


class Rings:
    def __init__(self):
        self.z, self.y, self.c, self.x = where()
        self.chip = self.z * 4 + self.y
        self.sib = device(self.z, self.y, 1 - self.c, self.x)

    def near(self, axis, d):
        if axis == 0:
            return device(rem4(self.z + d), self.y, self.c, self.x)
        if axis == 1:
            return device(self.z, rem4(self.y + d), self.c, self.x)
        return device(self.z, self.y, self.c, rem4(self.x + d))

    def along(self, d):
        return (lax.rem(self.chip + d + 16, 16) * 2 + self.c, self.x)


class Gather:
    def __init__(self, r, ref, rows, cut, lanes, first, send, recv):
        self.r, self.ref, self.rows, self.cut, self.lanes = r, ref, rows, cut, lanes
        self.first, self.send, self.recv, self.sent = first, send, recv, []

    def copy(self, phase, d, part, to, i):
        r = self.r
        axis = self.first if phase == 0 else 1 - self.first
        z, y = (rem4(r.z + d), r.y) if axis == 0 else (r.z, rem4(r.y + d))
        if phase == 0:
            rows = (pl.ds(0, self.rows), pl.ds(0, self.cut), pl.ds(self.cut, self.rows - self.cut))[part]
            ref = self.ref.at[z, y, rows, self.lanes]
        else:
            many = (pl.ds(0, 4), pl.ds(0, 2), pl.ds(2, 2))[part]
            ref = self.ref.at[z, many, :, self.lanes] if axis == 0 else self.ref.at[many, y, :, self.lanes]
        j = phase * 4 + i
        return remote(ref, ref, self.send.at[j], self.recv.at[j], r.near(axis, to))

    def start(self, *a):
        copy = self.copy(*a)
        copy.start()
        self.sent.append(copy)

    def full(self, phase):
        self.start(phase, 0, 0, 1, 0)
        self.start(phase, 0, 0, -1, 1)

    def forward(self, phase):
        self.copy(phase, -1, 0, 1, 0).wait_recv()
        self.start(phase, -1, 1, 1, 2)
        self.copy(phase, 1, 0, -1, 1).wait_recv()
        self.start(phase, 1, 2, -1, 3)

    def finish(self, phase):
        self.copy(phase, -2, 1, 1, 2).wait_recv()
        self.copy(phase, 2, 2, -1, 3).wait_recv()

    def drain(self):
        for copy in self.sent:
            copy.wait_send()
        self.sent = []


class Both:
    def __init__(self, parts):
        self.parts = parts

    def step(self, i):
        for p in self.parts:
            if i == 1:
                p.full(0)
            elif i == 2:
                p.forward(0)
            elif i == 3:
                p.finish(0)
                p.full(1)
            elif i == 4:
                p.forward(1)
            elif i == 5:
                p.finish(1)

    def run(self):
        for i in range(1, 6):
            self.step(i)

    def drain(self):
        for p in self.parts:
            p.drain()


class Scatter:
    def __init__(self, r, ref, lanes, width, first, bufs, send, recv):
        self.r, self.ref, self.lanes, self.width = r, ref, lanes, width
        self.first, self.bufs, self.send, self.recv, self.sent = first, bufs, send, recv, []

    def unit(self, phase, d, part):
        r = self.r
        axis = self.first if phase == 0 else 1 - self.first
        z, y = (rem4(r.z + d), r.y) if axis == 0 else (r.z, rem4(r.y + d))
        if phase == 1:
            rows = pl.ds(64 * part, 64)
            return self.ref.at[z, y, rows, self.lanes]
        many = pl.ds(2 * part, 2)
        return self.ref.at[z, many, :, self.lanes] if axis == 0 else self.ref.at[many, y, :, self.lanes]

    def landing(self, phase, i):
        return self.bufs[phase].at[i, :, :, self.lanes] if phase == 0 else self.bufs[phase].at[i, :, self.lanes]

    def copy(self, phase, d, part, to, i):
        j = phase * 6 + i
        axis = self.first if phase == 0 else 1 - self.first
        return remote(
            self.unit(phase, d, part), self.landing(phase, i), self.send.at[j], self.recv.at[j],
            self.r.near(axis, to),
        )

    def start(self, *a):
        copy = self.copy(*a)
        copy.start()
        self.sent.append(copy)

    def arrived(self, phase, i):
        self.copy(phase, 0, 0, 1, i).wait_recv()

    def add(self, phase, d, part, many):
        unit = self.unit(phase, d, part)
        lands = [self.landing(phase, i) for i in many]
        if phase == 0:
            def body(i):
                k, rows = i // 4, span(lax.rem(i, 4) * 32, 32)
                total = unit[k, rows, :].astype(F32)
                for l in lands:
                    total = total + l[k, rows, :].astype(F32)
                unit[k, rows, :] = total.astype(BF16)
            loop(8, body)
        else:
            def body(i):
                rows = span(i * 32, 32)
                total = unit[rows, :].astype(F32)
                for l in lands:
                    total = total + l[rows, :].astype(F32)
                unit[rows, :] = total.astype(BF16)
            loop(2, body)

    def begin(self, phase):
        self.start(phase, 2, 0, 1, 0)
        self.start(phase, 2, 1, -1, 1)
        self.start(phase, 1, 1, 1, 3)
        self.start(phase, -1, 0, -1, 4)

    def forward(self, phase):
        self.arrived(phase, 0)
        self.add(phase, 1, 0, (0,))
        self.start(phase, 1, 0, 1, 2)
        self.arrived(phase, 1)
        self.add(phase, -1, 1, (1,))
        self.start(phase, -1, 1, -1, 5)

    def finish(self, phase):
        self.arrived(phase, 4)
        self.arrived(phase, 2)
        self.add(phase, 0, 0, (2, 4))
        self.arrived(phase, 3)
        self.arrived(phase, 5)
        self.add(phase, 0, 1, (3, 5))

    def drain(self):
        for copy in self.sent:
            copy.wait_send()
        self.sent = []


class CrossSum:
    def __init__(self, r, part, got, mid, one, two, send, recv):
        self.r, self.part, self.got, self.mid, self.one, self.two = r, part, got, mid, one, two
        self.send, self.recv, self.sent = send, recv, []

    def start(self, copy):
        copy.start()
        self.sent.append(copy)

    def rows(self, c, x):
        return span((c * 4 + x) * 32, 32)

    def pair(self, d):
        x = rem4(self.r.x + d)
        return remote(
            self.part.at[self.rows(1 - self.r.c, x)], self.got.at[x],
            self.send.at[d], self.recv.at[d], self.r.sib,
        )

    def begin(self):
        for d in (2, 1, 3, 0):
            self.start(self.pair(d))

    def pairsum(self, d):
        self.pair(d).wait_recv()
        x = rem4(self.r.x + d)
        rows = self.rows(self.r.c, x)
        self.mid[x] = (self.part[rows].astype(F32) + self.got[x].astype(F32)).astype(BF16)

    def far(self, side):
        x = rem4(self.r.x + 2)
        return remote(
            self.mid.at[x, pl.ds(16 * side, 16)], self.one.at[side],
            self.send.at[4 + side], self.recv.at[4 + side], self.r.near(2, 1 - 2 * side),
        )

    def late(self, side, summed):
        d = 1 - 2 * side
        x = rem4(self.r.x + d)
        half = side if summed else 1 - side
        j = 6 + side * 2 + summed
        return remote(
            self.mid.at[x, pl.ds(16 * half, 16)], self.two.at[side, pl.ds(16 * half, 16)],
            self.send.at[j], self.recv.at[j], self.r.near(2, d),
        )

    def middle(self):
        self.pairsum(2)
        self.start(self.far(0))
        self.start(self.far(1))
        self.pairsum(1)
        self.start(self.late(0, 0))
        self.pairsum(3)
        self.start(self.late(1, 0))
        for side in range(2):
            self.far(side).wait_recv()
            x = rem4(self.r.x + 1 - 2 * side)
            rows = pl.ds(16 * side, 16)
            self.mid[x, rows] = (self.mid[x, rows].astype(F32) + self.one[side].astype(F32)).astype(BF16)
            self.start(self.late(side, 1))

    def end(self):
        self.pair(0).wait_recv()
        for side in range(2):
            self.late(side, 0).wait_recv()
            self.late(side, 1).wait_recv()

    def result(self, rows):
        base = (self.r.c * 4 + self.r.x) * 32
        own = self.part[pl.ds(pl.multiple_of(base + rows.start, rows.size), rows.size)].astype(F32)
        own = own + self.got[self.r.x, rows].astype(F32)
        return own + self.two[0, rows].astype(F32) + self.two[1, rows].astype(F32)

    def drain(self):
        for copy in self.sent:
            copy.wait_send()
        self.sent = []


class CrossGather:
    def __init__(self, r, ref, both, send, recv):
        self.r, self.ref, self.both, self.send, self.recv, self.sent = r, ref, both, send, recv, []

    def start(self, copy):
        copy.start()
        self.sent.append(copy)

    def rows(self, d, part, sibling=False):
        c = 1 - self.r.c if sibling else self.r.c
        base = rem4(self.r.x + d) * 32
        if self.both:
            base = base + c * 128
        if part is None:
            return self.ref.at[pl.ds(pl.multiple_of(base, 32), 32)]
        return self.ref.at[pl.ds(pl.multiple_of(base + 16 * part, 16), 16)]

    def ring(self, d, part, to, i):
        ref = self.rows(d, part)
        return remote(ref, ref, self.send.at[i], self.recv.at[i], self.r.near(2, to))

    def pair(self, d):
        ref = self.rows(d, None)
        return remote(ref, ref, self.send.at[4 + d % 4], self.recv.at[4 + d % 4], self.r.sib)

    def begin(self):
        self.start(self.ring(0, None, 1, 0))
        self.start(self.ring(0, None, -1, 1))
        if self.both:
            self.start(self.pair(0))

    def middle(self):
        self.ring(-1, None, 1, 0).wait_recv()
        self.start(self.ring(-1, 0, 1, 2))
        self.ring(1, None, -1, 1).wait_recv()
        self.start(self.ring(1, 1, -1, 3))
        if self.both:
            self.start(self.pair(-1))
            self.start(self.pair(1))

    def end(self):
        self.ring(-2, 0, 1, 2).wait_recv()
        self.ring(2, 1, -1, 3).wait_recv()
        if self.both:
            self.start(self.pair(2))
            for d in (0, -1, 1, 2):
                ref = self.rows(d, None, True)
                remote(ref, ref, self.send.at[4 + d % 4], self.recv.at[4 + d % 4], self.r.sib).wait_recv()

    def drain(self):
        for copy in self.sent:
            copy.wait_send()
        self.sent = []


class Refs:
    pass


SCRATCH = {
    "ga": ((4, 4, 128, LANES_A), BF16),
    "gb": ((4, 4, 128, LANES_B), BF16),
    "s0a": ((6, 2, 128, LANES_A), BF16),
    "s0b": ((6, 2, 128, LANES_B), BF16),
    "s1a": ((6, 64, LANES_A), BF16),
    "s1b": ((6, 64, LANES_B), BF16),
    "sib_a": ((64, LANES_A), BF16),
    "sib_b": ((64, LANES_B), BF16),
    "gains_all": ((4, 4, 16, 128), F32),
    "gains": ((8, 2048), F32),
    "keep": ((256, 256), F32),
    "gy": ((256, 2048), BF16),
    "n1": ((256, 2048), BF16),
    "n2": ((256, 2048), BF16),
    "dh": ((256, 2048), BF16),
    "part": ((256, 2048), BF16),
    "mid": ((4, 32, 2048), BF16),
    "got": ((4, 4, 32, 2048), BF16),
    "one": ((4, 2, 16, 2048), BF16),
    "two": ((4, 2, 32, 2048), BF16),
    "bo": ((128, 2048), BF16),
    "gt": ((128, 2048), BF16),
    "h": ((32, 2048), F32),
    "dhf": ((32, 2048), F32),
    "p": ((264, 768), F32),
    "q0": ((256, 256), F32),
    "q1": ((256, 256), F32),
    "q2": ((256, 256), F32),
    "u": ((256, 256), F32),
    "v": ((256, 256), F32),
    "z": ((256, 256), BF16),
    "st_re": ((257, 16, 256), F32),
    "st_im": ((257, 16, 256), F32),
    "ends": ((4, 4, 32, 256), F32),
    "back_ends": ((4, 4, 32, 256), F32),
    "gu": ((256, 1408), F32),
    "act": ((256, 768), BF16),
    "dgu": ((256, 1408), BF16),
    "dv": ((256, 256), F32),
    "dq": ((264, 768), F32),
    "dp": ((256, 768), BF16),
    "small": ((4, 4, 80, 256), BF16),
    "small_sum": ((80, 256), F32),
    "small_sib": ((80, 256), F32),
    "ggain": ((8, 2048), F32),
    "ggain_all": ((8, 8, 2048), F32),
}
SEMS = {
    "w": (4, 2, 8), "w_sib": (4, 2), "gain": (8,), "gain_sib": (), "keep_s": (), "gy_s": (), "n1_s": (),
    "p_s": (), "dq_s": (), "ends_s": (2, 8), "back_s": (2, 8), "sum": (4, 10), "cg": (4, 8),
    "rs": (4, 2, 12), "rs_sib": (4, 2), "small_s": (2, 8), "small_x": (), "gg": (8,),
}


def kernel(*refs):
    names = ["mine", "other", "gain_in", "keep_in", "tok", "cot", "taps", "poles"]
    outs = ["block_out", "grad_tok", "grad_w", "grad_small", "grad_gain"]
    k = Refs()
    for name, ref in zip(names + outs + list(SCRATCH), refs):
        setattr(k, name, ref)
    rest = refs[len(names) + len(outs) + len(SCRATCH):]
    S, R = {}, {}
    for i, name in enumerate(SEMS):
        S[name], R[name] = rest[2 * i], rest[2 * i + 1]
    local = rest[2 * len(SEMS)]
    r = Rings()
    g = (k.ga, k.gb)
    z, y, c, x = r.z, r.y, r.c, r.x

    barrier = pltpu.get_barrier_semaphore()
    peers = [r.sib] + [r.near(a, d) for a in range(3) for d in (1, -1)] + [r.along(1), r.along(-1)]
    for peer in peers:
        pl.semaphore_signal(barrier, inc=1, device_id=peer, device_id_type=MESH)
    pl.semaphore_wait(barrier, len(peers))

    def lanes(n, h):
        o, w = CHUNKS[n][h]
        return pl.ds(o, w)

    def weight(n, h, i):
        o, w = CHUNKS[n][h]
        return g[h][i, :, :, o:o + w].reshape(512, w)

    pending = []

    my64 = span(c * 64, 64)
    my128 = span(c * 128, 128)
    gather = [
        Both([Gather(r, g[h], 128, 64, lanes(n, h), 1 - h, S["w"].at[n, h], R["w"].at[n, h]) for h in range(2)])
        for n in range(4)
    ]

    def weight_sib(n, h):
        o, w = CHUNKS[n][h]
        return remote(
            k.other.at[:, pl.ds(o + (LANES_A if h else 0), w)], g[h].at[z, y, my64, lanes(n, h)],
            S["w_sib"].at[n, h], R["w_sib"].at[n, h], r.sib,
        )

    for n in range(4):
        for h in range(2):
            weight_sib(n, h).start()
            o, w = CHUNKS[n][h]
            so = o + (LANES_A if h else 0)
            g[h][z, y, my64, o:o + w] = k.mine[:, so:so + w]
        if n == 0:
            eight = span(c * 8, 8)
            gain_sib = remote(k.gain_in, k.gains_all.at[z, y, eight], S["gain_sib"], R["gain_sib"], r.sib)
            gain_sib.start()
            k.gains_all[z, y, eight] = k.gain_in[...]
    keep_sib = remote(k.keep_in, k.keep.at[my128], S["keep_s"], R["keep_s"], r.sib)
    keep_sib.start()
    k.keep[my128] = k.keep_in[...]
    gy_sib = remote(k.cot, k.gy.at[my128], S["gy_s"], R["gy_s"], r.sib)
    gy_sib.start()
    k.gy[my128] = k.cot[...]

    def ag(n, i):
        if i == 1:
            for h in range(2):
                weight_sib(n, h).wait_recv()
        gather[n].step(i)

    gain_all = Both([Gather(r, k.gains_all, 16, 8, pl.ds(0, 128), 1, S["gain"], R["gain"])])
    gain_sib.wait_recv()
    gain_all.step(1)
    ag(IN, 1)
    gain_all.step(2)
    gain_all.step(3)
    ag(IN, 2)
    gain_all.step(4)
    gain_all.step(5)
    ag(OUT, 1)
    ag(IN, 3)
    for i in range(16):
        k.gains[:, i * 128:(i + 1) * 128] = k.gains_all[i // 4, i % 4, 0:8] + k.gains_all[i // 4, i % 4, 8:16]

    def norm_one(i):
        rows = span(i * 16, 16)
        a = k.tok[rows, :].astype(F32)
        s = lax.rsqrt(jnp.mean(a * a, axis=-1, keepdims=True) + EPSILON)
        k.n1[pl.ds(pl.multiple_of(c * 128 + i * 16, 16), 16), :] = (a * s * k.gains[0:1, :]).astype(BF16)
    loop(8, norm_one)
    n1_sib = remote(k.n1.at[my128], k.n1.at[my128], S["n1_s"], R["n1_s"], r.sib)
    n1_sib.start()
    ag(OUT, 2)
    ag(GU, 1)
    ag(IN, 4)
    ag(OUT, 3)
    ag(GU, 2)
    k_other = span((1 - c) * 128, 128)
    remote(k.n1.at[k_other], k.n1.at[k_other], S["n1_s"], R["n1_s"], r.sib).wait_recv()
    ag(IN, 5)
    ag(DOWN, 1)
    ag(OUT, 4)
    ag(GU, 3)

    k.p[8:264, :] = jnp.zeros((256, 768), F32)

    def project(i):
        a = k.n1[:, pl.ds(pl.multiple_of(i * 512, 512), 512)]
        for h in range(2):
            o = 384 * h
            k.p[8:264, o:o + 384] += nn(a, weight(IN, h, i))
    loop(4, project)

    def round_p(i):
        rows = span(8 + i * 8, 8)
        k.p[rows, :] = k.p[rows, :].astype(BF16).astype(F32)
    loop(32, round_p)
    p_next = remote(k.p.at[256:264], k.p.at[0:8], S["p_s"], R["p_s"], r.along(1))
    p_next.start()
    ag(DOWN, 2)
    p_next.wait()
    remote(k.keep.at[k_other], k.keep.at[k_other], S["keep_s"], R["keep_s"], r.sib).wait_recv()

    def masks(i):
        rows = span(i * 16, 16)
        near = k.keep[rows, :]
        before = k.keep[span(jnp.maximum(i * 16 - 8, 0), 8), :]
        first = jnp.where(i == 0, 1.0, before[7:8, :])
        shifted = jnp.concatenate([first, near[0:15, :]], 0)
        return near, near * shifted

    def short(i):
        near, far = masks(i)
        ext = k.p[pl.ds(pl.multiple_of(i * 16, 16), 24), :]
        q = []
        for b in range(3):
            l = slice(b * 256, b * 256 + 256)
            e = ext[:, l]
            q.append(
                k.taps[0:1, l] * e[8:24] + near * k.taps[1:2, l] * e[7:23] + far * k.taps[2:3, l] * e[6:22]
            )
        rows = span(i * 16, 16)
        k.q0[rows, :] = q[0]
        k.q1[rows, :] = q[1]
        k.q2[rows, :] = q[2]
        k.u[rows, :] = q[1] * q[2]
    loop(16, short)

    zero = jnp.zeros((16, 256), F32)
    lr, li, cr, ci, pr, pi = (k.poles[i] for i in range(6))

    def advance(re, im, u, keep):
        kr, ki = keep * re, keep * im
        return lr * kr - li * ki + u, lr * ki + li * kr

    def end_state(i, state):
        rows = span(i * 8, 8)
        u, keep = k.u[rows, :], k.keep[rows, :]
        for j in range(8):
            state = advance(*state, u[j:j + 1, :], keep[j:j + 1, :])
        return state

    def exchange(re, im, ref, send, recv):
        ref[z, y, 0:16] = re
        ref[z, y, 16:32] = im
        return Both([
            Gather(r, ref, 32, 16, pl.ds(128 * h, 128), 1 - h, send.at[h], recv.at[h]) for h in range(2)
        ])

    end = lax.fori_loop(0, 32, end_state, (zero, zero))
    ends = exchange(*end, k.ends, S["ends_s"], R["ends_s"])
    ends.step(1)
    ag(OUT, 5)
    ends.step(2)
    ends.step(3)
    ag(GU, 4)
    ag(DOWN, 3)
    ends.step(4)
    ends.step(5)
    enter = (zero, zero)
    for i in range(15):
        er, ei = enter
        nr = pr * er - pi * ei + k.ends[i // 4, i % 4, 0:16]
        ni = pr * ei + pi * er + k.ends[i // 4, i % 4, 16:32]
        enter = (jnp.where(i < r.chip, nr, er), jnp.where(i < r.chip, ni, ei))
    k.st_re[0] = enter[0]
    k.st_im[0] = enter[1]

    def scan(i, state):
        rows = span(i * 8, 8)
        u, keep = k.u[rows, :], k.keep[rows, :]
        for j in range(8):
            state = advance(*state, u[j:j + 1, :], keep[j:j + 1, :])
            k.st_re[i * 8 + j + 1] = state[0]
            k.st_im[i * 8 + j + 1] = state[1]
            k.v[pl.ds(i * 8 + j, 1), :] = jnp.sum(cr * state[0] - ci * state[1], axis=0, keepdims=True)
        return state
    lax.fori_loop(0, 32, scan, enter)

    def gated(i):
        rows = span(i * 32, 32)
        k.z[rows, :] = (k.q0[rows, :] * k.v[rows, :]).astype(BF16)
    loop(8, gated)

    def out_weight(i):
        return jnp.concatenate([weight(OUT, 0, i), weight(OUT, 1, i)], 1)

    def mix(i):
        k.part[:, span(i * 512, 512)] = nt(k.z[...], out_weight(i)).astype(BF16)
    loop(4, mix)

    def cross(i):
        return CrossSum(r, k.part, k.got.at[i], k.mid, k.one.at[i], k.two.at[i], S["sum"].at[i], R["sum"].at[i])

    s_mix = cross(0)
    s_mix.begin()
    s_mix.middle()
    s_mix.end()

    own = (c * 4 + x) * 32

    def norm_two(i):
        rows = pl.ds(pl.multiple_of(i * 16, 16), 16)
        a = k.tok[pl.ds(pl.multiple_of(x * 32 + i * 16, 16), 16), :].astype(F32) + s_mix.result(rows)
        k.h[rows, :] = a
        s = lax.rsqrt(jnp.mean(a * a, axis=-1, keepdims=True) + EPSILON)
        k.n2[pl.ds(pl.multiple_of(own + i * 16, 16), 16), :] = (a * s * k.gains[1:2, :]).astype(BF16)
    loop(2, norm_two)
    g_n2 = CrossGather(r, k.n2, True, S["cg"].at[0], R["cg"].at[0])
    g_n2.begin()
    g_n2.middle()
    ag(GU, 5)
    ag(DOWN, 4)
    g_n2.end()
    s_mix.drain()

    def gate_up(i):
        a = k.n2[:, pl.ds(pl.multiple_of(i * 512, 512), 512)]
        for h in range(2):
            o, w = (0, 768) if h == 0 else (768, 640)
            t = nn(a, weight(GU, h, i))

            @pl.when(i == 0)
            def _():
                k.gu[:, o:o + w] = t

            @pl.when(i > 0)
            def _():
                k.gu[:, o:o + w] += t
    loop(4, gate_up)
    k.act[:, 640:768] = jnp.zeros((256, 128), BF16)

    def activate(i):
        rows = span(i * 16, 16)
        gu = k.gu[rows, :]
        gate, up = gu[:, 0:704], gu[:, 704:1408]
        k.act[rows, 0:704] = (gate * jax.nn.sigmoid(gate) * up).astype(BF16)
    loop(16, activate)
    ag(DOWN, 5)

    def down_weight(i):
        return jnp.concatenate([weight(DOWN, 0, i), weight(DOWN, 1, i)], 1)

    def ffn(i):
        k.part[:, span(i * 512, 512)] = nt(k.act[...], down_weight(i)).astype(BF16)
    loop(4, ffn)
    s_ffn = cross(1)
    s_ffn.begin()
    s_ffn.middle()
    s_ffn.end()

    def top(i):
        rows = pl.ds(pl.multiple_of(i * 16, 16), 16)
        k.bo[pl.ds(pl.multiple_of(x * 32 + i * 16, 16), 16), :] = (k.h[rows, :] + s_ffn.result(rows)).astype(BF16)
    loop(2, top)
    s_ffn.drain()
    g_bo = CrossGather(r, k.bo, False, S["cg"].at[1], R["cg"].at[1])
    g_bo.begin()
    g_bo.middle()

    remote(k.gy.at[k_other], k.gy.at[k_other], S["gy_s"], R["gy_s"], r.sib).wait_recv()
    for n in range(4):
        gather[n].drain()

    def d_act(i):
        t = nn(k.gy[:, pl.ds(pl.multiple_of(i * 512, 512), 512)], down_weight(i))

        @pl.when(i == 0)
        def _():
            k.dq[0:256, :] = t

        @pl.when(i > 0)
        def _():
            k.dq[0:256, :] += t
    loop(4, d_act)

    def d_gates(i):
        rows = span(i * 16, 16)
        gu = k.gu[rows, :]
        gate, up = gu[:, 0:704], gu[:, 704:1408]
        da = k.dq[rows, :][:, 0:704]
        sg = jax.nn.sigmoid(gate)
        dgate = da * up * sg * (1.0 + gate * (1.0 - sg))
        dup = da * (gate * sg)
        k.dgu[rows, :] = jnp.concatenate([dgate, dup], 1).astype(BF16)
    loop(16, d_gates)

    def d_n2(i):
        w = jnp.concatenate([weight(GU, 0, i), weight(GU, 1, i)], 1)
        k.part[:, span(i * 512, 512)] = nt(k.dgu[...], w).astype(BF16)
    loop(4, d_n2)
    s_dn2 = cross(2)
    s_dn2.begin()

    scatter = [
        [Scatter(r, g[h], lanes(n, h), CHUNKS[n][h][1], h, ((k.s0a, k.s1a), (k.s0b, k.s1b))[h],
                 S["rs"].at[n, h], R["rs"].at[n, h]) for h in range(2)]
        for n in range(4)
    ]
    sib_bufs = (k.sib_a, k.sib_b)

    def rs_sib(n, h):
        return remote(
            g[h].at[z, y, span((1 - c) * 64, 64), lanes(n, h)], sib_bufs[h].at[:, lanes(n, h)],
            S["rs_sib"].at[n, h], R["rs_sib"].at[n, h], r.sib,
        )

    def rs(n, i):
        for h in range(2):
            s = scatter[n][h]
            if i == 0:
                s.begin(0)
            elif i == 1:
                s.forward(0)
            elif i == 2:
                s.finish(0)
                s.begin(1)
            elif i == 3:
                s.forward(1)
            elif i == 4:
                s.finish(1)
                rs_sib(n, h).start()

    def weight_grad(n, a, b):
        wa, wb = CHUNKS[n][0][1], CHUNKS[n][1][1]

        def body(i):
            t = tn(a[:, pl.ds(pl.multiple_of(i * 512, 512), 512)], b[...]).astype(BF16)
            oa, ob = CHUNKS[n][0][0], CHUNKS[n][1][0]
            g[0][i, :, :, oa:oa + wa] = t[:, 0:wa].reshape(4, 128, wa)
            g[1][i, :, :, ob:ob + wb] = t[:, wa:wa + wb].reshape(4, 128, wb)
        loop(4, body)

    weight_grad(DOWN, k.gy, k.act)
    rs(DOWN, 0)
    s_dn2.middle()
    weight_grad(GU, k.n2, k.dgu)
    rs(GU, 0)
    g_bo.end()
    out_bo = pltpu.make_async_copy(k.bo, k.block_out, local.at[0])
    out_bo.start()
    s_dn2.end()

    def d_norm_two(i):
        rows = pl.ds(pl.multiple_of(i * 16, 16), 16)
        a = k.h[rows, :]
        s = lax.rsqrt(jnp.mean(a * a, axis=-1, keepdims=True) + EPSILON)
        hat = a * s
        dn = s_dn2.result(rows)
        dng = dn * k.gains[1:2, :]
        gy = k.gy[pl.ds(pl.multiple_of(own + i * 16, 16), 16), :].astype(F32)
        dh = gy + s * (dng - hat * jnp.mean(dng * hat, axis=-1, keepdims=True))
        k.dhf[rows, :] = dh
        k.dh[pl.ds(pl.multiple_of(own + i * 16, 16), 16), :] = dh.astype(BF16)
        t = jnp.sum(dn * hat, axis=0, keepdims=True)

        @pl.when(i == 0)
        def _():
            k.ggain[1:2, :] = t

        @pl.when(i > 0)
        def _():
            k.ggain[1:2, :] += t
    loop(2, d_norm_two)
    s_dn2.drain()
    g_dh = CrossGather(r, k.dh, True, S["cg"].at[2], R["cg"].at[2])
    g_dh.begin()
    rs(DOWN, 1)
    g_dh.middle()
    rs(DOWN, 2)
    rs(GU, 1)
    g_dh.end()

    def d_z(i):
        t = nn(k.dh[:, pl.ds(pl.multiple_of(i * 512, 512), 512)], out_weight(i))

        @pl.when(i == 0)
        def _():
            k.dv[...] = t

        @pl.when(i > 0)
        def _():
            k.dv[...] += t
    loop(4, d_z)

    def d_gated(i):
        rows = span(i * 32, 32)
        dz = k.dv[rows, :]
        k.dq[rows, 0:256] = dz * k.v[rows, :]
        k.dv[rows, :] = dz * k.q0[rows, :]
    loop(8, d_gated)

    def retreat(a, b, keep):
        ka, kb = keep * a, keep * b
        return ka, kb, lr * ka + li * kb, lr * kb - li * ka

    def start_state(i, state):
        rows = span((31 - i) * 8, 8)
        dv, keep = k.dv[rows, :], k.keep[rows, :]
        for j in reversed(range(8)):
            a = cr * dv[j:j + 1, :] + state[0]
            b = state[1] - ci * dv[j:j + 1, :]
            _, _, pa, pb = retreat(a, b, keep[j:j + 1, :])
            state = (pa, pb)
        return state

    begin = lax.fori_loop(0, 32, start_state, (zero, zero))
    backs = exchange(*begin, k.back_ends, S["back_s"], R["back_s"])
    backs.step(1)
    weight_grad(OUT, k.dh, k.z)
    rs(OUT, 0)
    backs.step(2)
    backs.step(3)
    rs(DOWN, 3)
    backs.step(4)
    rs(GU, 2)
    backs.step(5)
    arrive = (zero, zero)
    for i in reversed(range(1, 16)):
        er, ei = arrive
        nr = pr * er + pi * ei + k.back_ends[i // 4, i % 4, 0:16]
        ni = pr * ei - pi * er + k.back_ends[i // 4, i % 4, 16:32]
        arrive = (jnp.where(i > r.chip, nr, er), jnp.where(i > r.chip, ni, ei))

    def adjoint(i, carry):
        pa, pb, dcr, dci, dlr, dli = carry
        rows = span((31 - i) * 8, 8)
        dv, keep = k.dv[rows, :], k.keep[rows, :]
        for j in reversed(range(8)):
            t = (31 - i) * 8 + j
            d = dv[j:j + 1, :]
            a = cr * d + pa
            b = pb - ci * d
            k.u[pl.ds(t, 1), :] = jnp.sum(a, axis=0, keepdims=True)
            dcr = dcr + d * k.st_re[t + 1]
            dci = dci - d * k.st_im[t + 1]
            ka, kb, pa, pb = retreat(a, b, keep[j:j + 1, :])
            sr, si = k.st_re[t], k.st_im[t]
            dlr = dlr + ka * sr + kb * si
            dli = dli + kb * sr - ka * si
        return pa, pb, dcr, dci, dlr, dli

    _, _, dcr, dci, dlr, dli = lax.fori_loop(0, 32, adjoint, (*arrive, zero, zero, zero, zero))

    def d_branches(i):
        rows = span(i * 32, 32)
        du = k.u[rows, :]
        k.dq[rows, 256:512] = du * k.q2[rows, :]
        k.dq[rows, 512:768] = du * k.q1[rows, :]
    loop(8, d_branches)
    dq_next = remote(k.dq.at[0:8], k.dq.at[256:264], S["dq_s"], R["dq_s"], r.along(-1))
    dq_next.start()
    rs(OUT, 1)
    dq_next.wait()

    last = jnp.where(r.chip < 15, 1.0, 0.0)

    def d_short(i, taps):
        d = k.dq[pl.ds(pl.multiple_of(i * 16, 16), 24), :]
        near, far = masks(i)
        j = jnp.minimum(i * 16 + 16, 248)
        after = k.keep[span(j, 8), :]
        inside = i < 15
        tail_near = jnp.where(inside, after, last)
        tail_far = jnp.where(
            inside, after * jnp.concatenate([near[15:16, :], after[0:7, :]], 0), last
        )
        near = jnp.concatenate([near, tail_near], 0)
        far = jnp.concatenate([far, tail_far], 0)
        ext = k.p[pl.ds(pl.multiple_of(i * 16, 16), 24), :]
        rows = span(i * 16, 16)
        new = []
        for b in range(3):
            l = slice(b * 256, b * 256 + 256)
            e, db = ext[:, l], d[:, l]
            dn, df = near * db, far * db
            k.dp[rows, l] = (
                k.taps[0:1, l] * db[0:16] + k.taps[1:2, l] * dn[1:17] + k.taps[2:3, l] * df[2:18]
            ).astype(BF16)
            new.append(taps[3 * 0 + b] + jnp.sum(e[8:24] * db[0:16], axis=0, keepdims=True))
            new.append(taps[3 * 1 + b] + jnp.sum(e[7:23] * dn[0:16], axis=0, keepdims=True))
            new.append(taps[3 * 2 + b] + jnp.sum(e[6:22] * df[0:16], axis=0, keepdims=True))
        return tuple(new[3 * b + t] for t in range(3) for b in range(3))

    line = jnp.zeros((1, 256), F32)
    dtaps = lax.fori_loop(0, 16, d_short, (line,) * 9)

    def d_n1(i):
        w = jnp.concatenate([weight(IN, 0, i), weight(IN, 1, i)], 1)
        k.part[:, span(i * 512, 512)] = nt(k.dp[...], w).astype(BF16)
    loop(4, d_n1)
    s_dn1 = cross(3)
    s_dn1.begin()
    weight_grad(IN, k.n1, k.dp)
    rs(IN, 0)

    mine_small = [dcr, dci, dlr, dli]
    for i in range(4):
        k.small[z, y, 16 * i:16 * i + 16] = mine_small[i].astype(BF16)
    k.small[z, y, 64:80] = jnp.concatenate(list(dtaps) + [jnp.zeros((7, 256), F32)], 0).astype(BF16)
    smalls = Both([
        Gather(r, k.small, 80, 48, pl.ds(128 * h, 128), 1 - h, S["small_s"].at[h], R["small_s"].at[h])
        for h in range(2)
    ])
    s_dn1.middle()
    smalls.step(1)
    rs(GU, 3)
    rs(DOWN, 4)
    s_dn1.end()

    def d_norm_one(i):
        rows = pl.ds(pl.multiple_of(i * 16, 16), 16)
        here = pl.ds(pl.multiple_of(x * 32 + i * 16, 16), 16)
        a = k.tok[here, :].astype(F32)
        s = lax.rsqrt(jnp.mean(a * a, axis=-1, keepdims=True) + EPSILON)
        hat = a * s
        dn = s_dn1.result(rows)
        dng = dn * k.gains[0:1, :]
        k.gt[here, :] = (
            k.dhf[rows, :] + s * (dng - hat * jnp.mean(dng * hat, axis=-1, keepdims=True))
        ).astype(BF16)
        t = jnp.sum(dn * hat, axis=0, keepdims=True)

        @pl.when(i == 0)
        def _():
            k.ggain[0:1, :] = t

        @pl.when(i > 0)
        def _():
            k.ggain[0:1, :] += t
    loop(2, d_norm_one)
    s_dn1.drain()
    g_gt = CrossGather(r, k.gt, False, S["cg"].at[3], R["cg"].at[3])
    g_gt.begin()
    rs(IN, 1)
    smalls.step(2)
    g_gt.middle()
    smalls.step(3)
    rs(OUT, 2)
    rs(GU, 4)
    smalls.step(4)
    rs(IN, 2)
    g_gt.end()
    out_gt = pltpu.make_async_copy(k.gt, k.grad_tok, local.at[1])
    out_gt.start()
    smalls.step(5)

    def small_total(i):
        rows = span(i * 16, 16)
        t = jnp.zeros((16, 256), F32)
        for j in range(16):
            t = t + k.small[j // 4, j % 4, rows, :].astype(F32)
        k.small_sum[rows, :] = t
    loop(5, small_total)
    small_x = remote(k.small_sum, k.small_sib, S["small_x"], R["small_x"], r.sib)
    small_x.start()
    rs(OUT, 3)
    rs(IN, 3)
    rs(OUT, 4)
    rs(IN, 4)
    small_x.wait()

    copies = [out_bo, out_gt]
    for j, src in enumerate((k.small_sum, k.small_sib)):
        copies.append(pltpu.make_async_copy(src, k.grad_small.at[j], local.at[2 + j]))
    copies.append(pltpu.make_async_copy(k.ggain, k.grad_gain, local.at[4]))
    for n in range(4):
        for h in range(2):
            rs_sib(n, h).wait()
    for h in range(2):
        wide = pl.ds(LANES_A if h else 0, LANES_B if h else LANES_A)
        copies.append(pltpu.make_async_copy(g[h].at[z, y, my64], k.grad_w.at[0, :, wide], local.at[5 + 2 * h]))
        copies.append(pltpu.make_async_copy(sib_bufs[h], k.grad_w.at[1, :, wide], local.at[6 + 2 * h]))
    for copy in copies[2:]:
        copy.start()
    for copy in copies:
        copy.wait()
    for n in range(4):
        for h in range(2):
            weight_sib(n, h).wait_send()
            scatter[n][h].drain()
    for copy in (gain_sib, keep_sib, gy_sib, n1_sib):
        copy.wait_send()
    for group in (gain_all, ends, backs, smalls, g_n2, g_bo, g_dh, g_gt):
        group.drain()


def block(*arrays):
    sems = []
    for shape in SEMS.values():
        sems += [pltpu.SemaphoreType.DMA(shape)] * 2
    vmem = pl.BlockSpec(memory_space=pltpu.VMEM)
    return pl.pallas_call(
        kernel,
        out_shape=(
            jax.ShapeDtypeStruct((128, 2048), BF16),
            jax.ShapeDtypeStruct((128, 2048), BF16),
            jax.ShapeDtypeStruct((2, 64, LANES_A + LANES_B), BF16),
            jax.ShapeDtypeStruct((2, 80, 256), F32),
            jax.ShapeDtypeStruct((8, 2048), F32),
        ),
        in_specs=[vmem] * len(arrays),
        out_specs=[pl.BlockSpec(memory_space=pl.ANY)] * 5,
        scratch_shapes=[pltpu.VMEM(s, t) for s, t in SCRATCH.values()] + sems + [pltpu.SemaphoreType.DMA((9,))],
        compiler_params=pltpu.CompilerParams(
            collective_id=0, has_side_effects=True, vmem_limit_bytes=63 * 2**20
        ),
        name="block",
    )(*arrays)


def on_device(
    tokens, cotangent, resets, norm1_gain, in_weight, conv_weight, pole_decay, pole_angle, residue_re, residue_im,
    out_weight, norm2_gain, gate_weight, up_weight, down_weight,
):
    c = lax.rem(lax.axis_index("seq"), 2)

    def columns(c):
        def half(w, n):
            return lax.dynamic_slice_in_dim(w, c * n, n, axis=w.ndim - 1)

        i, o = half(in_weight, 256).reshape(64, 768), half(out_weight, 256)
        gu = jnp.concatenate([half(gate_weight, 704), half(up_weight, 704)], 1)
        d = jnp.pad(half(down_weight, 704), ((0, 0), (0, 64)))
        return jnp.concatenate(
            [i[:, :384], o[:, :128], gu[:, :768], d[:, :384], i[:, 384:], o[:, 128:], gu[:, 768:], d[:, 384:]], 1
        )

    def half(a):
        return lax.dynamic_slice_in_dim(a, c * 256, 256, axis=a.ndim - 1)

    gains = jnp.stack([norm1_gain, norm2_gain]).astype(F32)
    gains = lax.dynamic_update_slice(jnp.zeros((8, 128), F32), gains, (0, c * 64))
    keep = jnp.broadcast_to((1.0 - resets.astype(F32))[:, None], (128, 256))
    taps = jnp.pad(half(conv_weight).reshape(3, 768), ((0, 5), (0, 0)))
    decay, angle, res_re, res_im = (half(a) for a in (pole_decay, pole_angle, residue_re, residue_im))
    size, wide = jnp.exp(-decay), jnp.exp(-256.0 * decay)
    gin = jnp.sqrt(-jnp.expm1(-2.0 * decay))
    lr, li = size * jnp.cos(angle), size * jnp.sin(angle)
    poles = jnp.stack(
        [lr, li, gin * res_re, gin * res_im, wide * jnp.cos(256.0 * angle), wide * jnp.sin(256.0 * angle)]
    )
    block_out, grad_tok, grad_w, grad_small, ggain = block(
        columns(c), columns(1 - c), gains, keep, tokens, cotangent, taps, poles
    )

    def order(a, b):
        return jnp.where(c == 0, a, b), jnp.where(c == 0, b, a)

    first, second = order(grad_w[0], grad_w[1])
    s_first, s_second = order(grad_small[0], grad_small[1])

    def join(f):
        return jnp.concatenate([f(first), f(second)], -1).astype(F32)

    def cut(a, n):
        return [a[:, o:o + w] for o, w in ((CHUNKS[n][0][0], CHUNKS[n][0][1]), (LANES_A + CHUNKS[n][1][0], CHUNKS[n][1][1]))]

    def whole(a, n):
        return jnp.concatenate(cut(a, n), 1)

    grad_in = join(lambda a: whole(a, IN).reshape(64, 3, 256))
    grad_out = join(lambda a: whole(a, OUT))
    grad_gate = join(lambda a: whole(a, GU)[:, :704])
    grad_up = join(lambda a: whole(a, GU)[:, 704:])
    grad_down = join(lambda a: whole(a, DOWN)[:, :704])
    small = jnp.concatenate([s_first, s_second], 1)
    dcr, dci, dlr, dli = (small[16 * i:16 * i + 16] for i in range(4))
    grad_taps = small[64:73].reshape(3, 3, 512)
    size = jnp.exp(-pole_decay)
    gin = jnp.sqrt(-jnp.expm1(-2.0 * pole_decay))
    lr, li = size * jnp.cos(pole_angle), size * jnp.sin(pole_angle)
    dgin = residue_re * dcr + residue_im * dci
    grad_decay = dgin * size * size / gin - (lr * dlr + li * dli)
    grad_angle = lr * dli - li * dlr
    gain_sum = lax.psum_scatter(
        lax.psum(ggain[0:2], "mp"), "seq", scatter_dimension=1, tiled=True
    )
    return (
        block_out, grad_tok, gain_sum[0], grad_in, grad_taps, grad_decay, grad_angle, gin * dcr, gin * dci, grad_out,
        gain_sum[1], grad_gate, grad_up, grad_down,
    )


def solution(mesh):
    row, cols = P("seq", "mp"), P(None, "mp")
    return jax.shard_map(
        on_device,
        mesh=mesh,
        in_specs=(
            P("seq", None), P("seq", None), P("seq"), P("seq"), P("seq", None, "mp"), P(None, None, "mp"),
            cols, cols, cols, cols, row, P("seq"), row, row, row,
        ),
        out_specs=(
            P("seq", None), P("seq", None), P("seq"), P("seq", None, "mp"), P(None, None, "mp"),
            cols, cols, cols, cols, row, P("seq"), row, row, row,
        ),
        check_vma=False,
    )
```

time: 1430 us -> 360 us (0.25)
  waiting for transfers between devices: 907 us -> 66.2 us
  other arithmetic: 288 us -> 5.42 us
  Pallas kernels: 0 us -> 244 us
  matrix products: 66 us -> 0 us
  blocking collectives: 66.4 us -> 8.39 us
  local copies, waits for them, and re-layouts: 60.5 us -> 18.1 us
    reduce_scatter x4 -> x0, waiting for transfers between devices: 332 us -> none  [the longest x1 88.2 us: on_device(): lax.psum_scatter(grad_win.astype(jnp.bfloat16), 'seq', scatter_dimension=...]
    all_gather x12 -> x0, waiting for transfers between devices: 316 us -> none  [the longest x7 151 us: entering_2(): gathered = jax.tree.map(lambda a: lax.all_gather(a, axis), part)]
    pallas_call x0 -> x1, Pallas kernels: none -> 244 us  [block(): pl.pallas_call(kernel, out_shape=(jax.ShapeDtypeStruct((128, 2048), BF16)...]
    reduce_sum x16 -> x0, other arithmetic: 100 us -> none  [the longest x2 38.7 us: pole_powers(): phase = angle[None] * counts[:, None, None]]
    psum x3 -> x0, waiting for transfers between devices: 98.5 us -> none  [the longest x1 39.3 us: on_device(): mixer = lax.psum(mixer_part.astype(jnp.bfloat16), 'mp').astype(jnp.float32)]
    unnamed x23 -> x2, waiting for transfers between devices: 160 us -> 66.2 us
    unnamed x1 -> x0, blocking collectives: 66.4 us -> none
    dot_general x15 -> x0, matrix products: 66 us -> none  [the longest x1 5.87 us: on_device(): jnp.einsum('tbc,dbc->td', grad_proj_low, weight_in, preferred_element_typ...]
  transfers between devices with their start and end apart: 23 -> 1, of which waited for: 17 -> 1; matrix products, arithmetic and copies ran while one was open for 20% -> 2% of each run, Pallas kernels for 0% -> 0%
where the time goes in v1:
time: 360 us; the launch traced here: 356 us
  Pallas kernels  244 us (68%)
  waiting for transfers between devices  66.2 us (18%)
  local copies, waits for them, and re-layouts  18.1 us (5%)
  between operations  14.5 us (4%)
  blocking collectives  8.39 us (2%)
  other arithmetic  5.42 us (2%)
    pallas_call x1, Pallas kernels, block(): pl.pallas_call(kernel, out_shape=(jax.ShapeDtypeStruct((128, 2048), BF16)...  244 us
    unnamed x2, waiting for transfers between devices  66.2 us
    unnamed x56, local copies, waits for them, and re-layouts  13.8 us
    psum x1, blocking collectives, on_device(): lax.psum(ggain[0:2], 'mp')  8.39 us
  transfers between devices with their start and end apart: 1, of which 1 were waited for; matrix products, arithmetic and copies ran while one was open for 2% of the time, Pallas kernels for 0%

profile of v1, /device:TPU:1, one launch (start us, length us, event | category | flops | bytes accessed | tf_op | source)
XLA Modules:
  0.0 356.2 jit_solution(2411847504197653354)
XLA Ops:
  7.3 1.0 dynamic-slice_bitcast_fusion
  8.3 0.9 copy-done.3
  9.3 0.8 copy-done.10
  10.2 0.8 copy-done.9
  11.2 0.7 copy-done.15
  13.8 0.7 copy-done.14
  15.4 0.7 copy-done.17
  17.2 0.7 broadcast_in_dim.10.refs_3_
  18.0 243.5 %block.1 = (bf16[128,2048]{1,0:T(8,128)(2,1)}, bf16[128,2048]{1,0:T(8,128)(2,1)}, bf16[2,64,3200]{2,1,0:T(8,128)(2,1)}, f32[2,80,256]{2,1,0:T(8,128)}, f32[8,2048]{1,0:T(8,128)}) custom-call(bf16[64,3200]{1,0:T(8,128)(2,1)} %copy-done.8, bf16[64,3200]{1,0:T(8,128)(2,1)} %copy-done.7, f32[8,128]{1,0:T(8,128)} %copy-done.16, ...), custom_call_target="tpu_custom_call" | custom-call | tf_op jit(solution)/shard_map/block/pallas_call | solution.py:1036
  261.5 0.8 slice.172
  262.3 1.4 copy.39
  264.2 0.9 copy-done.11
  265.0 0.8 multiply_subtract_fusion
  265.8 0.8 fusion.18
  266.7 0.8 maximum_convert_fusion.1
  267.5 0.7 maximum_convert_fusion.2
  268.2 0.8 fusion.7
  269.0 0.8 fusion.4
  269.9 0.9 copy.38
  271.4 66.2 %reduce-scatter.4.cloned.1.call-done = f32[64,2]{1,0:T(8,128)} async-done(((f32[2048,2]{1,0:T(8,128)}), f32[64,2]{1,0:T(8,128)}) %reduce-scatter.4.cloned.1.call-update) | async-done | bytes 528
  337.6 0.8 copy.40
  338.4 8.4 %psum.8 = f32[2,64]{1,0:T(2,128)S(1)} all-reduce(f32[2,64]{1,0:T(2,128)S(1)} %copy.40), channel_id=1, replica_groups=mesh['seq'=32,'mp'=4] {'mp'}, use_global_device_ids=true, to_apply=%region_0.1 | all-reduce | flops 128 | bytes 1024 | tf_op jit(solution)/shard_map/psum | solution.py:1120
  347.3 0.8 copy.66
  348.6 0.8 copy.67
  (84 shorter events, 6.3 us)
Async XLA Ops:
  7.2 5.6 %copy-start = (f32[3,3,512]{2,1,0:T(4,128)S(1)}, f32[3,3,512]{2,1,0:T(4,128)}, u32[]{:S(2)}) copy-start(f32[3,3,512]{2,1,0:T(4,128)} %param.20) | copy-start | bytes 55300
  7.2 330.4 %reduce-scatter.4.cloned.1.call-start = ((), (), s32[]{:S(2)}) async-start(), calls=%async_computation.1 | async-start | bytes 1081344
  8.3 0.9 copy-start.3
  9.2 0.9 copy-start.10
  10.1 0.9 copy-start.9
  11.0 0.8 copy-start.15
  12.1 0.7 copy-start.19
  12.1 0.8 copy-start.6
  12.1 0.8 copy-start.2
  13.0 0.8 copy-start.13
  13.7 0.8 copy-start.14
  14.7 0.6 copy-start.12
  15.4 2.6 copy-start.8
  15.4 2.6 copy-start.7
  15.4 0.7 copy-start.17
  15.4 0.8 copy-start.18
  17.2 0.8 copy-start.16
  262.3 1.4 copy-start.1
  264.1 0.9 copy-start.11
  269.9 77.4 %copy-start.5 = (bf16[128,2048]{1,0:T(8,128)(2,1)S(1)}, bf16[128,2048]{1,0:T(8,128)(2,1)}, u32[]{:S(2)}) copy-start(bf16[128,2048]{1,0:T(8,128)(2,1)} %get-tuple-element.107) | copy-start | bytes 1572868
  347.3 1.2 copy-start.4
Sparse Core Ops, SparseCore 0:
  263.8 73.6 reduce-scatter.3

commit v2 on v1

v2 whole, which is shorter than its diff:
```python
import functools

import jax
import jax.numpy as jnp
from jax import lax
from jax.experimental import pallas as pl
from jax.experimental.pallas import tpu as pltpu
from jax.sharding import PartitionSpec as P

EPSILON = 1e-05
BF16, F32 = jnp.bfloat16, jnp.float32
MESH = pl.DeviceIdType.MESH
LANES_A, LANES_B = 1664, 1536
CHUNKS = (
    ((0, 384), (0, 384)),
    ((384, 128), (384, 128)),
    ((512, 384), (512, 384)),
    ((896, 384), (896, 256)),
    ((1280, 384), (1152, 384)),
)
IN, OUT, GU, GU_2, DOWN = range(5)
WHOLE = {IN: CHUNKS[IN], OUT: CHUNKS[OUT], GU: ((512, 768), (512, 640)), DOWN: CHUNKS[DOWN]}


def where():
    place = lax.axis_index("seq")
    chip = place // 2
    return chip // 4, lax.rem(chip, 4), lax.rem(place, 2), lax.axis_index("mp")


def device(z, y, c, x):
    return ((z * 4 + y) * 2 + c, x)


def rem4(a):
    return lax.rem(a + 4, 4)


def remote(src, dst, send, recv, to):
    return pltpu.make_async_remote_copy(
        src_ref=src, dst_ref=dst, send_sem=send, recv_sem=recv, device_id=to, device_id_type=MESH
    )


def nn(a, b):
    return jnp.dot(a, b, preferred_element_type=F32)


def nt(a, b):
    return lax.dot_general(a, b, (((1,), (1,)), ((), ())), preferred_element_type=F32)


def tn(a, b):
    return lax.dot_general(a, b, (((0,), (0,)), ((), ())), preferred_element_type=F32)


def expm1(x):
    series = x / 8.0 + 1.0
    for n in range(7, 1, -1):
        series = series * (x / n) + 1.0
    return jnp.where(jnp.abs(x) < 0.25, x * series, jnp.exp(x) - 1.0)


def fold(count, body, state):
    return lax.fori_loop(0, count, body, state)


def loop(count, body):
    lax.fori_loop(0, count, lambda i, _: (body(i), 0)[1], 0)


def span(start, size):
    return pl.ds(pl.multiple_of(start, size), size)


PLAN = {
    "start": (("ag", IN, 1),),
    "gain_y": (("ag", DOWN, 1), ("ag", IN, 2), ("ag", GU, 1), ("ag", OUT, 1),),
    "gain_z": (("ag", DOWN, 2), ("ag", IN, 3),),
    "n1": (("ag", IN, 4),),
    "edge": (("ag", IN, 5), ("ag", GU_2, 1),),
    "project": (("ag", OUT, 2), ("ag", GU, 2), ("ag", DOWN, 3), ("ag", IN, 6),),
    "short": (("ag", GU_2, 2),),
    "ends_y": (("ag", OUT, 3), ("ag", GU, 3),),
    "ends_z": (("ag", OUT, 4), ("ag", OUT, 5), ("ag", GU_2, 3), ("ag", GU, 4), ("ag", GU_2, 4),),
    "mix": (("ag", OUT, 6),),
    "mix_1": (("ag", GU, 5),),
    "n2_0": (("ag", GU_2, 5), ("ag", DOWN, 4), ("ag", DOWN, 5),),
    "n2_1": (("ag", GU, 6),),
    "ff": (("ag", GU_2, 6),),
    "act": (("wg", DOWN), ("rs", DOWN, 0), ("rs", DOWN, 1), ("ag", DOWN, 6),),
    "dn2_1": (("wg", GU),),
    "dn2_2": (("rs", GU, 0), ("rs", DOWN, 2), ("rs", GU_2, 0), ("rs", GU, 1),),
    "dh_0": (("ffn_0",),),
    "dh_1": (("ffn_1",), ("rs", DOWN, 3),),
    "backs_y": (("wg", OUT), ("rs", OUT, 0), ("ffn_2",),),
    "backs_z": (("rs", DOWN, 4), ("rs", GU, 2), ("rs", OUT, 1), ("ffn_3",),),
    "dq": (("rs", OUT, 2), ("rs", GU_2, 1), ("rs", GU_2, 2),),
    "dn1_0": (("wg", IN), ("rs", IN, 0), ("rs", IN, 1),),
    "dn1_1": (("small", 0), ("rs", IN, 2), ("rs", OUT, 3),),
    "dn1_2": (("rs", GU_2, 3), ("small", 1), ("rs", DOWN, 5),),
    "gt_0": (("ffn_4",), ("rs", IN, 3), ("rs", GU, 3),),
    "gt_1": (("rs", OUT, 4),),
    "gt_2": (("rs", IN, 4), ("rs", GU_2, 4), ("rs", GU, 4), ("small", 2),),
    "gt_3": (("rs", OUT, 5),),
    "gt_4": (("rs", IN, 5), ("rs", GU_2, 5), ("rs", GU, 5), ("ffn_5",),),
}


class Rings:
    def __init__(self):
        self.z, self.y, self.c, self.x = where()
        self.chip = self.z * 4 + self.y
        self.sib = device(self.z, self.y, 1 - self.c, self.x)

    def near(self, axis, d):
        if axis == 0:
            return device(rem4(self.z + d), self.y, self.c, self.x)
        if axis == 1:
            return device(self.z, rem4(self.y + d), self.c, self.x)
        return device(self.z, self.y, self.c, rem4(self.x + d))

    def along(self, d):
        return (lax.rem(self.chip + d + 16, 16) * 2 + self.c, self.x)


class Gather:
    def __init__(self, r, ref, rows, cut, lanes, first, send, recv):
        self.r, self.ref, self.rows, self.cut, self.lanes = r, ref, rows, cut, lanes
        self.first, self.send, self.recv, self.sent = first, send, recv, []

    def copy(self, phase, d, part, to, i):
        r = self.r
        axis = self.first if phase == 0 else 1 - self.first
        z, y = (rem4(r.z + d), r.y) if axis == 0 else (r.z, rem4(r.y + d))
        if phase == 0:
            rows = (pl.ds(0, self.rows), pl.ds(0, self.cut), pl.ds(self.cut, self.rows - self.cut))[part]
            ref = self.ref.at[z, y, rows, self.lanes]
        else:
            many = (pl.ds(0, 4), pl.ds(0, 2), pl.ds(2, 2))[part]
            ref = self.ref.at[z, many, :, self.lanes] if axis == 0 else self.ref.at[many, y, :, self.lanes]
        j = phase * 6 + i
        return remote(ref, ref, self.send.at[j], self.recv.at[j], r.near(axis, to))

    def start(self, *a):
        copy = self.copy(*a)
        copy.start()
        self.sent.append(copy)

    def first_halves(self, phase):
        self.start(phase, 0, 1, 1, 0)
        self.start(phase, 0, 2, -1, 1)

    def second_halves(self, phase):
        self.start(phase, 0, 2, 1, 2)
        self.start(phase, 0, 1, -1, 3)

    def forward(self, phase):
        self.copy(phase, -1, 1, 1, 0).wait_recv()
        self.start(phase, -1, 1, 1, 4)
        self.copy(phase, 1, 2, -1, 1).wait_recv()
        self.start(phase, 1, 2, -1, 5)

    def finish(self, phase):
        self.copy(phase, -1, 2, 1, 2).wait_recv()
        self.copy(phase, 1, 1, -1, 3).wait_recv()
        self.copy(phase, -2, 1, 1, 4).wait_recv()
        self.copy(phase, 2, 2, -1, 5).wait_recv()

    def drain(self):
        for copy in self.sent:
            copy.wait_send()
        self.sent = []


class Both:
    def __init__(self, parts):
        self.parts = parts

    def step(self, i):
        for p in self.parts:
            if i == 1:
                p.first_halves(0)
                p.second_halves(0)
            elif i == 2:
                p.forward(0)
            elif i == 3:
                p.finish(0)
                p.first_halves(1)
            elif i == 4:
                p.second_halves(1)
            elif i == 5:
                p.forward(1)
            elif i == 6:
                p.finish(1)

    def drain(self):
        for p in self.parts:
            p.drain()


class Trade:
    def __init__(self, r, axis, src, land, send, recv):
        self.r, self.axis, self.src, self.land, self.send, self.recv = r, axis, src, land, send, recv
        self.me = (r.z, r.y, r.x)[axis]

    def copy(self, d):
        return remote(
            self.src(rem4(self.me + d)), self.land.at[self.me], self.send.at[d - 1], self.recv.at[d - 1],
            self.r.near(self.axis, d),
        )

    def begin(self):
        for d in (2, 1, 3):
            self.copy(d).start()

    def end(self):
        for d in (1, 3, 2):
            landed = self.land.at[rem4(self.me - d)]
            remote(landed, landed, self.send.at[d - 1], self.recv.at[d - 1], self.r.near(self.axis, d)).wait_recv()

    def drain(self):
        for d in (1, 2, 3):
            self.copy(d).wait_send()


class Scatter:
    def __init__(self, r, ref, lanes, at, first, bufs, send, recv):
        self.r, self.ref, self.lanes, self.at = r, ref, lanes, at
        self.first, self.bufs, self.send, self.recv, self.sent = first, bufs, send, recv, []

    def unit(self, phase, d, part):
        r = self.r
        axis = self.first if phase == 0 else 1 - self.first
        z, y = (rem4(r.z + d), r.y) if axis == 0 else (r.z, rem4(r.y + d))
        if phase == 1:
            rows = pl.ds(64 * part, 64)
            return self.ref.at[z, y, rows, self.lanes]
        many = pl.ds(2 * part, 2)
        return self.ref.at[z, many, :, self.lanes] if axis == 0 else self.ref.at[many, y, :, self.lanes]

    def landing(self, phase, i):
        return self.bufs[phase].at[i, :, :, self.at] if phase == 0 else self.bufs[phase].at[i, :, self.at]

    def copy(self, phase, d, part, to, i):
        j = phase * 6 + i
        axis = self.first if phase == 0 else 1 - self.first
        return remote(
            self.unit(phase, d, part), self.landing(phase, i), self.send.at[j], self.recv.at[j],
            self.r.near(axis, to),
        )

    def start(self, *a):
        copy = self.copy(*a)
        copy.start()
        self.sent.append(copy)

    def arrived(self, phase, i):
        self.copy(phase, 0, 0, 1, i).wait_recv()

    def add(self, phase, d, part, many):
        unit = self.unit(phase, d, part)
        lands = [self.landing(phase, i) for i in many]
        if phase == 0:
            def body(i):
                k, rows = i // 4, span(lax.rem(i, 4) * 32, 32)
                total = unit[k, rows, :].astype(F32)
                for l in lands:
                    total = total + l[k, rows, :].astype(F32)
                unit[k, rows, :] = total.astype(BF16)
            loop(8, body)
        else:
            def body(i):
                rows = span(i * 32, 32)
                total = unit[rows, :].astype(F32)
                for l in lands:
                    total = total + l[rows, :].astype(F32)
                unit[rows, :] = total.astype(BF16)
            loop(2, body)

    def far(self, phase):
        self.start(phase, 2, 0, 1, 0)
        self.start(phase, 2, 1, -1, 1)

    def early(self, phase):
        self.start(phase, 1, 1, 1, 3)
        self.start(phase, -1, 0, -1, 4)

    def forward(self, phase):
        self.arrived(phase, 0)
        self.add(phase, 1, 0, (0,))
        self.start(phase, 1, 0, 1, 2)
        self.arrived(phase, 1)
        self.add(phase, -1, 1, (1,))
        self.start(phase, -1, 1, -1, 5)

    def finish(self, phase):
        self.arrived(phase, 4)
        self.arrived(phase, 2)
        self.add(phase, 0, 0, (2, 4))
        self.arrived(phase, 3)
        self.arrived(phase, 5)
        self.add(phase, 0, 1, (3, 5))

    def drain(self):
        for copy in self.sent:
            copy.wait_send()
        self.sent = []


class CrossSum:
    def __init__(self, r, part, got, mid, one, two, send, recv):
        self.r, self.part, self.got, self.mid, self.one, self.two = r, part, got, mid, one, two
        self.send, self.recv, self.sent = send, recv, []

    def start(self, copy):
        copy.start()
        self.sent.append(copy)

    def rows(self, c, x):
        return span((c * 4 + x) * 32, 32)

    def pair(self, d):
        x = rem4(self.r.x + d)
        return remote(
            self.part.at[self.rows(1 - self.r.c, x)], self.got.at[x],
            self.send.at[d], self.recv.at[d], self.r.sib,
        )

    def begin(self):
        for d in (2, 1, 3, 0):
            self.start(self.pair(d))

    def pairsum(self, d):
        self.pair(d).wait_recv()
        x = rem4(self.r.x + d)
        rows = self.rows(self.r.c, x)
        self.mid[x] = (self.part[rows].astype(F32) + self.got[x].astype(F32)).astype(BF16)

    def far(self, side):
        x = rem4(self.r.x + 2)
        return remote(
            self.mid.at[x, pl.ds(16 * side, 16)], self.one.at[side],
            self.send.at[4 + side], self.recv.at[4 + side], self.r.near(2, 1 - 2 * side),
        )

    def late(self, side, summed):
        d = 1 - 2 * side
        x = rem4(self.r.x + d)
        half = side if summed else 1 - side
        j = 6 + side * 2 + summed
        return remote(
            self.mid.at[x, pl.ds(16 * half, 16)], self.two.at[side, pl.ds(16 * half, 16)],
            self.send.at[j], self.recv.at[j], self.r.near(2, d),
        )

    def middle(self):
        self.near_half()
        self.far_half()

    def near_half(self):
        self.pairsum(2)
        self.start(self.far(0))
        self.start(self.far(1))
        self.pairsum(1)
        self.start(self.late(0, 0))
        self.pairsum(3)
        self.start(self.late(1, 0))

    def far_half(self):
        for side in range(2):
            self.far(side).wait_recv()
            x = rem4(self.r.x + 1 - 2 * side)
            rows = pl.ds(16 * side, 16)
            self.mid[x, rows] = (self.mid[x, rows].astype(F32) + self.one[side].astype(F32)).astype(BF16)
            self.start(self.late(side, 1))

    def end(self):
        self.pair(0).wait_recv()
        for side in range(2):
            self.late(side, 0).wait_recv()
            self.late(side, 1).wait_recv()

    def result(self, rows):
        base = (self.r.c * 4 + self.r.x) * 32
        own = self.part[pl.ds(pl.multiple_of(base + rows.start, rows.size), rows.size)].astype(F32)
        own = own + self.got[self.r.x, rows].astype(F32)
        return own + self.two[0, rows].astype(F32) + self.two[1, rows].astype(F32)

    def drain(self):
        for copy in self.sent:
            copy.wait_send()
        self.sent = []


class CrossGather:
    def __init__(self, r, ref, both, send, recv):
        self.r, self.ref, self.both, self.send, self.recv, self.sent = r, ref, both, send, recv, []

    def start(self, copy):
        copy.start()
        self.sent.append(copy)

    def rows(self, d, part, sibling=False):
        c = 1 - self.r.c if sibling else self.r.c
        base = rem4(self.r.x + d) * 32
        if self.both:
            base = base + c * 128
        if part is None:
            return self.ref.at[pl.ds(pl.multiple_of(base, 32), 32)]
        return self.ref.at[pl.ds(pl.multiple_of(base + 16 * part, 16), 16)]

    def ring(self, d, part, to, i):
        ref = self.rows(d, part)
        return remote(ref, ref, self.send.at[i], self.recv.at[i], self.r.near(2, to))

    def pair(self, d, sibling=False):
        ref = self.rows(d, None, sibling)
        return remote(ref, ref, self.send.at[6 + d % 4], self.recv.at[6 + d % 4], self.r.sib)

    def begin(self):
        self.start(self.ring(0, 0, 1, 0))
        self.start(self.ring(0, 1, -1, 1))
        self.start(self.ring(0, 1, 1, 2))
        self.start(self.ring(0, 0, -1, 3))
        if self.both:
            self.start(self.pair(0))

    def middle(self):
        self.ring(-1, 0, 1, 0).wait_recv()
        self.start(self.ring(-1, 0, 1, 4))
        self.ring(1, 1, -1, 1).wait_recv()
        self.start(self.ring(1, 1, -1, 5))
        self.ring(-1, 1, 1, 2).wait_recv()
        self.ring(1, 0, -1, 3).wait_recv()
        if self.both:
            self.start(self.pair(-1))
            self.start(self.pair(1))

    def end(self):
        self.ring(-2, 0, 1, 4).wait_recv()
        self.ring(2, 1, -1, 5).wait_recv()
        if self.both:
            self.start(self.pair(2))
            for d in (0, -1, 1, 2):
                self.pair(d, True).wait_recv()

    def drain(self):
        for copy in self.sent:
            copy.wait_send()
        self.sent = []


class Refs:
    pass


SCRATCH = {
    "other": ((64, LANES_A + LANES_B), BF16),
    "tab": ((8, 16, 256), F32),
    "ga": ((4, 4, 128, LANES_A), BF16),
    "gb": ((4, 4, 128, LANES_B), BF16),
    "s0a": ((6, 2, 128, LANES_A), BF16),
    "s0b": ((6, 2, 128, LANES_B), BF16),
    "s1a": ((6, 64, LANES_A), BF16),
    "s1b": ((6, 64, LANES_B), BF16),
    "da": ((4, 4, 128, 384), BF16),
    "db": ((4, 4, 128, 384), BF16),
    "sib_a": ((64, LANES_A), BF16),
    "sib_b": ((64, LANES_B), BF16),
    "gains_y": ((4, 16, 128), F32),
    "gains_all": ((4, 4, 16, 128), F32),
    "gains": ((8, 2048), F32),
    "gain_in": ((8, 128), F32),
    "taps": ((8, 768), F32),
    "keep": ((256, 256), F32),
    "gy": ((256, 2048), BF16),
    "n1": ((272, 2048), BF16),
    "n2": ((256, 2048), BF16),
    "dh": ((256, 2048), BF16),
    "part": ((256, 2048), BF16),
    "mid": ((4, 32, 2048), BF16),
    "part_f": ((256, 2048), BF16),
    "mid_f": ((4, 32, 2048), BF16),
    "got": ((4, 4, 32, 2048), BF16),
    "one": ((4, 2, 16, 2048), BF16),
    "two": ((4, 2, 32, 2048), BF16),
    "bo": ((128, 2048), BF16),
    "gt": ((128, 2048), BF16),
    "h": ((32, 2048), F32),
    "dhf": ((32, 2048), F32),
    "p": ((272, 768), F32),
    "q0": ((256, 256), F32),
    "q1": ((256, 256), F32),
    "q2": ((256, 256), F32),
    "u": ((256, 256), F32),
    "v": ((256, 256), F32),
    "z": ((256, 256), BF16),
    "st_re": ((257, 16, 256), F32),
    "st_im": ((257, 16, 256), F32),
    "ends_y": ((4, 32, 256), F32),
    "ends_z": ((4, 32, 256), F32),
    "backs_y": ((4, 32, 256), F32),
    "backs_z": ((4, 32, 256), F32),
    "gu": ((256, 1408), F32),
    "act": ((256, 768), BF16),
    "dgu": ((256, 1408), BF16),
    "dv": ((256, 256), F32),
    "dq": ((264, 768), F32),
    "dp": ((256, 768), BF16),
    "small_y": ((4, 80, 256), BF16),
    "small_z": ((4, 80, 256), BF16),
    "small_sum": ((80, 256), F32),
    "small_sib": ((80, 256), F32),
    "ggain": ((8, 2048), F32),
    "gg_z": ((4, 8, 512), F32),
    "gg_1": ((8, 512), F32),
    "gg_y": ((4, 8, 128), F32),
    "gg_2": ((8, 128), F32),
    "gg_s": ((8, 128), F32),
    "gg_x": ((4, 8, 128), F32),
    "gg_out": ((8, 128), F32),
}
SEMS = {
    "w": (5, 2, 12), "w_sib": (5, 2), "gain_sib": (), "keep_s": (), "gy_s": (), "n1_s": (),
    "edge": (), "dq_s": (), "trade": (11, 3), "sum": (4, 10), "cg": (4, 10),
    "rs": (5, 2, 12), "rs_sib": (5, 2), "small_x": (), "gg_s": (),
}


def kernel(*refs):
    names = [
        "in_w", "out_w", "gate_w", "up_w", "down_w", "gain_1", "gain_2", "resets", "tok", "cot", "conv_w",
        "decay", "angle", "res_re", "res_im",
    ]
    outs = ["block_out", "grad_tok", "grad_w", "grad_small", "grad_gain"]
    k = Refs()
    for name, ref in zip(names + outs + list(SCRATCH), refs):
        setattr(k, name, ref)
    rest = refs[len(names) + len(outs) + len(SCRATCH):]
    S, R = {}, {}
    for i, name in enumerate(SEMS):
        S[name], R[name] = rest[2 * i], rest[2 * i + 1]
    local = rest[2 * len(SEMS)]
    r = Rings()
    g = (k.ga, k.gb)
    z, y, c, x = r.z, r.y, r.c, r.x

    barrier = pltpu.get_barrier_semaphore()
    peers = [r.sib] + [r.near(a, d) for a in range(3) for d in (1, 2, 3)] + [r.along(1), r.along(-1)]
    for peer in peers:
        pl.semaphore_signal(barrier, inc=1, device_id=peer, device_id_type=MESH)
    pl.semaphore_wait(barrier, len(peers))

    def lanes(n, h):
        o, w = CHUNKS[n][h]
        return pl.ds(o, w)

    def columns(n, start, stop):
        (oa, wa), (ob, _) = WHOLE[n]
        parts = []
        if start < wa:
            parts.append(g[0][:, :, :, oa + start:oa + min(stop, wa)])
        if stop > wa:
            parts.append(g[1][:, :, :, ob + max(start - wa, 0):ob + stop - wa])
        return jnp.concatenate([p.reshape(2048, p.shape[-1]) for p in parts], 1)

    def weight(n, h, i):
        o, w = WHOLE[n][h]
        return g[h][i, :, :, o:o + w].reshape(512, w)

    trades = []

    def trade(axis, src, land):
        i = len(trades)
        trades.append(Trade(r, axis, src if callable(src) else lambda _: src, land, S["trade"].at[i], R["trade"].at[i]))
        return trades[-1]

    my64 = span(c * 64, 64)
    my128 = span(c * 128, 128)
    gather = [
        Both([Gather(r, g[h], 128, 64, lanes(n, h), 1 - h, S["w"].at[n, h], R["w"].at[n, h]) for h in range(2)])
        for n in range(5)
    ]

    def put(cc, n, sink):
        wa = WHOLE[n][0][1]

        def store(start, value):
            stop = start + value.shape[1]
            if start < wa:
                sink(0, WHOLE[n][0][0] + start, value[:, :min(stop, wa) - start])
            if stop > wa:
                sink(1, WHOLE[n][1][0] + max(start - wa, 0), value[:, max(wa - start, 0):])

        def main(ref):
            return ref[:, pl.ds(pl.multiple_of(cc * 640, 128), 640)]

        def tail(ref):
            a = ref[:, 1280:1408].astype(F32)
            return jnp.where(cc == 0, a[:, 0:64], a[:, 64:128])

        channels = pl.ds(pl.multiple_of(cc * 256, 256), 256)
        if n == IN:
            for b in range(3):
                store(b * 256, k.in_w[b, :, channels])
        elif n == OUT:
            store(0, k.out_w[:, channels])
        elif n == GU:
            store(0, main(k.gate_w))
            store(640, main(k.up_w))
            store(1280, jnp.concatenate([tail(k.gate_w), tail(k.up_w)], 1).astype(BF16))
        else:
            store(0, main(k.down_w))
            store(640, jnp.concatenate([tail(k.down_w), jnp.zeros((64, 64), F32)], 1).astype(BF16))

    def to_other(h, at, value):
        at = at + (LANES_A if h else 0)
        k.other[:, at:at + value.shape[1]] = value

    def to_own(h, at, value):
        g[h][z, y, my64, at:at + value.shape[1]] = value

    def weight_sib(n, h):
        o, w = CHUNKS[n][h]
        return remote(
            k.other.at[:, pl.ds(o + (LANES_A if h else 0), w)], g[h].at[z, y, my64, lanes(n, h)],
            S["w_sib"].at[n, h], R["w_sib"].at[n, h], r.sib,
        )

    eight = span(c * 8, 8)
    side = lax.broadcasted_iota(jnp.int32, (1, 128), 1) // 64 == c
    for i, ref in enumerate((k.gain_1, k.gain_2)):
        a = ref[...].astype(F32)
        k.gain_in[i:i + 1, :] = jnp.where(side, jnp.concatenate([a, a], 1), 0.0)
    k.gain_in[2:8, :] = jnp.zeros((6, 128), F32)
    gain_sib = remote(k.gain_in, k.gains_y.at[y, eight], S["gain_sib"], R["gain_sib"], r.sib)
    gain_sib.start()
    k.gains_y[y, eight] = k.gain_in[...]
    for n in (IN, OUT, GU, DOWN):
        put(1 - c, n, to_other)
        for m in (GU, GU_2) if n == GU else (n,):
            for h in range(2):
                weight_sib(m, h).start()
        put(c, n, to_own)
    keep = 1.0 - k.resets[...].astype(F32)
    keep = jnp.broadcast_to(keep, (128, 128)).T
    k.keep[my128] = jnp.concatenate([keep, keep], 1)
    keep_sib = remote(k.keep.at[my128], k.keep.at[my128], S["keep_s"], R["keep_s"], r.sib)
    keep_sib.start()
    gy_sib = remote(k.cot, k.gy.at[my128], S["gy_s"], R["gy_s"], r.sib)
    k.gy[my128] = k.cot[...]

    channels = pl.ds(pl.multiple_of(c * 256, 256), 256)
    decay, angle = k.decay[:, channels], k.angle[:, channels]
    size = jnp.exp(-decay)
    gin = jnp.sqrt(-expm1(-2.0 * decay))
    power = (size * jnp.cos(angle), size * jnp.sin(angle))
    k.tab[0], k.tab[1] = power
    k.tab[2] = gin * k.res_re[:, channels]
    k.tab[3] = gin * k.res_im[:, channels]
    for _ in range(8):
        power = (power[0] * power[0] - power[1] * power[1], 2.0 * power[0] * power[1])
    k.tab[4], k.tab[5] = power
    k.tab[6] = gin
    k.tab[7] = size * size / gin
    for i in range(3):
        for b in range(3):
            k.taps[i:i + 1, b * 256:b * 256 + 256] = k.conv_w[i, b:b + 1, channels]

    def ag(n, i):
        if i == 1:
            for h in range(2):
                weight_sib(n, h).wait_recv()
        gather[n].step(i)

    tasks = {}

    def task(f):
        tasks[f.__name__] = f
        return f

    def at(point):
        for name, *rest in PLAN.get(point, ()):
            tasks[name](*rest)

    task(ag)
    at("start")
    gain_y = trade(1, k.gains_y.at[y], k.gains_y)
    gain_z = trade(0, k.gains_y, k.gains_all)
    gain_sib.wait_recv()
    gain_y.begin()
    at("gain_y")
    gain_y.end()
    gain_z.begin()
    k.gains_all[z] = k.gains_y[...]
    at("gain_z")
    gain_z.end()
    for i in range(16):
        k.gains[:, i * 128:(i + 1) * 128] = k.gains_all[i // 4, i % 4, 0:8] + k.gains_all[i // 4, i % 4, 8:16]

    def norm_one(i):
        rows = span(i * 16, 16)
        a = k.tok[rows, :].astype(F32)
        s = lax.rsqrt(jnp.mean(a * a, axis=-1, keepdims=True) + EPSILON)
        k.n1[pl.ds(pl.multiple_of(16 + c * 128 + i * 16, 16), 16), :] = (a * s * k.gains[0:1, :]).astype(BF16)
    loop(8, norm_one)

    def n1_rows(c):
        return k.n1.at[pl.ds(pl.multiple_of(16 + c * 128, 16), 128)]

    n1_sib = remote(n1_rows(c), n1_rows(c), S["n1_s"], R["n1_s"], r.sib)
    n1_sib.start()
    at("n1")
    k_other = span((1 - c) * 128, 128)
    remote(n1_rows(1 - c), n1_rows(1 - c), S["n1_s"], R["n1_s"], r.sib).wait_recv()
    edge = remote(k.n1.at[256:272], k.n1.at[0:16], S["edge"], R["edge"], r.along(1))
    edge.start()
    gy_sib.start()
    at("edge")

    edge.wait_recv()
    at("project")

    def project(_):
        for o in range(0, 768, 256):
            k.p[:, o:o + 256] = nn(k.n1[...], columns(IN, o, o + 256))
    loop(1, project)

    def round_p(i):
        rows = span(i * 16, 16)
        k.p[rows, :] = k.p[rows, :].astype(BF16).astype(F32)
    loop(17, round_p)
    remote(k.keep.at[k_other], k.keep.at[k_other], S["keep_s"], R["keep_s"], r.sib).wait_recv()
    at("short")

    def masks(i):
        rows = span(i * 16, 16)
        near = k.keep[rows, :]
        before = k.keep[span(jnp.maximum(i * 16 - 8, 0), 8), :]
        first = jnp.where(i == 0, 1.0, before[7:8, :])
        shifted = jnp.concatenate([first, near[0:15, :]], 0)
        return near, near * shifted

    def short(i):
        near, far = masks(i)
        ext = k.p[pl.ds(pl.multiple_of(i * 16 + 8, 8), 24), :]
        q = []
        for b in range(3):
            l = slice(b * 256, b * 256 + 256)
            e = ext[:, l]
            q.append(
                k.taps[0:1, l] * e[8:24] + near * k.taps[1:2, l] * e[7:23] + far * k.taps[2:3, l] * e[6:22]
            )
        rows = span(i * 16, 16)
        k.q0[rows, :] = q[0]
        k.q1[rows, :] = q[1]
        k.q2[rows, :] = q[2]
        k.u[rows, :] = q[1] * q[2]
    loop(16, short)

    zero = jnp.zeros((16, 256), F32)
    lr, li, cr, ci, pr, pi = (k.tab[i] for i in range(6))

    def advance(re, im, u, keep):
        kr, ki = keep * re, keep * im
        return lr * kr - li * ki + u, lr * ki + li * kr

    def end_state(i, state):
        rows = span(i * 8, 8)
        u, keep = k.u[rows, :], k.keep[rows, :]
        for j in range(8):
            state = advance(*state, u[j:j + 1, :], keep[j:j + 1, :])
        return state

    def times(a, b, g, h):
        return a * g - b * h, a * h + b * g

    def chain(own, ref_y, ref_z, sign, between):
        order = range(4) if sign > 0 else range(3, -1, -1)
        qr, qi = pr, sign * pi

        def put(ref, at, state):
            ref[at, 0:16] = state[0]
            ref[at, 16:32] = state[1]

        def horner(ref, wr, wi, state, here, every):
            for i in order:
                nr, ni = times(wr, wi, *state)
                nr, ni = nr + ref[i, 0:16], ni + ref[i, 16:32]
                use = (i < here) if sign > 0 else (i > here)
                state = (nr, ni) if every else (jnp.where(use, nr, state[0]), jnp.where(use, ni, state[1]))
            return state

        put(ref_y, y, own)
        t = trade(1, ref_y.at[y], ref_y)
        t.begin()
        at(between[0])
        t.end()
        put(ref_z, z, horner(ref_y, qr, qi, (zero, zero), y, True))
        t = trade(0, ref_z.at[z], ref_z)
        t.begin()
        at(between[1])
        t.end()
        w = times(*times(qr, qi, qr, qi), *times(qr, qi, qr, qi))
        return horner(ref_y, qr, qi, horner(ref_z, *w, (zero, zero), z, False), y, False)

    end = fold(32, end_state, (zero, zero))
    enter = chain(end, k.ends_y, k.ends_z, 1, ("ends_y", "ends_z"))
    k.st_re[0] = enter[0]
    k.st_im[0] = enter[1]
    at("scan")

    def scan(i, state):
        rows = span(i * 8, 8)
        u, keep = k.u[rows, :], k.keep[rows, :]
        for j in range(8):
            state = advance(*state, u[j:j + 1, :], keep[j:j + 1, :])
            k.st_re[i * 8 + j + 1] = state[0]
            k.st_im[i * 8 + j + 1] = state[1]
            k.v[pl.ds(i * 8 + j, 1), :] = jnp.sum(cr * state[0] - ci * state[1], axis=0, keepdims=True)
        return state
    fold(32, scan, enter)

    def gated(i):
        rows = span(i * 32, 32)
        k.z[rows, :] = (k.q0[rows, :] * k.v[rows, :]).astype(BF16)
    loop(8, gated)

    at("mix")
    def out_weight(i):
        return jnp.concatenate([weight(OUT, 0, i), weight(OUT, 1, i)], 1)

    def mix(i):
        k.part[:, span(i * 512, 512)] = nt(k.z[...], out_weight(i)).astype(BF16)
    loop(4, mix)

    def cross(i):
        part, mid = (k.part_f, k.mid_f) if i == 1 else (k.part, k.mid)
        return CrossSum(r, part, k.got.at[i], mid, k.one.at[i], k.two.at[i], S["sum"].at[i], R["sum"].at[i])

    s_mix = cross(0)
    s_mix.begin()
    at("mix_0")
    s_mix.near_half()
    at("mix_1")
    s_mix.far_half()
    at("mix_2")
    s_mix.end()

    own = (c * 4 + x) * 32

    def norm_two(i):
        rows = pl.ds(pl.multiple_of(i * 16, 16), 16)
        a = k.tok[pl.ds(pl.multiple_of(x * 32 + i * 16, 16), 16), :].astype(F32) + s_mix.result(rows)
        k.h[rows, :] = a
        s = lax.rsqrt(jnp.mean(a * a, axis=-1, keepdims=True) + EPSILON)
        k.n2[pl.ds(pl.multiple_of(own + i * 16, 16), 16), :] = (a * s * k.gains[1:2, :]).astype(BF16)
    loop(2, norm_two)
    g_n2 = CrossGather(r, k.n2, True, S["cg"].at[0], R["cg"].at[0])
    g_n2.begin()
    at("n2_0")
    g_n2.middle()
    at("n2_1")
    g_n2.end()
    s_mix.drain()
    at("ff")

    def gate_up(_):
        for o in range(0, 1408, 256):
            e = min(o + 256, 1408)
            k.gu[:, o:e] = nn(k.n2[...], columns(GU, o, e))
    loop(1, gate_up)
    def halves(t):
        last = t[:, 1280:1408]
        turned = jnp.concatenate([last[:, 64:128], last[:, 0:64]], 1)
        return jnp.concatenate([t[:, 0:640], last], 1), jnp.concatenate([t[:, 640:1280], turned], 1)

    used = lax.broadcasted_iota(jnp.int32, (1, 768), 1) < 704

    def activate(i):
        rows = span(i * 16, 16)
        gate, up = halves(k.gu[rows, :])
        k.act[rows, :] = jnp.where(used, gate * jax.nn.sigmoid(gate) * up, 0.0).astype(BF16)
    loop(16, activate)

    def down_weight(i):
        return jnp.concatenate([weight(DOWN, 0, i), weight(DOWN, 1, i)], 1)

    s_ffn = cross(1)
    g_bo = CrossGather(r, k.bo, False, S["cg"].at[1], R["cg"].at[1])
    out_bo = pltpu.make_async_copy(k.bo, k.block_out, local.at[0])

    @task
    def ffn_0():
        def ffn(i):
            k.part_f[:, span(i * 512, 512)] = nt(k.act[...], down_weight(i)).astype(BF16)
        loop(4, ffn)
        s_ffn.begin()

    @task
    def ffn_1():
        s_ffn.near_half()

    @task
    def ffn_2():
        s_ffn.far_half()

    @task
    def ffn_3():
        s_ffn.end()

        def top(i):
            rows = pl.ds(pl.multiple_of(i * 16, 16), 16)
            here = pl.ds(pl.multiple_of(x * 32 + i * 16, 16), 16)
            k.bo[here, :] = (k.h[rows, :] + s_ffn.result(rows)).astype(BF16)
        loop(2, top)
        s_ffn.drain()
        g_bo.begin()

    @task
    def ffn_4():
        g_bo.middle()

    @task
    def ffn_5():
        g_bo.end()
        out_bo.start()

    d_refs = (k.da, k.db)
    scatter = []
    for n in range(5):
        scatter.append([])
        for h in range(2):
            ref, here = (d_refs[h], pl.ds(0, 384)) if n == DOWN else (g[h], lanes(n, h))
            bufs = ((k.s0a, k.s1a), (k.s0b, k.s1b))[h]
            scatter[n].append(Scatter(r, ref, here, lanes(n, h), h, bufs, S["rs"].at[n, h], R["rs"].at[n, h]))
    sib_bufs = (k.sib_a, k.sib_b)

    def rs_sib(n, h):
        s = scatter[n][h]
        return remote(
            s.ref.at[z, y, span((1 - c) * 64, 64), s.lanes], sib_bufs[h].at[:, s.at],
            S["rs_sib"].at[n, h], R["rs_sib"].at[n, h], r.sib,
        )

    @task
    def rs(n, i):
        for h in range(2):
            s = scatter[n][h]
            if i == 0:
                s.far(0)
            elif i == 1:
                s.early(0)
            elif i == 2:
                s.forward(0)
            elif i == 3:
                s.finish(0)
                s.far(1)
                s.early(1)
            elif i == 4:
                s.forward(1)
            elif i == 5:
                s.finish(1)
                rs_sib(n, h).start()

    @task
    def wg(n):
        a, b, first = {
            IN: (k.n1, k.dp, 16), OUT: (k.dh, k.z, 0), GU: (k.n2, k.dgu, 0), DOWN: (k.gy, k.act, 0)
        }[n]
        if n == GU:
            gather[GU_2].drain()
        if n != DOWN:
            gather[n].drain()
        (oa, wa), (ob, wb) = ((0, 384), (0, 384)) if n == DOWN else WHOLE[n]
        into = d_refs if n == DOWN else g

        def weight_grad(i):
            t = tn(a[pl.ds(first, 256), pl.ds(pl.multiple_of(i * 512, 512), 512)], b[...]).astype(BF16)
            into[0][i, :, :, oa:oa + wa] = t[:, 0:wa].reshape(4, 128, wa)
            into[1][i, :, :, ob:ob + wb] = t[:, wa:wa + wb].reshape(4, 128, wb)
        weight_grad.width = wa + wb
        loop(4, weight_grad)

    remote(k.gy.at[k_other], k.gy.at[k_other], S["gy_s"], R["gy_s"], r.sib).wait_recv()
    at("act")

    def d_act(_):
        for o in range(0, 768, 256):
            k.dq[0:256, o:o + 256] = nn(k.gy[...], columns(DOWN, o, o + 256))
    loop(1, d_act)
    at("da")

    def d_gates(i):
        rows = span(i * 16, 16)
        gate, up = halves(k.gu[rows, :])
        da = k.dq[rows, :]
        sg = jax.nn.sigmoid(gate)
        dgate = da * up * sg * (1.0 + gate * (1.0 - sg))
        dup = da * (gate * sg)
        last = jnp.concatenate([dgate[:, 640:704], dup[:, 640:704]], 1)
        k.dgu[rows, :] = jnp.concatenate([dgate[:, 0:640], dup[:, 0:640], last], 1).astype(BF16)
    loop(16, d_gates)

    def d_n2(i):
        w = jnp.concatenate([weight(GU, 0, i), weight(GU, 1, i)], 1)
        k.part[:, span(i * 512, 512)] = nt(k.dgu[...], w).astype(BF16)
    loop(4, d_n2)
    s_dn2 = cross(2)
    s_dn2.begin()
    at("dn2_0")
    s_dn2.near_half()
    at("dn2_1")
    s_dn2.far_half()
    at("dn2_2")
    s_dn2.end()

    def d_norm_two(i):
        rows = pl.ds(pl.multiple_of(i * 16, 16), 16)
        a = k.h[rows, :]
        s = lax.rsqrt(jnp.mean(a * a, axis=-1, keepdims=True) + EPSILON)
        hat = a * s
        dn = s_dn2.result(rows)
        dng = dn * k.gains[1:2, :]
        gy = k.gy[pl.ds(pl.multiple_of(own + i * 16, 16), 16), :].astype(F32)
        dh = gy + s * (dng - hat * jnp.mean(dng * hat, axis=-1, keepdims=True))
        k.dhf[rows, :] = dh
        k.dh[pl.ds(pl.multiple_of(own + i * 16, 16), 16), :] = dh.astype(BF16)
        t = jnp.sum(dn * hat, axis=0, keepdims=True)

        @pl.when(i == 0)
        def _():
            k.ggain[...] = jnp.zeros((8, 2048), F32)
            k.ggain[1:2, :] = t

        @pl.when(i > 0)
        def _():
            k.ggain[1:2, :] += t
    loop(2, d_norm_two)
    s_dn2.drain()
    g_dh = CrossGather(r, k.dh, True, S["cg"].at[2], R["cg"].at[2])
    g_dh.begin()
    at("dh_0")
    g_dh.middle()
    at("dh_1")
    g_dh.end()
    at("dz")

    def d_z(_):
        k.dv[...] = nn(k.dh[...], columns(OUT, 0, 256))
    loop(1, d_z)

    def d_gated(i):
        rows = span(i * 32, 32)
        dz = k.dv[rows, :]
        k.dq[rows, 0:256] = dz * k.v[rows, :]
        k.dv[rows, :] = dz * k.q0[rows, :]
    loop(8, d_gated)

    def retreat(a, b, keep):
        ka, kb = keep * a, keep * b
        return ka, kb, lr * ka + li * kb, lr * kb - li * ka

    def start_state(i, state):
        rows = span((31 - i) * 8, 8)
        dv, keep = k.dv[rows, :], k.keep[rows, :]
        for j in reversed(range(8)):
            a = cr * dv[j:j + 1, :] + state[0]
            b = state[1] - ci * dv[j:j + 1, :]
            _, _, pa, pb = retreat(a, b, keep[j:j + 1, :])
            state = (pa, pb)
        return state

    begin = fold(32, start_state, (zero, zero))
    arrive = chain(begin, k.backs_y, k.backs_z, -1, ("backs_y", "backs_z"))
    at("adjoint")

    def adjoint(i, carry):
        rows = span((31 - i) * 8, 8)
        dv, keep = k.dv[rows, :], k.keep[rows, :]
        for j in reversed(range(8)):
            t = (31 - i) * 8 + j
            d = dv[j:j + 1, :]
            a = cr * d + carry[0]
            b = carry[1] - ci * d
            k.u[pl.ds(t, 1), :] = jnp.sum(a, axis=0, keepdims=True)
            _, _, pa, pb = retreat(a, b, keep[j:j + 1, :])
            carry = (pa, pb)
        return carry

    fold(32, adjoint, arrive)

    def d_poles(i, carry):
        pa, pb, dcr, dci, dlr, dli = carry
        rows = span((31 - i) * 8, 8)
        dv, keep = k.dv[rows, :], k.keep[rows, :]
        for j in reversed(range(8)):
            t = (31 - i) * 8 + j
            d = dv[j:j + 1, :]
            a = cr * d + pa
            b = pb - ci * d
            dcr = dcr + d * k.st_re[t + 1]
            dci = dci - d * k.st_im[t + 1]
            ka, kb, pa, pb = retreat(a, b, keep[j:j + 1, :])
            sr, si = k.st_re[t], k.st_im[t]
            dlr = dlr + ka * sr + kb * si
            dli = dli + kb * sr - ka * si
        return pa, pb, dcr, dci, dlr, dli

    def d_branches(i):
        rows = span(i * 32, 32)
        du = k.u[rows, :]
        k.dq[rows, 256:512] = du * k.q2[rows, :]
        k.dq[rows, 512:768] = du * k.q1[rows, :]
    loop(8, d_branches)
    dq_next = remote(k.dq.at[0:8], k.dq.at[256:264], S["dq_s"], R["dq_s"], r.along(-1))
    dq_next.start()
    at("dq")
    dq_next.wait()

    last = jnp.where(r.chip < 15, 1.0, 0.0)

    def d_short(i, taps):
        d = k.dq[pl.ds(pl.multiple_of(i * 16, 16), 24), :]
        near, far = masks(i)
        j = jnp.minimum(i * 16 + 16, 248)
        after = k.keep[span(j, 8), :]
        inside = i < 15
        tail_near = jnp.where(inside, after, last)
        tail_far = jnp.where(
            inside, after * jnp.concatenate([near[15:16, :], after[0:7, :]], 0), last
        )
        near = jnp.concatenate([near, tail_near], 0)
        far = jnp.concatenate([far, tail_far], 0)
        ext = k.p[pl.ds(pl.multiple_of(i * 16 + 8, 8), 24), :]
        rows = span(i * 16, 16)
        new = []
        for b in range(3):
            l = slice(b * 256, b * 256 + 256)
            e, db = ext[:, l], d[:, l]
            dn, df = near * db, far * db
            k.dp[rows, l] = (
                k.taps[0:1, l] * db[0:16] + k.taps[1:2, l] * dn[1:17] + k.taps[2:3, l] * df[2:18]
            ).astype(BF16)
            new.append(taps[3 * 0 + b] + jnp.sum(e[8:24] * db[0:16], axis=0, keepdims=True))
            new.append(taps[3 * 1 + b] + jnp.sum(e[7:23] * dn[0:16], axis=0, keepdims=True))
            new.append(taps[3 * 2 + b] + jnp.sum(e[6:22] * df[0:16], axis=0, keepdims=True))
        return tuple(new[3 * b + t] for t in range(3) for b in range(3))

    line = jnp.zeros((1, 256), F32)
    dtaps = fold(16, d_short, (line,) * 9)

    def d_n1(i):
        w = jnp.concatenate([weight(IN, 0, i), weight(IN, 1, i)], 1)
        k.part[:, span(i * 512, 512)] = nt(k.dp[...], w).astype(BF16)
    loop(4, d_n1)
    s_dn1 = cross(3)
    s_dn1.begin()
    at("dn1_0")

    small_1 = trade(1, k.small_y.at[y], k.small_y)
    small_2 = trade(0, k.small_z.at[z], k.small_z)

    def small_total(ref):
        return sum(ref[j].astype(F32) for j in range(4))

    small_x = remote(k.small_sum, k.small_sib, S["small_x"], R["small_x"], r.sib)

    @task
    def small(i):
        if i == 0:
            _, _, *dpoles = fold(32, d_poles, (*arrive, zero, zero, zero, zero))
            for j in range(4):
                k.small_y[y, 16 * j:16 * j + 16] = dpoles[j].astype(BF16)
            k.small_y[y, 64:80] = jnp.concatenate(list(dtaps) + [jnp.zeros((7, 256), F32)], 0).astype(BF16)
            small_1.begin()
        elif i == 1:
            small_1.end()
            k.small_z[z] = small_total(k.small_y).astype(BF16)
            small_2.begin()
        else:
            small_2.end()
            k.small_sum[...] = small_total(k.small_z)
            dcr, dci, dlr, dli = (k.small_sum[16 * j:16 * j + 16, :] for j in range(4))
            dgin = k.res_re[:, channels] * dcr + k.res_im[:, channels] * dci
            k.small_sum[0:16, :] = dgin * k.tab[7] - (lr * dlr + li * dli)
            k.small_sum[16:32, :] = lr * dli - li * dlr
            k.small_sum[32:48, :] = k.tab[6] * dcr
            k.small_sum[48:64, :] = k.tab[6] * dci
            small_x.start()

    at("dn1_x")
    s_dn1.near_half()
    at("dn1_1")
    s_dn1.far_half()
    at("dn1_2")
    s_dn1.end()

    def d_norm_one(i):
        rows = pl.ds(pl.multiple_of(i * 16, 16), 16)
        here = pl.ds(pl.multiple_of(x * 32 + i * 16, 16), 16)
        a = k.tok[here, :].astype(F32)
        s = lax.rsqrt(jnp.mean(a * a, axis=-1, keepdims=True) + EPSILON)
        hat = a * s
        dn = s_dn1.result(rows)
        dng = dn * k.gains[0:1, :]
        k.gt[here, :] = (
            k.dhf[rows, :] + s * (dng - hat * jnp.mean(dng * hat, axis=-1, keepdims=True))
        ).astype(BF16)
        t = jnp.sum(dn * hat, axis=0, keepdims=True)

        @pl.when(i == 0)
        def _():
            k.ggain[0:1, :] = t

        @pl.when(i > 0)
        def _():
            k.ggain[0:1, :] += t
    loop(2, d_norm_one)
    g_gt = CrossGather(r, k.gt, False, S["cg"].at[3], R["cg"].at[3])
    g_gt.begin()

    def piece(ref, width):
        return lambda i: ref.at[:, pl.ds(pl.multiple_of(i * width, width), width)]

    gg_1 = trade(0, piece(k.ggain, 512), k.gg_z)
    gg_2 = trade(1, piece(k.gg_1, 128), k.gg_y)
    gg_3 = trade(2, k.gg_s, k.gg_x)
    gg_sib = remote(k.gg_2, k.gg_s, S["gg_s"], R["gg_s"], r.sib)
    gg_1.begin()
    k.gg_z[z] = k.ggain[:, span(z * 512, 512)]
    at("gt_0")
    gg_1.end()
    k.gg_1[...] = sum(k.gg_z[j] for j in range(4))
    gg_2.begin()
    k.gg_y[y] = k.gg_1[:, span(y * 128, 128)]
    at("gt_1")
    g_gt.middle()
    at("gt_2")
    gg_2.end()
    k.gg_2[...] = sum(k.gg_y[j] for j in range(4))
    gg_sib.start()
    at("gt_3")
    gg_sib.wait()
    k.gg_s[...] = k.gg_s[...] + k.gg_2[...]
    gg_3.begin()
    k.gg_x[x] = k.gg_s[...]
    g_gt.end()
    out_gt = pltpu.make_async_copy(k.gt, k.grad_tok, local.at[1])
    out_gt.start()
    at("gt_4")
    small_x.wait()
    gg_3.end()
    k.gg_out[...] = sum(k.gg_x[j] for j in range(4))

    copies = [out_bo, out_gt]
    for j, src in enumerate((k.small_sum, k.small_sib)):
        copies.append(pltpu.make_async_copy(src, k.grad_small.at[j], local.at[2 + j]))
    copies.append(pltpu.make_async_copy(k.gg_out, k.grad_gain, local.at[4]))
    for n in range(5):
        for h in range(2):
            rs_sib(n, h).wait()
    for h in range(2):
        o, w = (0, 1280) if h == 0 else (LANES_A, 1152)
        end = o + w
        down, wide = pl.ds(end, 384), pl.ds(o, w)
        copies.append(pltpu.make_async_copy(g[h].at[z, y, my64, pl.ds(0, w)], k.grad_w.at[0, :, wide], local.at[5 + 3 * h]))
        copies.append(pltpu.make_async_copy(d_refs[h].at[z, y, my64], k.grad_w.at[0, :, down], local.at[6 + 3 * h]))
        copies.append(pltpu.make_async_copy(sib_bufs[h], k.grad_w.at[1, :, pl.ds(o, w + 384)], local.at[7 + 3 * h]))
    for copy in copies[2:]:
        copy.start()
    for copy in copies:
        copy.wait()
    for n in range(5):
        gather[n].drain()
        for h in range(2):
            weight_sib(n, h).wait_send()
            scatter[n][h].drain()
    for copy in (gain_sib, keep_sib, gy_sib, n1_sib, edge):
        copy.wait_send()
    for group in trades + [s_dn1, g_n2, g_bo, g_dh, g_gt]:
        group.drain()


def block(*arrays):
    sems = []
    for shape in SEMS.values():
        sems += [pltpu.SemaphoreType.DMA(shape)] * 2
    vmem = pl.BlockSpec(memory_space=pltpu.VMEM)
    return pl.pallas_call(
        kernel,
        out_shape=(
            jax.ShapeDtypeStruct((128, 2048), BF16),
            jax.ShapeDtypeStruct((128, 2048), BF16),
            jax.ShapeDtypeStruct((2, 64, LANES_A + LANES_B), BF16),
            jax.ShapeDtypeStruct((2, 80, 256), F32),
            jax.ShapeDtypeStruct((8, 128), F32),
        ),
        in_specs=[vmem] * len(arrays),
        out_specs=[pl.BlockSpec(memory_space=pl.ANY)] * 5,
        scratch_shapes=[pltpu.VMEM(s, t) for s, t in SCRATCH.values()] + sems + [pltpu.SemaphoreType.DMA((11,))],
        compiler_params=pltpu.CompilerParams(
            collective_id=0, has_side_effects=True, vmem_limit_bytes=63 * 2**20
        ),
        name="block",
    )(*arrays)


def results(*refs):
    sources, refs = refs[:5], refs[5:]
    (bo, gt, g_gain_1, g_in, g_taps, g_decay, g_angle, g_re, g_im, g_out, g_gain_2, g_gate, g_up, g_down) = refs[:14]
    grad_w, small, gain, sems = refs[14:]
    c = lax.rem(lax.axis_index("seq"), 2)
    copies = [
        pltpu.make_async_copy(source, ref, sems.at[i])
        for i, (source, ref) in enumerate(zip(sources, (bo, gt, grad_w, small, gain)))
    ]
    for copy in copies:
        copy.start()
    for copy in copies[::-1]:
        copy.wait()

    def cols(core, n, start, stop):
        wa = WHOLE[n][0][1]
        parts = []
        if start < wa:
            parts.append(grad_w[core, :, WHOLE[n][0][0] + start:WHOLE[n][0][0] + min(stop, wa)])
        if stop > wa:
            o = LANES_A + WHOLE[n][1][0]
            parts.append(grad_w[core, :, o + max(start - wa, 0):o + stop - wa])
        return jnp.concatenate(parts, 1).astype(F32)

    for at, core in ((0, c), (1, 1 - c)):
        for b in range(3):
            g_in[b, :, at * 256:at * 256 + 256] = cols(core, IN, b * 256, b * 256 + 256)
        g_out[:, at * 256:at * 256 + 256] = cols(core, OUT, 0, 256)
        g_gate[:, at * 640:at * 640 + 640] = cols(core, GU, 0, 640)
        g_up[:, at * 640:at * 640 + 640] = cols(core, GU, 640, 1280)
        g_down[:, at * 640:at * 640 + 640] = cols(core, DOWN, 0, 640)
        here = slice(at * 256, at * 256 + 256)
        for i, ref in enumerate((g_decay, g_angle, g_re, g_im)):
            ref[:, here] = small[core, 16 * i:16 * i + 16, :]
        for i in range(3):
            g_taps[i, :, here] = small[core, 64 + 3 * i:67 + 3 * i, :]
    first, second = cols(c, GU, 1280, 1408), cols(1 - c, GU, 1280, 1408)
    g_gate[:, 1280:1408] = jnp.concatenate([first[:, 0:64], second[:, 0:64]], 1)
    g_up[:, 1280:1408] = jnp.concatenate([first[:, 64:128], second[:, 64:128]], 1)
    first, second = cols(c, DOWN, 640, 768), cols(1 - c, DOWN, 640, 768)
    g_down[:, 1280:1408] = jnp.concatenate([first[:, 0:64], second[:, 0:64]], 1)
    for i, ref in enumerate((g_gain_1, g_gain_2)):
        a = gain[i:i + 1, :]
        ref[...] = jnp.where(c == 0, a[:, 0:64], a[:, 64:128])


def on_device(
    tokens, cotangent, resets, norm1_gain, in_weight, conv_weight, pole_decay, pole_angle, residue_re, residue_im,
    out_weight, norm2_gain, gate_weight, up_weight, down_weight,
):
    raw = block(
        in_weight.transpose(1, 0, 2), out_weight, gate_weight, up_weight, down_weight, norm1_gain.reshape(1, 64),
        norm2_gain.reshape(1, 64), resets.reshape(1, 128), tokens, cotangent, conv_weight, pole_decay, pole_angle,
        residue_re, residue_im,
    )
    vmem = pl.BlockSpec(memory_space=pltpu.VMEM)
    shapes = [
        ((128, 2048), BF16), ((128, 2048), BF16), ((1, 64), F32), ((3, 64, 512), F32), ((3, 3, 512), F32),
        ((16, 512), F32), ((16, 512), F32), ((16, 512), F32), ((16, 512), F32), ((64, 512), F32), ((1, 64), F32),
        ((64, 1408), F32), ((64, 1408), F32), ((64, 1408), F32),
    ]
    outs = list(pl.pallas_call(
        results,
        out_shape=[jax.ShapeDtypeStruct(s, t) for s, t in shapes],
        in_specs=[pl.BlockSpec(memory_space=pl.ANY)] * len(raw),
        out_specs=[vmem] * len(shapes),
        scratch_shapes=[pltpu.VMEM(a.shape, a.dtype) for a in raw[2:]] + [pltpu.SemaphoreType.DMA((5,))],
        compiler_params=pltpu.CompilerParams(vmem_limit_bytes=60 * 2**20),
        name="results",
    )(*raw))
    outs[2], outs[10] = outs[2].reshape(64), outs[10].reshape(64)
    outs[3] = outs[3].transpose(1, 0, 2)
    return tuple(outs)


def solution(mesh):
    row, cols = P("seq", "mp"), P(None, "mp")
    return jax.shard_map(
        on_device,
        mesh=mesh,
        in_specs=(
            P("seq", None), P("seq", None), P("seq"), P("seq"), P("seq", None, "mp"), P(None, None, "mp"),
            cols, cols, cols, cols, row, P("seq"), row, row, row,
        ),
        out_specs=(
            P("seq", None), P("seq", None), P("seq"), P("seq", None, "mp"), P(None, None, "mp"),
            cols, cols, cols, cols, row, P("seq"), row, row, row,
        ),
        check_vma=False,
    )
```

time: 360 us -> 174 us (0.48); the launches traced: 356 us -> 174 us
  Pallas kernels: 244 us -> 173 us
  waiting for transfers between devices: 66.2 us -> 0 us
  local copies, waits for them, and re-layouts: 18.1 us -> 0 us
  between operations: 14.5 us -> 0.66 us
  blocking collectives: 8.39 us -> 0 us
  other arithmetic: 5.42 us -> 0 us
    pallas_call x1, Pallas kernels: 244 us -> 170 us  [block(): pl.pallas_call(kernel, out_shape=(jax.ShapeDtypeStruct((128, 2048), BF16)...]
    unnamed x2 -> x0, waiting for transfers between devices: 66.2 us -> none
    unnamed x56 -> x0, local copies, waits for them, and re-layouts: 13.8 us -> none
    psum x1 -> x0, blocking collectives: 8.39 us -> none  [on_device(): lax.psum(ggain[0:2], 'mp')]
  transfers between devices with their start and end apart: 1 -> 0, of which waited for: 1 -> 0; matrix products, arithmetic and copies ran while one was open for 2% -> 0% of each run, Pallas kernels for 0% -> 0%
where the time goes in v2:
time: 174 us
  Pallas kernels  173 us (99%)
    pallas_call x1, Pallas kernels, block(): pl.pallas_call(kernel, out_shape=(jax.ShapeDtypeStruct((128, 2048), BF16)...  170 us

profile of v2, /device:TPU:1, one launch (start us, length us, event | category | flops | bytes accessed | tf_op | source)
XLA Modules:
  0.0 174.0 jit_solution(1299689024027884485)
XLA Ops:
  0.7 170.3 %block.1 = (bf16[128,2048]{1,0:T(8,128)(2,1)}, bf16[128,2048]{1,0:T(8,128)(2,1)}, bf16[2,64,3200]{2,1,0:T(8,128)(2,1)}, f32[2,80,256]{2,1,0:T(8,128)}, f32[8,128]{1,0:T(8,128)}) custom-call(bf16[3,64,512]{2,1,0:T(8,128)(2,1)} %bitcast.7, bf16[64,512]{1,0:T(8,128)(2,1)} %refs_1_.1, bf16[64,1408]{1,0:T(8,128)(2,1)} %refs_2_.1, bf16[64,1408]{1,0:T(8,128)(2,1)} %refs_3_.1, ...), custom_call_target="tpu_custom_call" | custom-call | tf_op jit(solution)/shard_map/block/pallas_call | solution.py:1291
  170.9 3.1 %results.1 = (bf16[128,2048]{1,0:T(8,128)(2,1)}, bf16[128,2048]{1,0:T(8,128)(2,1)}, f32[1,64]{1,0:T(1,128)}, f32[3,64,512]{2,1,0:T(8,128)}, f32[3,3,512]{2,1,0:T...) custom-call(bf16[128,2048]{1,0:T(8,128)(2,1)} %get-tuple-element.33., ...), custom_call_target="tpu_custom_call" | custom-call | tf_op jit(solution)/shard_map/results/pallas_call | solution.py:1371

commit v3 on v2

v3 whole, which is shorter than its diff:
```python
import functools

import jax
import jax.numpy as jnp
from jax import lax
from jax.experimental import pallas as pl
from jax.experimental.pallas import tpu as pltpu
from jax.sharding import PartitionSpec as P

EPSILON = 1e-05
BF16, F32 = jnp.bfloat16, jnp.float32
MESH = pl.DeviceIdType.MESH
LANES_A, LANES_B = 1664, 1536
CHUNKS = (
    ((0, 128), (0, 128)),
    ((128, 256), (128, 256)),
    ((384, 128), (384, 128)),
    ((512, 384), (512, 384)),
    ((896, 384), (896, 256)),
    ((1280, 384), (1152, 384)),
)
IN, IN_2, OUT, GU, GU_2, DOWN = range(6)
def pieces(a, b, last=False):
    both = [(0, 0, *a, 0, 128), (1, 1, *b, 0, 128)]
    return both + [(0, 0, 1536, 128, 0, 64), (1, 0, 1536, 128, 64, 64)] * last


GATHERS = (
    (0, False, pieces((0, 384), (0, 384))),
    (0, False, pieces((384, 1152), (384, 1152), True)),
    (1, True, pieces((0, 384), (0, 384))),
    (1, False, pieces((384, 128), (384, 128))),
    (1, True, pieces((512, 384), (512, 384))),
    (1, True, pieces((896, 384), (896, 256))),
    (1, True, pieces((1280, 256), (1152, 384), True)),
)
A_IN, A_REST, B_IN, B_OUT, B_GU, B_GU_2, B_DOWN = range(7)
SECOND = (CHUNKS[0], CHUNKS[1], CHUNKS[2], ((512, 768), (512, 640)), CHUNKS[5])
SCATTERS = [pieces(*parts) for parts in CHUNKS[:5] + SECOND[:4]]
SCATTERS = SCATTERS[:5] + [pieces((1280, 256), (1152, 384), True)] + SCATTERS[5:] + [pieces((1280, 256), (1152, 384), True)]
S_IN, S_IN_2, S_OUT, S_GU, S_DOWN = range(6, 11)
WHOLE = {n: CHUNKS[n] for n in (IN, IN_2, OUT, DOWN)} | {GU: ((512, 768), (512, 640))}


def where():
    place = lax.axis_index("seq")
    chip = place // 2
    return chip // 4, lax.rem(chip, 4), lax.rem(place, 2), lax.axis_index("mp")


def device(z, y, c, x):
    return ((z * 4 + y) * 2 + c, x)


def rem4(a):
    return lax.rem(a + 4, 4)


def remote(src, dst, send, recv, to):
    return pltpu.make_async_remote_copy(
        src_ref=src, dst_ref=dst, send_sem=send, recv_sem=recv, device_id=to, device_id_type=MESH
    )


def waiting(ref, sem):
    return remote(ref, ref, sem, sem, device(0, 0, 0, 0))


def nn(a, b):
    return jnp.dot(a, b, preferred_element_type=F32)


def nt(a, b):
    return lax.dot_general(a, b, (((1,), (1,)), ((), ())), preferred_element_type=F32)


def tn(a, b):
    return lax.dot_general(a, b, (((0,), (0,)), ((), ())), preferred_element_type=F32)


def expm1(x):
    series = x / 8.0 + 1.0
    for n in range(7, 1, -1):
        series = series * (x / n) + 1.0
    return jnp.where(jnp.abs(x) < 0.25, x * series, jnp.exp(x) - 1.0)


def fold(count, body, state):
    return lax.fori_loop(0, count, body, state)


def loop(count, body):
    lax.fori_loop(0, count, lambda i, _: (body(i), 0)[1], 0)


def span(start, size):
    return pl.ds(pl.multiple_of(start, size), size)


(
    START, GAIN_Y, GAIN_Z, NORM_1, EDGE, PROJECT, SHORT, ENDS_Y,
    ENDS_Z, SCAN, MIX, MIX_0, MIX_1, MIX_2, N2_0, N2_1,
    FF, ACT, DA, DN2_0, DN2_1, DN2_2, DH_0, DH_1,
    DZ, BACKS_Y, BACKS_Z, ADJOINT, DQ, DN1_0, DN1_X, DN1_1,
    DN1_2, GT_0, GT_1, GT_2, GT_3, GT_4,
) = range(38)
AG, RS, WG, FFN, SMALL, SHORT_1 = range(6)
PLAN = {
    START: ((AG, A_IN, 1),),
    GAIN_Y: ((AG, A_REST, 1),),
    GAIN_Z: ((AG, A_IN, 3), (AG, A_REST, 3), (AG, A_IN, 4), (AG, B_IN, 1), (AG, B_IN, 2), (AG, A_REST, 4),),
    NORM_1: ((AG, B_IN, 3),),
    EDGE: ((AG, B_GU_2, 1), (AG, B_IN, 4), (AG, B_OUT, 1),),
    ENDS_Y: ((AG, B_GU_2, 2), (AG, B_OUT, 3),),
    ENDS_Z: ((AG, B_GU, 1), (AG, B_DOWN, 1), (AG, B_GU, 2), (AG, B_OUT, 4),),
    MIX_1: ((AG, B_GU, 3),),
    MIX_2: ((AG, B_GU_2, 3),),
    N2_0: ((AG, B_DOWN, 2),),
    N2_1: ((AG, B_DOWN, 3), (AG, B_GU, 4), (AG, B_GU_2, 4),),
    ACT: ((WG, DOWN), (RS, DOWN, 0), (AG, B_DOWN, 4),),
    DA: ((RS, DOWN, 1),),
    DN2_1: ((RS, DOWN, 2), (WG, GU), (RS, GU, 0), (RS, GU_2, 0),),
    DH_0: ((RS, GU, 1), (RS, GU_2, 1),),
    BACKS_Y: ((RS, GU, 2), (RS, DOWN, 3), (WG, OUT), (RS, OUT, 0),),
    BACKS_Z: ((RS, OUT, 1), (FFN, 0), (RS, GU_2, 2), (FFN, 1), (SHORT_1,), (WG, IN), (RS, S_DOWN, 0),
        (RS, GU, 3),),
    DQ: ((RS, IN, 0), (RS, OUT, 2), (RS, GU_2, 3), (FFN, 2), (RS, S_GU, 0), (RS, IN, 1),),
    DN1_X: ((WG, IN_2), (RS, IN_2, 0), (RS, IN, 2), (RS, IN_2, 1),),
    DN1_1: ((SMALL, 0),),
    DN1_2: ((RS, IN_2, 2),),
    GT_0: ((RS, IN, 3), (RS, S_IN, 0), (RS, OUT, 3), (RS, S_OUT, 0), (RS, S_DOWN, 1), (SMALL, 1),),
    GT_1: ((FFN, 3), (RS, IN_2, 3), (RS, S_IN_2, 0),),
    GT_2: ((RS, S_IN, 1), (RS, S_GU, 1), (RS, S_OUT, 1), (RS, S_DOWN, 2), (FFN, 4), (SMALL, 2),),
    GT_3: ((RS, S_IN_2, 1),),
    GT_4: ((RS, S_GU, 2), (FFN, 5), (RS, S_IN, 2), (RS, S_OUT, 2), (RS, S_IN_2, 2),),
}


class Rings:
    def __init__(self):
        self.z, self.y, self.c, self.x = where()
        self.chip = self.z * 4 + self.y
        self.sib = device(self.z, self.y, 1 - self.c, self.x)

    def near(self, axis, d):
        if axis == 0:
            return device(rem4(self.z + d), self.y, self.c, self.x)
        if axis == 1:
            return device(self.z, rem4(self.y + d), self.c, self.x)
        return device(self.z, self.y, self.c, rem4(self.x + d))

    def along(self, d):
        return (lax.rem(self.chip + d + 16, 16) * 2 + self.c, self.x)


class Gather:
    def __init__(self, r, ref, lanes, rows, phase, axis, split, send, recv):
        self.r, self.ref, self.lanes, self.rows = r, ref, lanes, rows
        self.phase, self.axis, self.split = phase, axis, split
        self.send, self.recv, self.sent = send, recv, []

    def copy(self, d, part, to, i):
        r, axis = self.r, self.axis
        z, y = (rem4(r.z + d), r.y) if axis == 0 else (r.z, rem4(r.y + d))
        if self.phase == 0:
            o, n = self.rows
            rows = (pl.ds(o, n), pl.ds(o, n // 2), pl.ds(o + n // 2, n // 2))[part]
            ref = self.ref.at[z, y, rows, self.lanes]
        else:
            many, rows = (pl.ds(0, 4), pl.ds(0, 2), pl.ds(2, 2))[part], pl.ds(*self.rows)
            ref = self.ref.at[z, many, rows, self.lanes] if axis == 0 else self.ref.at[many, y, rows, self.lanes]
        return remote(ref, ref, self.send, self.recv.at[i], r.near(axis, to))

    def start(self, *a):
        copy = self.copy(*a)
        copy.start()
        self.sent.append(copy)

    def step(self, i):
        if i == 1 and not self.split:
            self.start(0, 0, 1, 0)
            self.start(0, 0, -1, 1)
        elif i == 1:
            self.start(0, 1, 1, 0)
            self.start(0, 2, -1, 1)
        elif i == 2 and not self.split:
            pass
        elif i == 2:
            self.start(0, 2, 1, 2)
            self.start(0, 1, -1, 2)
        elif i == 3:
            self.copy(-1, 1 if self.split else 0, 1, 0).wait_recv()
            self.start(-1, 1, 1, 2)
            self.copy(1, 2 if self.split else 0, -1, 1).wait_recv()
            self.start(1, 2, -1, 2)
        else:
            waiting(self.units(2 if self.split else 1), self.recv.at[2]).wait_recv()

    def units(self, count):
        rows = pl.ds(*self.rows)
        if self.phase == 0:
            return self.ref.at[0, pl.ds(0, count), rows, self.lanes]
        return self.ref.at[pl.ds(0, count), :, rows, self.lanes]

    def drain(self):
        if self.sent:
            waiting(self.units(3), self.send).wait_send()
        self.sent = []


class Trade:
    def __init__(self, r, axis, src, land, send, recv):
        self.r, self.axis, self.src, self.land, self.send, self.recv = r, axis, src, land, send, recv
        self.me, self.sent = (r.z, r.y, r.x)[axis], []

    def copy(self, d):
        return remote(
            self.src(rem4(self.me + d)), self.land.at[self.me], self.send, self.recv,
            self.r.near(self.axis, d),
        )

    def begin(self):
        for d in (2, 1, 3):
            copy = self.copy(d)
            copy.start()
            self.sent.append(copy)

    def end(self):
        waiting(self.land.at[0:3], self.recv).wait_recv()

    def drain(self):
        if self.sent:
            waiting(self.land.at[0:3], self.send).wait_send()


class Scatter:
    def __init__(self, r, ref, lanes, rows, at, phase, axis, buf, send, recv):
        self.r, self.ref, self.lanes, self.rows, self.at = r, ref, lanes, rows, at
        self.phase, self.axis, self.buf, self.send, self.recv, self.sent = phase, axis, buf, send, recv, []

    def unit(self, d, part):
        r, axis = self.r, self.axis
        z, y = (rem4(r.z + d), r.y) if axis == 0 else (r.z, rem4(r.y + d))
        if self.phase == 1:
            o, n = self.rows
            return self.ref.at[z, y, pl.ds(o + n // 2 * part, n // 2), self.lanes]
        many, rows = pl.ds(2 * part, 2), pl.ds(*self.rows)
        return self.ref.at[z, many, rows, self.lanes] if axis == 0 else self.ref.at[many, y, rows, self.lanes]

    def landing(self, i):
        o, n = self.rows
        if self.phase == 0:
            return self.buf.at[i, :, pl.ds(o, n), self.at]
        return self.buf.at[i, pl.ds(o // 2, n // 2), self.at]

    def copy(self, d, part, to, i):
        return remote(
            self.unit(d, part), self.landing(i), self.send, self.recv.at[min(i, 2)],
            self.r.near(self.axis, to),
        )

    def start(self, *a):
        copy = self.copy(*a)
        copy.start()
        self.sent.append(copy)

    def arrived(self, i):
        self.copy(0, 0, 1, i).wait_recv()

    def add(self, d, part, many):
        unit = self.unit(d, part)
        lands, many = [self.landing(i) for i in many], self.rows[1] // 32
        if self.phase == 0:
            def body(i):
                k, rows = i // many, span(lax.rem(i, many) * 32, 32)
                total = unit[k, rows, :].astype(F32)
                for l in lands:
                    total = total + l[k, rows, :].astype(F32)
                unit[k, rows, :] = total.astype(BF16)
            loop(2 * many, body)
        else:
            def body(i):
                rows = span(i * 32, 32)
                total = unit[rows, :].astype(F32)
                for l in lands:
                    total = total + l[rows, :].astype(F32)
                unit[rows, :] = total.astype(BF16)
            loop(many // 2, body)

    def far(self):
        self.start(2, 0, 1, 0)
        self.start(2, 1, -1, 1)

    def early(self):
        self.start(1, 1, 1, 3)
        self.start(-1, 0, -1, 4)

    def forward(self):
        self.arrived(0)
        self.add(1, 0, (0,))
        self.start(1, 0, 1, 2)
        self.arrived(1)
        self.add(-1, 1, (1,))
        self.start(-1, 1, -1, 5)

    def units(self, count):
        o, n = self.rows
        if self.phase == 0:
            return self.buf.at[pl.ds(0, 2 * count), :, pl.ds(o, n), self.at]
        return self.buf.at[pl.ds(0, 2 * count), pl.ds(o // 2, n // 2), self.at]

    def finish(self):
        waiting(self.units(2), self.recv.at[2]).wait_recv()
        self.add(0, 0, (2, 4))
        self.add(0, 1, (3, 5))

    def drain(self):
        if self.sent:
            waiting(self.units(3), self.send).wait_send()
        self.sent = []


class CrossSum:
    def __init__(self, r, part, got, mid, one, two, send, recv):
        self.r, self.part, self.got, self.mid, self.one, self.two = r, part, got, mid, one, two
        self.send, self.recv, self.sent = send, recv, []

    def start(self, copy):
        copy.start()
        self.sent.append(copy)

    def rows(self, c, x):
        return span((c * 4 + x) * 32, 32)

    def pair(self, d):
        x = rem4(self.r.x + d)
        return remote(
            self.part.at[self.rows(1 - self.r.c, x)], self.got.at[x],
            self.send, self.recv.at[(4, 1, 0, 1)[d]], self.r.sib,
        )

    def begin(self):
        for d in (2, 1, 3, 0):
            self.start(self.pair(d))

    def pairsum(self, d):
        x = rem4(self.r.x + d)
        rows = self.rows(self.r.c, x)
        self.mid[x] = (self.part[rows].astype(F32) + self.got[x].astype(F32)).astype(BF16)

    def far(self, side):
        x = rem4(self.r.x + 2)
        return remote(
            self.mid.at[x, pl.ds(16 * side, 16)], self.one.at[side],
            self.send, self.recv.at[2 + side], self.r.near(2, 1 - 2 * side),
        )

    def late(self, side, summed):
        d = 1 - 2 * side
        x = rem4(self.r.x + d)
        half = side if summed else 1 - side
        return remote(
            self.mid.at[x, pl.ds(16 * half, 16)], self.two.at[side, pl.ds(16 * half, 16)],
            self.send, self.recv.at[4], self.r.near(2, d),
        )

    def middle(self):
        self.near_half()
        self.far_half()

    def near_half(self):
        self.pair(2).wait_recv()
        self.pairsum(2)
        self.start(self.far(0))
        self.start(self.far(1))
        waiting(self.part.at[0:64], self.recv.at[1]).wait_recv()
        self.pairsum(1)
        self.start(self.late(0, 0))
        self.pairsum(3)
        self.start(self.late(1, 0))

    def far_half(self):
        for side in range(2):
            self.far(side).wait_recv()
            x = rem4(self.r.x + 1 - 2 * side)
            rows = pl.ds(16 * side, 16)
            self.mid[x, rows] = (self.mid[x, rows].astype(F32) + self.one[side].astype(F32)).astype(BF16)
            self.start(self.late(side, 1))

    def end(self):
        waiting(self.part.at[0:96], self.recv.at[4]).wait_recv()

    def result(self, rows):
        base = (self.r.c * 4 + self.r.x) * 32
        own = self.part[pl.ds(pl.multiple_of(base + rows.start, rows.size), rows.size)].astype(F32)
        own = own + self.got[self.r.x, rows].astype(F32)
        return own + self.two[0, rows].astype(F32) + self.two[1, rows].astype(F32)

    def drain(self):
        if self.sent:
            waiting(self.part.at[0:224], self.send).wait_send()
        self.sent = []


class CrossGather:
    def __init__(self, r, ref, both, send, recv):
        self.r, self.ref, self.both, self.send, self.recv, self.sent = r, ref, both, send, recv, []

    def start(self, copy):
        copy.start()
        self.sent.append(copy)

    def rows(self, d, part):
        base = rem4(self.r.x + d) * 32
        if self.both:
            base = base + self.r.c * 128
        if part is None:
            return self.ref.at[pl.ds(pl.multiple_of(base, 32), 32)]
        return self.ref.at[pl.ds(pl.multiple_of(base + 16 * part, 16), 16)]

    def ring(self, d, part, to, i):
        ref = self.rows(d, part)
        return remote(ref, ref, self.send, self.recv.at[i], self.r.near(2, to))

    def pair(self, d):
        ref = self.rows(d, None)
        return remote(ref, ref, self.send, self.recv.at[4], self.r.sib)

    def begin(self):
        self.start(self.ring(0, 0, 1, 0))
        self.start(self.ring(0, 1, -1, 1))
        self.start(self.ring(0, 1, 1, 2))
        self.start(self.ring(0, 0, -1, 2))
        if self.both:
            self.start(self.pair(0))

    def middle(self):
        self.ring(-1, 0, 1, 0).wait_recv()
        self.start(self.ring(-1, 0, 1, 3))
        self.ring(1, 1, -1, 1).wait_recv()
        self.start(self.ring(1, 1, -1, 3))
        waiting(self.ref.at[0:32], self.recv.at[2]).wait_recv()
        if self.both:
            self.start(self.pair(-1))
            self.start(self.pair(1))

    def end(self):
        waiting(self.ref.at[0:32], self.recv.at[3]).wait_recv()
        if self.both:
            self.start(self.pair(2))
            waiting(self.ref.at[0:128], self.recv.at[4]).wait_recv()

    def drain(self):
        waiting(self.ref.at[0:224 if self.both else 96], self.send).wait_send()


class Refs:
    pass


class Inputs:
    in_w = out_w = gate_w = up_w = down_w = gain_1 = gain_2 = resets = tok = cot = conv_w = 0
    decay = angle = res_re = res_im = 0


class Outputs:
    block_out = grad_tok = grad_w = grad_small = grad_gain = 0


class Scratch:
    other = ((64, LANES_A + LANES_B), BF16)
    tab = ((8, 16, 256), F32)
    ga = ((4, 4, 128, LANES_A), BF16)
    gb = ((4, 4, 128, LANES_B), BF16)
    s0a = ((6, 2, 128, LANES_A), BF16)
    s0b = ((6, 2, 128, LANES_B), BF16)
    s1a = ((6, 64, LANES_A), BF16)
    s1b = ((6, 64, LANES_B), BF16)
    da = ((4, 4, 128, 384), BF16)
    ia = ((4, 4, 128, 128), BF16)
    ib = ((4, 4, 128, 128), BF16)
    db = ((4, 4, 128, 384), BF16)
    sib_a = ((64, LANES_A), BF16)
    sib_b = ((64, LANES_B), BF16)
    gains_y = ((4, 16, 128), F32)
    gains_all = ((4, 4, 16, 128), F32)
    gains = ((8, 2048), F32)
    gain_in = ((8, 128), F32)
    taps = ((8, 768), F32)
    keep = ((256, 256), F32)
    gy = ((256, 2048), BF16)
    n1 = ((272, 2048), BF16)
    n2 = ((256, 2048), BF16)
    dh = ((256, 2048), BF16)
    part = ((256, 2048), BF16)
    mid = ((4, 32, 2048), BF16)
    part_f = ((256, 2048), BF16)
    mid_f = ((4, 32, 2048), BF16)
    got = ((4, 4, 32, 2048), BF16)
    one = ((4, 2, 16, 2048), BF16)
    two = ((4, 2, 32, 2048), BF16)
    bo = ((128, 2048), BF16)
    gt = ((128, 2048), BF16)
    h = ((32, 2048), F32)
    dhf = ((32, 2048), F32)
    p = ((272, 768), F32)
    q0 = ((256, 256), F32)
    q1 = ((256, 256), F32)
    q2 = ((256, 256), F32)
    u = ((256, 256), F32)
    v = ((256, 256), F32)
    z = ((256, 256), BF16)
    st_re = ((257, 16, 256), F32)
    st_im = ((257, 16, 256), F32)
    ends_y = ((4, 32, 256), F32)
    ends_z = ((4, 32, 256), F32)
    backs_y = ((4, 32, 256), F32)
    backs_z = ((4, 32, 256), F32)
    gu = ((256, 1408), F32)
    act = ((256, 768), BF16)
    dgu = ((256, 1408), BF16)
    dv = ((256, 256), F32)
    dq = ((264, 768), F32)
    dp = ((256, 768), BF16)
    small_y = ((4, 80, 256), BF16)
    small_z = ((4, 80, 256), BF16)
    small_sum = ((80, 256), F32)
    small_sib = ((80, 256), F32)
    ggain = ((8, 2048), F32)
    gg_z = ((4, 8, 512), F32)
    gg_1 = ((8, 512), F32)
    gg_y = ((4, 8, 128), F32)
    gg_2 = ((8, 128), F32)
    gg_s = ((8, 128), F32)
    gg_x = ((4, 8, 128), F32)
    gg_out = ((8, 128), F32)


def fields(group):
    return [(name, value) for name, value in vars(group).items() if name[0] != "_"]


class Sems:
    w = (7, 4), (7, 4, 3)
    w_sib = (2,), (2,)
    gain_sib = keep_s = gy_s = n1_s = edge = dq_s = dq_1 = small_x = gg_s = (), ()
    trade = (11,), (11,)
    sum = (4,), (4, 5)
    cg = (4,), (4, 5)
    rs = (11, 4), (11, 4, 3)
    rs_sib = (5,), (5,)


def kernel(*refs):
    names = [name for group in (Inputs, Outputs, Scratch) for name, _ in fields(group)]
    k, S, R = Refs(), Refs(), Refs()
    for name, ref in zip(names, refs):
        setattr(k, name, ref)
    rest = refs[len(names):]
    for i, (name, _) in enumerate(fields(Sems)):
        setattr(S, name, rest[2 * i])
        setattr(R, name, rest[2 * i + 1])
    local = rest[-1]
    r = Rings()
    g = (k.ga, k.gb)
    z, y, c, x = r.z, r.y, r.c, r.x

    barrier = pltpu.get_barrier_semaphore()
    peers = [r.sib] + [r.near(a, d) for a in range(3) for d in (1, 2, 3)] + [r.along(1), r.along(-1)]
    for peer in peers:
        pl.semaphore_signal(barrier, inc=1, device_id=peer, device_id_type=MESH)

    def lanes(n, h):
        o, w = CHUNKS[n][h]
        return pl.ds(o, w)

    def columns(n, start, stop):
        (oa, wa), (ob, _) = WHOLE[n]
        parts = []
        if start < wa:
            parts.append(g[0][:, :, :, oa + start:oa + min(stop, wa)])
        if stop > wa:
            parts.append(g[1][:, :, :, ob + max(start - wa, 0):ob + stop - wa])
        return jnp.concatenate([p.reshape(2048, p.shape[-1]) for p in parts], 1)

    def weight(n, h, i):
        o, w = WHOLE[n][h]
        return g[h][i, :, :, o:o + w].reshape(512, w)

    trades = []

    def trade(axis, src, land):
        i = len(trades)
        trades.append(Trade(r, axis, src if callable(src) else lambda _: src, land, S.trade.at[i], R.trade.at[i]))
        return trades[-1]

    my64 = span(c * 64, 64)
    my128 = span(c * 128, 128)
    gather = []
    for n, (phase, split, parts) in enumerate(GATHERS):
        gather.append([
            Gather(r, g[b], pl.ds(o, w), rows, phase, 1 - way if phase == 0 else way, split and rows[1] == 128,
                   S.w.at[n, i], R.w.at[n, i])
            for i, (way, b, o, w, *rows) in enumerate(parts)
        ])

    def put(cc, n, sink):
        wa = WHOLE[n][0][1]

        def store(start, value):
            stop = start + value.shape[1]
            if start < wa:
                sink(0, WHOLE[n][0][0] + start, value[:, :min(stop, wa) - start])
            if stop > wa:
                sink(1, WHOLE[n][1][0] + max(start - wa, 0), value[:, max(wa - start, 0):])

        def main(ref):
            return ref[:, pl.ds(pl.multiple_of(cc * 640, 128), 640)]

        def tail(ref):
            a = ref[:, 1280:1408].astype(F32)
            return jnp.where(cc == 0, a[:, 0:64], a[:, 64:128])

        channels = pl.ds(pl.multiple_of(cc * 256, 256), 256)
        if n == IN:
            store(0, k.in_w[0, :, channels])
        elif n == IN_2:
            store(0, k.in_w[1, :, channels])
            store(256, k.in_w[2, :, channels])
        elif n == OUT:
            store(0, k.out_w[:, channels])
        elif n == GU:
            store(0, main(k.gate_w))
            store(640, main(k.up_w))
            store(1280, jnp.concatenate([tail(k.gate_w), tail(k.up_w)], 1).astype(BF16))
        else:
            store(0, main(k.down_w))
            store(640, jnp.concatenate([tail(k.down_w), jnp.zeros((64, 64), F32)], 1).astype(BF16))

    def to_other(h, at, value):
        at = at + (LANES_A if h else 0)
        k.other[:, at:at + value.shape[1]] = value

    def to_own(h, at, value):
        g[h][z, y, my64, at:at + value.shape[1]] = value

    def weight_sib(n, h):
        o, w = ((0, 384), (384, (1280, 1152)[h]))[n]
        return remote(
            k.other.at[:, pl.ds(o + (LANES_A if h else 0), w)], g[h].at[z, y, my64, pl.ds(o, w)],
            S.w_sib.at[n], R.w_sib.at[n], r.sib,
        )

    eight = span(c * 8, 8)
    side = lax.broadcasted_iota(jnp.int32, (1, 128), 1) // 64 == c
    for i, ref in enumerate((k.gain_1, k.gain_2)):
        a = ref[...].astype(F32)
        k.gain_in[i:i + 1, :] = jnp.where(side, jnp.concatenate([a, a], 1), 0.0)
    k.gain_in[2:8, :] = jnp.zeros((6, 128), F32)
    k.gains_y[y, eight] = k.gain_in[...]
    for n in (IN, IN_2):
        put(1 - c, n, to_other)
        put(c, n, to_own)
    keep = 1.0 - k.resets[...].astype(F32)
    keep = jnp.broadcast_to(keep, (128, 128)).T
    k.keep[my128] = jnp.concatenate([keep, keep], 1)
    pl.semaphore_wait(barrier, len(peers))

    gain_sib = remote(k.gain_in, k.gains_y.at[y, eight], S.gain_sib, R.gain_sib, r.sib)
    keep_sib = remote(k.keep.at[my128], k.keep.at[my128], S.keep_s, R.keep_s, r.sib)
    gy_sib = remote(k.cot, k.gy.at[my128], S.gy_s, R.gy_s, r.sib)
    def share(n):
        for h in range(2):
            weight_sib(n, h).start()

    share(A_IN)
    gain_sib.start()

    def ag(n, i):
        if i == 1 and n in (A_IN, A_REST):
            waiting(k.other.at[:, 0:(768, 2432)[n]], R.w_sib.at[n]).wait_recv()
        for piece in gather[n]:
            piece.step(i)

    tasks = {}

    def at(point):
        for name, *rest in PLAN.get(point, ()):
            tasks[name](*rest)

    tasks[AG] = ag
    at(START)
    gain_y = trade(1, k.gains_y.at[y], k.gains_y)
    gain_z = trade(0, k.gains_y, k.gains_all)
    gain_sib.wait_recv()
    gain_y.begin()

    for n in (OUT, GU, DOWN):
        put(1 - c, n, to_other)
        put(c, n, to_own)
    share(A_REST)
    keep_sib.start()
    at(GAIN_Y)
    gain_y.end()
    gain_z.begin()
    k.gains_all[z] = k.gains_y[...]
    at(GAIN_Z)
    k.gy[my128] = k.cot[...]

    channels = pl.ds(pl.multiple_of(c * 256, 256), 256)
    decay, angle = k.decay[:, channels], k.angle[:, channels]
    size = jnp.exp(-decay)
    gin = jnp.sqrt(-expm1(-2.0 * decay))
    power = (size * jnp.cos(angle), size * jnp.sin(angle))
    k.tab[0], k.tab[1] = power
    k.tab[2] = gin * k.res_re[:, channels]
    k.tab[3] = gin * k.res_im[:, channels]
    for _ in range(8):
        power = (power[0] * power[0] - power[1] * power[1], 2.0 * power[0] * power[1])
    k.tab[4], k.tab[5] = power
    k.tab[6] = gin
    k.tab[7] = size * size / gin
    for i in range(3):
        for b in range(3):
            k.taps[i:i + 1, b * 256:b * 256 + 256] = k.conv_w[i, b:b + 1, channels]

    gain_z.end()
    for i in range(16):
        k.gains[:, i * 128:(i + 1) * 128] = k.gains_all[i // 4, i % 4, 0:8] + k.gains_all[i // 4, i % 4, 8:16]

    def norm_one(i):
        rows = span(i * 16, 16)
        a = k.tok[rows, :].astype(F32)
        s = lax.rsqrt(jnp.mean(a * a, axis=-1, keepdims=True) + EPSILON)
        k.n1[pl.ds(pl.multiple_of(16 + c * 128 + i * 16, 16), 16), :] = (a * s * k.gains[0:1, :]).astype(BF16)
    loop(8, norm_one)

    def n1_rows(c):
        return k.n1.at[pl.ds(pl.multiple_of(16 + c * 128, 16), 128)]

    n1_sib = remote(n1_rows(c), n1_rows(c), S.n1_s, R.n1_s, r.sib)
    n1_sib.start()
    at(NORM_1)
    k_other = span((1 - c) * 128, 128)
    remote(n1_rows(1 - c), n1_rows(1 - c), S.n1_s, R.n1_s, r.sib).wait_recv()
    edge = remote(k.n1.at[256:272], k.n1.at[0:16], S.edge, R.edge, r.along(1))
    edge.start()
    gy_sib.start()
    at(EDGE)

    edge.wait_recv()
    at(PROJECT)

    def project(_):
        for o in range(0, 512, 256):
            k.p[:, 256 + o:512 + o] = nn(k.n1[...], columns(IN_2, o, o + 256))
        k.p[:, 0:256] = nn(k.n1[...], columns(IN, 0, 256))
    loop(1, project)

    def round_p(i):
        rows = span(i * 16, 16)
        k.p[rows, :] = k.p[rows, :].astype(BF16).astype(F32)
    loop(17, round_p)
    remote(k.keep.at[k_other], k.keep.at[k_other], S.keep_s, R.keep_s, r.sib).wait_recv()
    at(SHORT)

    def masks(i):
        rows = span(i * 16, 16)
        near = k.keep[rows, :]
        before = k.keep[span(jnp.maximum(i * 16 - 8, 0), 8), :]
        first = jnp.where(i == 0, 1.0, before[7:8, :])
        shifted = jnp.concatenate([first, near[0:15, :]], 0)
        return near, near * shifted

    def short(i):
        near, far = masks(i)
        ext = k.p[pl.ds(pl.multiple_of(i * 16 + 8, 8), 24), :]
        q = []
        for b in range(3):
            l = slice(b * 256, b * 256 + 256)
            e = ext[:, l]
            q.append(
                k.taps[0:1, l] * e[8:24] + near * k.taps[1:2, l] * e[7:23] + far * k.taps[2:3, l] * e[6:22]
            )
        rows = span(i * 16, 16)
        k.q0[rows, :] = q[0]
        k.q1[rows, :] = q[1]
        k.q2[rows, :] = q[2]
        k.u[rows, :] = q[1] * q[2]
    loop(16, short)

    zero = jnp.zeros((16, 256), F32)
    lr, li, cr, ci, pr, pi = (k.tab[i] for i in range(6))

    def advance(re, im, u, keep):
        kr, ki = keep * re, keep * im
        return lr * kr - li * ki + u, lr * ki + li * kr

    def end_state(i, state):
        rows = span(i * 8, 8)
        u, keep = k.u[rows, :], k.keep[rows, :]
        for j in range(8):
            state = advance(*state, u[j:j + 1, :], keep[j:j + 1, :])
        return state

    def times(a, b, g, h):
        return a * g - b * h, a * h + b * g

    def chain(own, ref_y, ref_z, sign, between):
        order = range(4) if sign > 0 else range(3, -1, -1)
        qr, qi = pr, sign * pi

        def put(ref, at, state):
            ref[at, 0:16] = state[0]
            ref[at, 16:32] = state[1]

        def horner(ref, wr, wi, state, here, every):
            for i in order:
                nr, ni = times(wr, wi, *state)
                nr, ni = nr + ref[i, 0:16], ni + ref[i, 16:32]
                use = (i < here) if sign > 0 else (i > here)
                state = (nr, ni) if every else (jnp.where(use, nr, state[0]), jnp.where(use, ni, state[1]))
            return state

        put(ref_y, y, own)
        t = trade(1, ref_y.at[y], ref_y)
        t.begin()
        at(between[0])
        t.end()
        put(ref_z, z, horner(ref_y, qr, qi, (zero, zero), y, True))
        t = trade(0, ref_z.at[z], ref_z)
        t.begin()
        at(between[1])
        t.end()
        w = times(*times(qr, qi, qr, qi), *times(qr, qi, qr, qi))
        return horner(ref_y, qr, qi, horner(ref_z, *w, (zero, zero), z, False), y, False)

    end = fold(32, end_state, (zero, zero))
    enter = chain(end, k.ends_y, k.ends_z, 1, (ENDS_Y, ENDS_Z))
    k.st_re[0] = enter[0]
    k.st_im[0] = enter[1]
    at(SCAN)

    def scan(i, state):
        rows = span(i * 8, 8)
        u, keep = k.u[rows, :], k.keep[rows, :]
        for j in range(8):
            state = advance(*state, u[j:j + 1, :], keep[j:j + 1, :])
            k.st_re[i * 8 + j + 1] = state[0]
            k.st_im[i * 8 + j + 1] = state[1]
            k.v[pl.ds(i * 8 + j, 1), :] = jnp.sum(cr * state[0] - ci * state[1], axis=0, keepdims=True)
        return state
    fold(32, scan, enter)

    def gated(i):
        rows = span(i * 32, 32)
        k.z[rows, :] = (k.q0[rows, :] * k.v[rows, :]).astype(BF16)
    loop(8, gated)

    at(MIX)
    def out_weight(i):
        return jnp.concatenate([weight(OUT, 0, i), weight(OUT, 1, i)], 1)

    def mix(i):
        k.part[:, span(i * 512, 512)] = nt(k.z[...], out_weight(i)).astype(BF16)
    loop(4, mix)

    def cross(i):
        part, mid = (k.part_f, k.mid_f) if i == 1 else (k.part, k.mid)
        return CrossSum(r, part, k.got.at[i], mid, k.one.at[i], k.two.at[i], S.sum.at[i], R.sum.at[i])

    s_mix = cross(0)
    s_mix.begin()
    at(MIX_0)
    s_mix.near_half()
    at(MIX_1)
    s_mix.far_half()
    at(MIX_2)
    s_mix.end()

    own = (c * 4 + x) * 32

    def norm_two(i):
        rows = pl.ds(pl.multiple_of(i * 16, 16), 16)
        a = k.tok[pl.ds(pl.multiple_of(x * 32 + i * 16, 16), 16), :].astype(F32) + s_mix.result(rows)
        k.h[rows, :] = a
        s = lax.rsqrt(jnp.mean(a * a, axis=-1, keepdims=True) + EPSILON)
        k.n2[pl.ds(pl.multiple_of(own + i * 16, 16), 16), :] = (a * s * k.gains[1:2, :]).astype(BF16)
    loop(2, norm_two)
    g_n2 = CrossGather(r, k.n2, True, S.cg.at[0], R.cg.at[0])
    g_n2.begin()
    at(N2_0)
    g_n2.middle()
    at(N2_1)
    g_n2.end()
    s_mix.drain()
    at(FF)

    def gate_up(_):
        for o in range(0, 1408, 256):
            e = min(o + 256, 1408)
            k.gu[:, o:e] = nn(k.n2[...], columns(GU, o, e))
    loop(1, gate_up)
    def halves(t):
        last = t[:, 1280:1408]
        turned = jnp.concatenate([last[:, 64:128], last[:, 0:64]], 1)
        return jnp.concatenate([t[:, 0:640], last], 1), jnp.concatenate([t[:, 640:1280], turned], 1)

    used = lax.broadcasted_iota(jnp.int32, (1, 768), 1) < 704

    def activate(i):
        rows = span(i * 16, 16)
        gate, up = halves(k.gu[rows, :])
        k.act[rows, :] = jnp.where(used, gate * jax.nn.sigmoid(gate) * up, 0.0).astype(BF16)
    loop(16, activate)

    def down_weight(i):
        return jnp.concatenate([weight(DOWN, 0, i), weight(DOWN, 1, i)], 1)

    s_ffn = cross(1)
    g_bo = CrossGather(r, k.bo, False, S.cg.at[1], R.cg.at[1])
    out_bo = pltpu.make_async_copy(k.bo, k.block_out, local.at[0])

    def ffn_step(i):
        if i == 0:
            def ffn(i):
                k.part_f[:, span(i * 512, 512)] = nt(k.act[...], down_weight(i)).astype(BF16)
            loop(4, ffn)
            s_ffn.begin()
        elif i == 1:
            s_ffn.near_half()
        elif i == 2:
            s_ffn.far_half()
        elif i == 3:
            s_ffn.end()

            def top(i):
                rows = pl.ds(pl.multiple_of(i * 16, 16), 16)
                here = pl.ds(pl.multiple_of(x * 32 + i * 16, 16), 16)
                k.bo[here, :] = (k.h[rows, :] + s_ffn.result(rows)).astype(BF16)
            loop(2, top)
            s_ffn.drain()
            g_bo.begin()
        elif i == 4:
            g_bo.middle()
        else:
            g_bo.end()
            out_bo.start()

    tasks[FFN] = ffn_step

    apart = {DOWN: (k.da, k.db), IN: (k.ia, k.ib)}
    scatter = []
    for n, parts in enumerate(SCATTERS):
        phase = 0 if n < S_IN else 1
        m = {S_IN: IN, S_DOWN: DOWN}.get(n, n if phase == 0 else None)
        scatter.append([])
        for i, (way, b, o, w, *rows) in enumerate(parts):
            ref, here = g[b], pl.ds(o, w)
            if m in apart:
                ref, here = apart[m][b], pl.ds(o - CHUNKS[m][b][0], w)
            buf = ((k.s0a, k.s0b), (k.s1a, k.s1b))[phase][b]
            axis = 1 - way if phase == 0 else way
            scatter[n].append(
                Scatter(r, ref, here, rows, pl.ds(o, w), phase, axis, buf, S.rs.at[n, i], R.rs.at[n, i])
            )

    def finished(n, h):
        o, w = SECOND[n - S_IN][h]
        m = {S_IN: IN, S_DOWN: DOWN}.get(n)
        return (apart[m][h], pl.ds(0, w), pl.ds(o, w)) if m in apart else (g[h], pl.ds(o, w), pl.ds(o, w))

    sib_bufs = (k.sib_a, k.sib_b)

    def rs_sib(n, h):
        ref, here, at = finished(n, h)
        return remote(
            ref.at[z, y, span((1 - c) * 64, 64), here], sib_bufs[h].at[:, at],
            S.rs_sib.at[n - S_IN], R.rs_sib.at[n - S_IN], r.sib,
        )

    def rs(n, i):
        for s in scatter[n]:
            if n < S_IN:
                (s.far, s.early, s.forward, s.finish)[i]()
            elif i == 0:
                s.far()
                s.early()
            elif i == 1:
                s.forward()
            else:
                s.finish()
        if n >= S_IN and i == 2:
            for h in range(2):
                rs_sib(n, h).start()

    tasks[RS] = rs

    def wg(n):
        a, b, first = {
            IN: (k.n1, k.dp.at[:, 0:256], 16), IN_2: (k.n1, k.dp.at[:, 256:768], 16), OUT: (k.dh, k.z, 0),
            GU: (k.n2, k.dgu, 0), DOWN: (k.gy, k.act, 0),
        }[n]
        for m in {GU: (B_GU, B_GU_2), OUT: (B_OUT,), IN_2: (B_IN,)}.get(n, ()) + ((A_IN, A_REST) if n == GU else ()):
            for piece in gather[m]:
                piece.drain()
        (oa, wa), (ob, wb) = [(0, CHUNKS[n][h][1]) for h in range(2)] if n in apart else WHOLE[n]
        into = apart.get(n, g)

        def weight_grad(i):
            t = tn(a[pl.ds(first, 256), pl.ds(pl.multiple_of(i * 512, 512), 512)], b[...]).astype(BF16)
            into[0][i, :, :, oa:oa + wa] = t[:, 0:wa].reshape(4, 128, wa)
            into[1][i, :, :, ob:ob + wb] = t[:, wa:wa + wb].reshape(4, 128, wb)
        weight_grad.width = wa + wb
        loop(4, weight_grad)

    tasks[WG] = wg

    remote(k.gy.at[k_other], k.gy.at[k_other], S.gy_s, R.gy_s, r.sib).wait_recv()
    at(ACT)

    def d_act(_):
        for o in range(0, 768, 256):
            k.dq[0:256, o:o + 256] = nn(k.gy[...], columns(DOWN, o, o + 256))
    loop(1, d_act)
    at(DA)

    def d_gates(i):
        rows = span(i * 16, 16)
        gate, up = halves(k.gu[rows, :])
        da = k.dq[rows, :]
        sg = jax.nn.sigmoid(gate)
        dgate = da * up * sg * (1.0 + gate * (1.0 - sg))
        dup = da * (gate * sg)
        last = jnp.concatenate([dgate[:, 640:704], dup[:, 640:704]], 1)
        k.dgu[rows, :] = jnp.concatenate([dgate[:, 0:640], dup[:, 0:640], last], 1).astype(BF16)
    loop(16, d_gates)

    def d_n2(i):
        w = jnp.concatenate([weight(GU, 0, i), weight(GU, 1, i)], 1)
        k.part[:, span(i * 512, 512)] = nt(k.dgu[...], w).astype(BF16)
    loop(4, d_n2)
    s_dn2 = cross(2)
    s_dn2.begin()
    at(DN2_0)
    s_dn2.near_half()
    at(DN2_1)
    s_dn2.far_half()
    at(DN2_2)
    s_dn2.end()

    def d_norm_two(i):
        rows = pl.ds(pl.multiple_of(i * 16, 16), 16)
        a = k.h[rows, :]
        s = lax.rsqrt(jnp.mean(a * a, axis=-1, keepdims=True) + EPSILON)
        hat = a * s
        dn = s_dn2.result(rows)
        dng = dn * k.gains[1:2, :]
        gy = k.gy[pl.ds(pl.multiple_of(own + i * 16, 16), 16), :].astype(F32)
        dh = gy + s * (dng - hat * jnp.mean(dng * hat, axis=-1, keepdims=True))
        k.dhf[rows, :] = dh
        k.dh[pl.ds(pl.multiple_of(own + i * 16, 16), 16), :] = dh.astype(BF16)
        t = jnp.sum(dn * hat, axis=0, keepdims=True)

        @pl.when(i == 0)
        def _():
            k.ggain[...] = jnp.zeros((8, 2048), F32)
            k.ggain[1:2, :] = t

        @pl.when(i > 0)
        def _():
            k.ggain[1:2, :] += t
    loop(2, d_norm_two)
    s_dn2.drain()
    g_dh = CrossGather(r, k.dh, True, S.cg.at[2], R.cg.at[2])
    g_dh.begin()
    at(DH_0)
    g_dh.middle()
    at(DH_1)
    g_dh.end()
    at(DZ)

    def d_z(_):
        k.dv[...] = nn(k.dh[...], columns(OUT, 0, 256))
    loop(1, d_z)

    def d_gated(i):
        rows = span(i * 32, 32)
        dz = k.dv[rows, :]
        k.dq[rows, 0:256] = dz * k.v[rows, :]
        k.dv[rows, :] = dz * k.q0[rows, :]
    loop(8, d_gated)

    first = slice(0, 256)
    others = slice(256, 768)

    def dq_edge(at, send, recv):
        return remote(k.dq.at[0:8, at], k.dq.at[256:264, at], send, recv, r.along(-1))

    dq_first = dq_edge(first, S.dq_1, R.dq_1)
    dq_first.start()

    last = jnp.where(r.chip < 15, 1.0, 0.0)

    def d_short(i, taps, branches):
        near, far = masks(i)
        j = jnp.minimum(i * 16 + 16, 248)
        after = k.keep[span(j, 8), :]
        inside = i < 15
        tail_near = jnp.where(inside, after, last)
        tail_far = jnp.where(
            inside, after * jnp.concatenate([near[15:16, :], after[0:7, :]], 0), last
        )
        near = jnp.concatenate([near, tail_near], 0)
        far = jnp.concatenate([far, tail_far], 0)
        ext = k.p[pl.ds(pl.multiple_of(i * 16 + 8, 8), 24), :]
        rows = span(i * 16, 16)
        new = []
        for n, b in enumerate(branches):
            l = slice(b * 256, b * 256 + 256)
            e, db = ext[:, l], k.dq[pl.ds(pl.multiple_of(i * 16, 16), 24), l]
            dn, df = near * db, far * db
            k.dp[rows, l] = (
                k.taps[0:1, l] * db[0:16] + k.taps[1:2, l] * dn[1:17] + k.taps[2:3, l] * df[2:18]
            ).astype(BF16)
            new.append(taps[3 * n + 0] + jnp.sum(e[8:24] * db[0:16], axis=0, keepdims=True))
            new.append(taps[3 * n + 1] + jnp.sum(e[7:23] * dn[0:16], axis=0, keepdims=True))
            new.append(taps[3 * n + 2] + jnp.sum(e[6:22] * df[0:16], axis=0, keepdims=True))
        return tuple(new)

    line = jnp.zeros((1, 256), F32)
    def d_short_1(i, taps):
        return d_short(i, taps, (0,))

    def d_short_2(i, taps):
        return d_short(i, taps, (1, 2))

    d_taps = []

    def short_1():
        dq_first.wait()
        d_taps.extend(fold(16, d_short_1, (line,) * 3))

    tasks[SHORT_1] = short_1

    def retreat(a, b, keep):
        ka, kb = keep * a, keep * b
        return ka, kb, lr * ka + li * kb, lr * kb - li * ka

    def start_state(i, state):
        rows = span((31 - i) * 8, 8)
        dv, keep = k.dv[rows, :], k.keep[rows, :]
        for j in reversed(range(8)):
            a = cr * dv[j:j + 1, :] + state[0]
            b = state[1] - ci * dv[j:j + 1, :]
            _, _, pa, pb = retreat(a, b, keep[j:j + 1, :])
            state = (pa, pb)
        return state

    begin = fold(32, start_state, (zero, zero))
    arrive = chain(begin, k.backs_y, k.backs_z, -1, (BACKS_Y, BACKS_Z))
    at(ADJOINT)

    def adjoint(i, carry):
        rows = span((31 - i) * 8, 8)
        dv, keep = k.dv[rows, :], k.keep[rows, :]
        for j in reversed(range(8)):
            t = (31 - i) * 8 + j
            d = dv[j:j + 1, :]
            a = cr * d + carry[0]
            b = carry[1] - ci * d
            k.u[pl.ds(t, 1), :] = jnp.sum(a, axis=0, keepdims=True)
            _, _, pa, pb = retreat(a, b, keep[j:j + 1, :])
            carry = (pa, pb)
        return carry

    fold(32, adjoint, arrive)

    def d_poles(i, carry):
        pa, pb, dcr, dci, dlr, dli = carry
        rows = span((31 - i) * 8, 8)
        dv, keep = k.dv[rows, :], k.keep[rows, :]
        for j in reversed(range(8)):
            t = (31 - i) * 8 + j
            d = dv[j:j + 1, :]
            a = cr * d + pa
            b = pb - ci * d
            dcr = dcr + d * k.st_re[t + 1]
            dci = dci - d * k.st_im[t + 1]
            ka, kb, pa, pb = retreat(a, b, keep[j:j + 1, :])
            sr, si = k.st_re[t], k.st_im[t]
            dlr = dlr + ka * sr + kb * si
            dli = dli + kb * sr - ka * si
        return pa, pb, dcr, dci, dlr, dli

    def d_branches(i):
        rows = span(i * 32, 32)
        du = k.u[rows, :]
        k.dq[rows, 256:512] = du * k.q2[rows, :]
        k.dq[rows, 512:768] = du * k.q1[rows, :]
    loop(8, d_branches)
    dq_next = dq_edge(others, S.dq_s, R.dq_s)
    dq_next.start()
    at(DQ)
    dq_next.wait()
    d_taps.extend(fold(16, d_short_2, (line,) * 6))

    def d_n1(i):
        w = jnp.concatenate([weight(n, h, i) for n in (IN, IN_2) for h in range(2)], 1)
        k.part[:, span(i * 512, 512)] = nt(k.dp[...], w).astype(BF16)
    loop(4, d_n1)
    s_dn1 = cross(3)
    s_dn1.begin()
    at(DN1_0)

    small_1 = trade(1, k.small_y.at[y], k.small_y)
    small_2 = trade(0, k.small_z.at[z], k.small_z)

    def small_total(ref):
        return sum(ref[j].astype(F32) for j in range(4))

    small_x = remote(k.small_sum, k.small_sib, S.small_x, R.small_x, r.sib)

    def small(i):
        if i == 0:
            _, _, *dpoles = fold(32, d_poles, (*arrive, zero, zero, zero, zero))
            for j in range(4):
                k.small_y[y, 16 * j:16 * j + 16] = dpoles[j].astype(BF16)
            k.small_y[y, 64:80] = jnp.concatenate([d_taps[3 * b + t] for t in range(3) for b in range(3)] + [jnp.zeros((7, 256), F32)], 0).astype(BF16)
            small_1.begin()
        elif i == 1:
            small_1.end()
            k.small_z[z] = small_total(k.small_y).astype(BF16)
            small_2.begin()
        else:
            small_2.end()
            k.small_sum[...] = small_total(k.small_z)
            dcr, dci, dlr, dli = (k.small_sum[16 * j:16 * j + 16, :] for j in range(4))
            dgin = k.res_re[:, channels] * dcr + k.res_im[:, channels] * dci
            k.small_sum[0:16, :] = dgin * k.tab[7] - (lr * dlr + li * dli)
            k.small_sum[16:32, :] = lr * dli - li * dlr
            k.small_sum[32:48, :] = k.tab[6] * dcr
            k.small_sum[48:64, :] = k.tab[6] * dci
            small_x.start()

    tasks[SMALL] = small
    at(DN1_X)
    s_dn1.near_half()
    at(DN1_1)
    s_dn1.far_half()
    at(DN1_2)
    s_dn1.end()

    def d_norm_one(i):
        rows = pl.ds(pl.multiple_of(i * 16, 16), 16)
        here = pl.ds(pl.multiple_of(x * 32 + i * 16, 16), 16)
        a = k.tok[here, :].astype(F32)
        s = lax.rsqrt(jnp.mean(a * a, axis=-1, keepdims=True) + EPSILON)
        hat = a * s
        dn = s_dn1.result(rows)
        dng = dn * k.gains[0:1, :]
        k.gt[here, :] = (
            k.dhf[rows, :] + s * (dng - hat * jnp.mean(dng * hat, axis=-1, keepdims=True))
        ).astype(BF16)
        t = jnp.sum(dn * hat, axis=0, keepdims=True)

        @pl.when(i == 0)
        def _():
            k.ggain[0:1, :] = t

        @pl.when(i > 0)
        def _():
            k.ggain[0:1, :] += t
    loop(2, d_norm_one)
    g_gt = CrossGather(r, k.gt, False, S.cg.at[3], R.cg.at[3])
    g_gt.begin()

    def piece(ref, width):
        return lambda i: ref.at[:, pl.ds(pl.multiple_of(i * width, width), width)]

    gg_1 = trade(0, piece(k.ggain, 512), k.gg_z)
    gg_2 = trade(1, piece(k.gg_1, 128), k.gg_y)
    gg_3 = trade(2, k.gg_s, k.gg_x)
    gg_sib = remote(k.gg_2, k.gg_s, S.gg_s, R.gg_s, r.sib)
    gg_1.begin()
    k.gg_z[z] = k.ggain[:, span(z * 512, 512)]
    at(GT_0)
    gg_1.end()
    k.gg_1[...] = sum(k.gg_z[j] for j in range(4))
    gg_2.begin()
    k.gg_y[y] = k.gg_1[:, span(y * 128, 128)]
    at(GT_1)
    g_gt.middle()
    at(GT_2)
    gg_2.end()
    k.gg_2[...] = sum(k.gg_y[j] for j in range(4))
    gg_sib.start()
    at(GT_3)
    gg_sib.wait()
    k.gg_s[...] = k.gg_s[...] + k.gg_2[...]
    gg_3.begin()
    k.gg_x[x] = k.gg_s[...]
    g_gt.end()
    out_gt = pltpu.make_async_copy(k.gt, k.grad_tok, local.at[1])
    out_gt.start()
    at(GT_4)
    small_x.wait()
    gg_3.end()
    k.gg_out[...] = sum(k.gg_x[j] for j in range(4))

    for n in range(S_IN, 11):
        both = k.other.at[:, 0:SECOND[n - S_IN][0][1] + SECOND[n - S_IN][1][1]]
        waiting(both, S.rs_sib.at[n - S_IN]).wait_send()
        waiting(both, R.rs_sib.at[n - S_IN]).wait_recv()
        for h in range(2):
            (ref, here, at), (o, w) = finished(n, h), SECOND[n - S_IN][h]
            there = pl.ds(o + (LANES_A if h else 0), w)
            pltpu.make_async_copy(ref.at[z, y, my64, here], k.grad_w.at[0, :, there], local.at[2]).start()
            pltpu.make_async_copy(sib_bufs[h].at[:, at], k.grad_w.at[1, :, there], local.at[2]).start()
    for j, src in enumerate((k.small_sum, k.small_sib)):
        pltpu.make_async_copy(src, k.grad_small.at[j], local.at[3]).start()
    out_gain = pltpu.make_async_copy(k.gg_out, k.grad_gain, local.at[4])
    out_gain.start()
    out_bo.wait()
    out_gt.wait()
    pltpu.make_async_copy(k.grad_w, k.grad_w, local.at[2]).wait()
    pltpu.make_async_copy(k.grad_small, k.grad_small, local.at[3]).wait()
    out_gain.wait()
    for n in (A_IN, A_REST):
        waiting(k.other.at[:, 0:(768, 2432)[n]], S.w_sib.at[n]).wait_send()
    for piece in sum(gather + scatter, []):
        piece.drain()
    for copy in [gain_sib, keep_sib, gy_sib, n1_sib, edge]:
        copy.wait_send()
    for group in trades + [s_dn1, g_n2, g_bo, g_dh, g_gt]:
        group.drain()


def block(*arrays):
    sems = []
    for _, shape in fields(Sems):
        sems += [pltpu.SemaphoreType.DMA(a) for a in shape]
    vmem = pl.BlockSpec(memory_space=pltpu.VMEM)
    return pl.pallas_call(
        kernel,
        out_shape=(
            jax.ShapeDtypeStruct((128, 2048), BF16),
            jax.ShapeDtypeStruct((128, 2048), BF16),
            jax.ShapeDtypeStruct((2, 64, LANES_A + LANES_B), BF16),
            jax.ShapeDtypeStruct((2, 80, 256), F32),
            jax.ShapeDtypeStruct((8, 128), F32),
        ),
        in_specs=[vmem] * len(arrays),
        out_specs=[pl.BlockSpec(memory_space=pl.ANY)] * 5,
        scratch_shapes=[pltpu.VMEM(*value) for _, value in fields(Scratch)] + sems + [pltpu.SemaphoreType.DMA((5,))],
        compiler_params=pltpu.CompilerParams(
            collective_id=0, has_side_effects=True, vmem_limit_bytes=63 * 2**20
        ),
        name="block",
    )(*arrays)


def results(*refs):
    sources, refs = refs[:5], refs[5:]
    (bo, gt, g_gain_1, g_in, g_taps, g_decay, g_angle, g_re, g_im, g_out, g_gain_2, g_gate, g_up, g_down) = refs[:14]
    grad_w, small, gain, sems = refs[14:]
    c = lax.rem(lax.axis_index("seq"), 2)
    copies = [
        pltpu.make_async_copy(source, ref, sems.at[i])
        for i, (source, ref) in enumerate(zip(sources, (bo, gt, grad_w, small, gain)))
    ]
    for copy in copies[::-1]:
        copy.start()
    for copy in copies[2:]:
        copy.wait()

    def cols(core, n, start, stop):
        wa = WHOLE[n][0][1]
        parts = []
        if start < wa:
            parts.append(grad_w[core, :, WHOLE[n][0][0] + start:WHOLE[n][0][0] + min(stop, wa)])
        if stop > wa:
            o = LANES_A + WHOLE[n][1][0]
            parts.append(grad_w[core, :, o + max(start - wa, 0):o + stop - wa])
        return jnp.concatenate(parts, 1).astype(F32)

    for at, core in ((0, c), (1, 1 - c)):
        g_in[0, :, at * 256:at * 256 + 256] = cols(core, IN, 0, 256)
        for b in (1, 2):
            g_in[b, :, at * 256:at * 256 + 256] = cols(core, IN_2, b * 256 - 256, b * 256)
        g_out[:, at * 256:at * 256 + 256] = cols(core, OUT, 0, 256)
        g_gate[:, at * 640:at * 640 + 640] = cols(core, GU, 0, 640)
        g_up[:, at * 640:at * 640 + 640] = cols(core, GU, 640, 1280)
        g_down[:, at * 640:at * 640 + 640] = cols(core, DOWN, 0, 640)
        here = slice(at * 256, at * 256 + 256)
        for i, ref in enumerate((g_decay, g_angle, g_re, g_im)):
            ref[:, here] = small[core, 16 * i:16 * i + 16, :]
        for i in range(3):
            g_taps[i, :, here] = small[core, 64 + 3 * i:67 + 3 * i, :]
    first, second = cols(c, GU, 1280, 1408), cols(1 - c, GU, 1280, 1408)
    g_gate[:, 1280:1408] = jnp.concatenate([first[:, 0:64], second[:, 0:64]], 1)
    g_up[:, 1280:1408] = jnp.concatenate([first[:, 64:128], second[:, 64:128]], 1)
    first, second = cols(c, DOWN, 640, 768), cols(1 - c, DOWN, 640, 768)
    g_down[:, 1280:1408] = jnp.concatenate([first[:, 0:64], second[:, 0:64]], 1)
    for i, ref in enumerate((g_gain_1, g_gain_2)):
        a = gain[i:i + 1, :]
        ref[...] = jnp.where(c == 0, a[:, 0:64], a[:, 64:128])
    for copy in copies[:2]:
        copy.wait()


def on_device(
    tokens, cotangent, resets, norm1_gain, in_weight, conv_weight, pole_decay, pole_angle, residue_re, residue_im,
    out_weight, norm2_gain, gate_weight, up_weight, down_weight,
):
    raw = block(
        in_weight.transpose(1, 0, 2), out_weight, gate_weight, up_weight, down_weight, norm1_gain.reshape(1, 64),
        norm2_gain.reshape(1, 64), resets.reshape(1, 128), tokens, cotangent, conv_weight, pole_decay, pole_angle,
        residue_re, residue_im,
    )
    vmem = pl.BlockSpec(memory_space=pltpu.VMEM)
    shapes = [
        ((128, 2048), BF16), ((128, 2048), BF16), ((1, 64), F32), ((3, 64, 512), F32), ((3, 3, 512), F32),
        ((16, 512), F32), ((16, 512), F32), ((16, 512), F32), ((16, 512), F32), ((64, 512), F32), ((1, 64), F32),
        ((64, 1408), F32), ((64, 1408), F32), ((64, 1408), F32),
    ]
    outs = list(pl.pallas_call(
        results,
        out_shape=[jax.ShapeDtypeStruct(s, t) for s, t in shapes],
        in_specs=[pl.BlockSpec(memory_space=pl.ANY)] * len(raw),
        out_specs=[vmem] * len(shapes),
        scratch_shapes=[pltpu.VMEM(a.shape, a.dtype) for a in raw[2:]] + [pltpu.SemaphoreType.DMA((5,))],
        compiler_params=pltpu.CompilerParams(vmem_limit_bytes=60 * 2**20),
        name="results",
    )(*raw))
    outs[2], outs[10] = outs[2].reshape(64), outs[10].reshape(64)
    outs[3] = outs[3].transpose(1, 0, 2)
    return tuple(outs)


def solution(mesh):
    row, cols = P("seq", "mp"), P(None, "mp")
    return jax.shard_map(
        on_device,
        mesh=mesh,
        in_specs=(
            P("seq", None), P("seq", None), P("seq"), P("seq"), P("seq", None, "mp"), P(None, None, "mp"),
            cols, cols, cols, cols, row, P("seq"), row, row, row,
        ),
        out_specs=(
            P("seq", None), P("seq", None), P("seq"), P("seq", None, "mp"), P(None, None, "mp"),
            cols, cols, cols, cols, row, P("seq"), row, row, row,
        ),
        check_vma=False,
    )
```

time: 174 us -> 166 us (0.954)
  Pallas kernels: 173 us -> 166 us
    pallas_call x1, Pallas kernels: 170 us -> 162 us  [block(): pl.pallas_call(kernel, out_shape=(jax.ShapeDtypeStruct((128, 2048), BF16)...]
where the time goes in v3:
time: 166 us
  Pallas kernels  166 us (100%)
    pallas_call x1, Pallas kernels, block(): pl.pallas_call(kernel, out_shape=(jax.ShapeDtypeStruct((128, 2048), BF16)...  162 us

profile of v3, /device:TPU:1, one launch (start us, length us, event | category | flops | bytes accessed | tf_op | source)
XLA Modules:
  0.0 166.2 jit_solution(14835976994865367322)
XLA Ops:
  0.7 162.4 %block.1 = (bf16[128,2048]{1,0:T(8,128)(2,1)}, bf16[128,2048]{1,0:T(8,128)(2,1)}, bf16[2,64,3200]{2,1,0:T(8,128)(2,1)}, f32[2,80,256]{2,1,0:T(8,128)}, f32[8,128]{1,0:T(8,128)}) custom-call(bf16[3,64,512]{2,1,0:T(8,128)(2,1)} %bitcast.7, bf16[64,512]{1,0:T(8,128)(2,1)} %refs_1_.1, bf16[64,1408]{1,0:T(8,128)(2,1)} %refs_2_.1, bf16[64,1408]{1,0:T(8,128)(2,1)} %refs_3_.1, ...), custom_call_target="tpu_custom_call" | custom-call | tf_op jit(solution)/shard_map/block/pallas_call | solution.py:1344
  163.1 3.1 %results.1 = (bf16[128,2048]{1,0:T(8,128)(2,1)}, bf16[128,2048]{1,0:T(8,128)(2,1)}, f32[1,64]{1,0:T(1,128)}, f32[3,64,512]{2,1,0:T(8,128)}, f32[3,3,512]{2,1,0:T...) custom-call(bf16[128,2048]{1,0:T(8,128)(2,1)} %get-tuple-element.33., ...), custom_call_target="tpu_custom_call" | custom-call | tf_op jit(solution)/shard_map/results/pallas_call | solution.py:1427

commit v4 on v3

--- a/solution.py
+++ b/solution.py
@@ -107,32 +107,31 @@
 AG, RS, WG, FFN, SMALL, SHORT_1 = range(6)
 PLAN = {
     START: ((AG, A_IN, 1),),
-    GAIN_Y: ((AG, A_REST, 1),),
-    GAIN_Z: ((AG, A_IN, 3), (AG, A_REST, 3), (AG, A_IN, 4), (AG, B_IN, 1), (AG, B_IN, 2), (AG, A_REST, 4),),
-    NORM_1: ((AG, B_IN, 3),),
-    EDGE: ((AG, B_GU_2, 1), (AG, B_IN, 4), (AG, B_OUT, 1),),
-    ENDS_Y: ((AG, B_GU_2, 2), (AG, B_OUT, 3),),
-    ENDS_Z: ((AG, B_GU, 1), (AG, B_DOWN, 1), (AG, B_GU, 2), (AG, B_OUT, 4),),
-    MIX_1: ((AG, B_GU, 3),),
-    MIX_2: ((AG, B_GU_2, 3),),
-    N2_0: ((AG, B_DOWN, 2),),
-    N2_1: ((AG, B_DOWN, 3), (AG, B_GU, 4), (AG, B_GU_2, 4),),
-    ACT: ((WG, DOWN), (RS, DOWN, 0), (AG, B_DOWN, 4),),
-    DA: ((RS, DOWN, 1),),
-    DN2_1: ((RS, DOWN, 2), (WG, GU), (RS, GU, 0), (RS, GU_2, 0),),
-    DH_0: ((RS, GU, 1), (RS, GU_2, 1),),
-    BACKS_Y: ((RS, GU, 2), (RS, DOWN, 3), (WG, OUT), (RS, OUT, 0),),
-    BACKS_Z: ((RS, OUT, 1), (FFN, 0), (RS, GU_2, 2), (FFN, 1), (SHORT_1,), (WG, IN), (RS, S_DOWN, 0),
-        (RS, GU, 3),),
-    DQ: ((RS, IN, 0), (RS, OUT, 2), (RS, GU_2, 3), (FFN, 2), (RS, S_GU, 0), (RS, IN, 1),),
-    DN1_X: ((WG, IN_2), (RS, IN_2, 0), (RS, IN, 2), (RS, IN_2, 1),),
+    GAIN_Y: ((AG, A_REST, 1), (AG, A_IN, 3),),
+    GAIN_Z: ((AG, A_REST, 3), (AG, A_IN, 4), (AG, B_IN, 1), (AG, B_IN, 2),),
+    EDGE: ((AG, B_IN, 3),),
+    PROJECT: ((AG, A_REST, 4), (AG, B_OUT, 1), (AG, B_GU_2, 1), (AG, B_IN, 4),),
+    ENDS_Y: ((AG, B_DOWN, 1),),
+    ENDS_Z: ((AG, B_OUT, 3), (AG, B_GU_2, 2), (AG, B_GU, 1), (AG, B_GU_2, 3),),
+    MIX: ((AG, B_OUT, 4),),
+    MIX_2: ((AG, B_GU, 2), (AG, B_GU, 3),),
+    N2_0: ((AG, B_DOWN, 2), (AG, B_DOWN, 3), (AG, B_GU_2, 4),),
+    FF: ((AG, B_GU, 4),),
+    ACT: ((WG, DOWN), (RS, DOWN, 0), (RS, DOWN, 1), (AG, B_DOWN, 4),),
+    DN2_1: ((RS, DOWN, 2), (WG, GU),),
+    DN2_2: ((RS, GU, 0), (RS, GU_2, 0), (FFN, 0), (RS, GU, 1),),
+    DH_1: ((RS, GU_2, 1), (FFN, 1),),
+    BACKS_Y: ((RS, GU, 2), (RS, DOWN, 3), (SHORT_1,), (WG, IN),),
+    BACKS_Z: ((RS, IN, 0), (FFN, 2), (WG, OUT), (RS, GU_2, 2), (RS, OUT, 0), (FFN, 3), (RS, OUT, 1),),
+    DQ: ((RS, IN, 1), (RS, IN, 2), (RS, GU_2, 3), (RS, GU, 3), (RS, S_GU, 0), (RS, OUT, 2),),
+    DN1_0: ((WG, IN_2), (RS, IN_2, 0), (RS, IN_2, 1),),
     DN1_1: ((SMALL, 0),),
-    DN1_2: ((RS, IN_2, 2),),
-    GT_0: ((RS, IN, 3), (RS, S_IN, 0), (RS, OUT, 3), (RS, S_OUT, 0), (RS, S_DOWN, 1), (SMALL, 1),),
-    GT_1: ((FFN, 3), (RS, IN_2, 3), (RS, S_IN_2, 0),),
-    GT_2: ((RS, S_IN, 1), (RS, S_GU, 1), (RS, S_OUT, 1), (RS, S_DOWN, 2), (FFN, 4), (SMALL, 2),),
-    GT_3: ((RS, S_IN_2, 1),),
-    GT_4: ((RS, S_GU, 2), (FFN, 5), (RS, S_IN, 2), (RS, S_OUT, 2), (RS, S_IN_2, 2),),
+    DN1_2: ((RS, IN, 3), (RS, S_IN, 0), (RS, OUT, 3), (RS, IN_2, 2),),
+    GT_0: ((RS, S_DOWN, 0), (SMALL, 1), (FFN, 4),),
+    GT_2: ((RS, S_OUT, 0), (RS, IN_2, 3), (RS, S_IN_2, 0), (RS, S_GU, 1), (RS, S_DOWN, 1), (RS, S_IN, 1),),
+    GT_3: ((RS, S_IN_2, 1), (SMALL, 2),),
+    GT_4: ((RS, S_OUT, 1), (RS, S_GU, 2), (FFN, 5), (RS, S_DOWN, 2), (RS, S_IN_2, 2), (RS, S_IN, 2),
+        (RS, S_OUT, 2),),
 }
 
 
@@ -142,20 +141,21 @@
         self.chip = self.z * 4 + self.y
         self.sib = device(self.z, self.y, 1 - self.c, self.x)
 
-    def near(self, axis, d):
+    def near(self, axis, d, other=False):
+        c = 1 - self.c if other else self.c
         if axis == 0:
-            return device(rem4(self.z + d), self.y, self.c, self.x)
+            return device(rem4(self.z + d), self.y, c, self.x)
         if axis == 1:
-            return device(self.z, rem4(self.y + d), self.c, self.x)
-        return device(self.z, self.y, self.c, rem4(self.x + d))
+            return device(self.z, rem4(self.y + d), c, self.x)
+        return device(self.z, self.y, c, rem4(self.x + d))
 
     def along(self, d):
         return (lax.rem(self.chip + d + 16, 16) * 2 + self.c, self.x)
 
 
 class Gather:
-    def __init__(self, r, ref, lanes, rows, phase, axis, split, send, recv):
-        self.r, self.ref, self.lanes, self.rows = r, ref, lanes, rows
+    def __init__(self, r, ref, lanes, rows, phase, axis, split, send, recv, own=None):
+        self.r, self.ref, self.lanes, self.rows, self.own = r, ref, lanes, rows, own
         self.phase, self.axis, self.split = phase, axis, split
         self.send, self.recv, self.sent = send, recv, []
 
@@ -177,7 +177,14 @@
         self.sent.append(copy)
 
     def step(self, i):
-        if i == 1 and not self.split:
+        if i == 1 and self.own:
+            there = self.ref.at[self.r.z, self.r.y, self.own[1], self.lanes]
+            for j, d in enumerate((1, -1)):
+                for other, src in enumerate((there, self.own[0])):
+                    to = self.r.near(self.axis, d, bool(other))
+                    self.sent.append(remote(src, there, self.send, self.recv.at[j], to))
+                    self.sent[-1].start()
+        elif i == 1 and not self.split:
             self.start(0, 0, 1, 0)
             self.start(0, 0, -1, 1)
         elif i == 1:
@@ -482,8 +489,9 @@
     db = ((4, 4, 128, 384), BF16)
     sib_a = ((64, LANES_A), BF16)
     sib_b = ((64, LANES_B), BF16)
-    gains_y = ((4, 16, 128), F32)
-    gains_all = ((4, 4, 16, 128), F32)
+    gain_pair = ((2, 8, 128), F32)
+    gains_y = ((4, 8, 128), F32)
+    gains_all = ((4, 4, 8, 128), F32)
     gains = ((8, 2048), F32)
     gain_in = ((8, 128), F32)
     taps = ((8, 768), F32)
@@ -512,10 +520,10 @@
     z = ((256, 256), BF16)
     st_re = ((257, 16, 256), F32)
     st_im = ((257, 16, 256), F32)
-    ends_y = ((4, 32, 256), F32)
-    ends_z = ((4, 32, 256), F32)
-    backs_y = ((4, 32, 256), F32)
-    backs_z = ((4, 32, 256), F32)
+    ends_y = ((4, 32, 256), BF16)
+    ends_z = ((4, 32, 256), BF16)
+    backs_y = ((4, 32, 256), BF16)
+    backs_z = ((4, 32, 256), BF16)
     gu = ((256, 1408), F32)
     act = ((256, 768), BF16)
     dgu = ((256, 1408), BF16)
@@ -541,13 +549,13 @@
 
 
 class Sems:
-    w = (7, 4), (7, 4, 3)
+    w = (18,), (18, 3)
     w_sib = (2,), (2,)
     gain_sib = keep_s = gy_s = n1_s = edge = dq_s = dq_1 = small_x = gg_s = (), ()
     trade = (11,), (11,)
     sum = (4,), (4, 5)
     cg = (4,), (4, 5)
-    rs = (11, 4), (11, 4, 3)
+    rs = (26,), (26, 3)
     rs_sib = (5,), (5,)
 
 
@@ -567,6 +575,7 @@
 
     barrier = pltpu.get_barrier_semaphore()
     peers = [r.sib] + [r.near(a, d) for a in range(3) for d in (1, 2, 3)] + [r.along(1), r.along(-1)]
+    peers += [r.near(a, d, True) for a in range(2) for d in (1, -1)]
     for peer in peers:
         pl.semaphore_signal(barrier, inc=1, device_id=peer, device_id_type=MESH)
 
@@ -598,9 +607,11 @@
     my128 = span(c * 128, 128)
     gather = []
     for n, (phase, split, parts) in enumerate(GATHERS):
+        first = sum(len(group) for group in gather)
         gather.append([
             Gather(r, g[b], pl.ds(o, w), rows, phase, 1 - way if phase == 0 else way, split and rows[1] == 128,
-                   S.w.at[n, i], R.w.at[n, i])
+                   S.w.at[first + i], R.w.at[first + i],
+                   (k.other.at[:, pl.ds(o + (LANES_A if b else 0), w)], my64) if n == A_IN else None)
             for i, (way, b, o, w, *rows) in enumerate(parts)
         ])
 
@@ -651,13 +662,11 @@
             S.w_sib.at[n], R.w_sib.at[n], r.sib,
         )
 
-    eight = span(c * 8, 8)
     side = lax.broadcasted_iota(jnp.int32, (1, 128), 1) // 64 == c
     for i, ref in enumerate((k.gain_1, k.gain_2)):
         a = ref[...].astype(F32)
         k.gain_in[i:i + 1, :] = jnp.where(side, jnp.concatenate([a, a], 1), 0.0)
     k.gain_in[2:8, :] = jnp.zeros((6, 128), F32)
-    k.gains_y[y, eight] = k.gain_in[...]
     for n in (IN, IN_2):
         put(1 - c, n, to_other)
         put(c, n, to_own)
@@ -666,7 +675,7 @@
     k.keep[my128] = jnp.concatenate([keep, keep], 1)
     pl.semaphore_wait(barrier, len(peers))
 
-    gain_sib = remote(k.gain_in, k.gains_y.at[y, eight], S.gain_sib, R.gain_sib, r.sib)
+    gain_sib = remote(k.gain_in, k.gain_pair.at[c], S.gain_sib, R.gain_sib, r.sib)
     keep_sib = remote(k.keep.at[my128], k.keep.at[my128], S.keep_s, R.keep_s, r.sib)
     gy_sib = remote(k.cot, k.gy.at[my128], S.gy_s, R.gy_s, r.sib)
     def share(n):
@@ -677,7 +686,7 @@
     gain_sib.start()
 
     def ag(n, i):
-        if i == 1 and n in (A_IN, A_REST):
+        if (n, i) in ((A_IN, 4), (A_REST, 1)):
             waiting(k.other.at[:, 0:(768, 2432)[n]], R.w_sib.at[n]).wait_recv()
         for piece in gather[n]:
             piece.step(i)
@@ -693,6 +702,7 @@
     gain_y = trade(1, k.gains_y.at[y], k.gains_y)
     gain_z = trade(0, k.gains_y, k.gains_all)
     gain_sib.wait_recv()
+    k.gains_y[y] = k.gain_in[...] + k.gain_pair[1 - c]
     gain_y.begin()
 
     for n in (OUT, GU, DOWN):
@@ -726,7 +736,7 @@
 
     gain_z.end()
     for i in range(16):
-        k.gains[:, i * 128:(i + 1) * 128] = k.gains_all[i // 4, i % 4, 0:8] + k.gains_all[i // 4, i % 4, 8:16]
+        k.gains[:, i * 128:(i + 1) * 128] = k.gains_all[i // 4, i % 4]
 
     def norm_one(i):
         rows = span(i * 16, 16)
@@ -811,13 +821,13 @@
         qr, qi = pr, sign * pi
 
         def put(ref, at, state):
-            ref[at, 0:16] = state[0]
-            ref[at, 16:32] = state[1]
+            ref[at, 0:16] = state[0].astype(BF16)
+            ref[at, 16:32] = state[1].astype(BF16)
 
         def horner(ref, wr, wi, state, here, every):
             for i in order:
                 nr, ni = times(wr, wi, *state)
-                nr, ni = nr + ref[i, 0:16], ni + ref[i, 16:32]
+                nr, ni = nr + ref[i, 0:16].astype(F32), ni + ref[i, 16:32].astype(F32)
                 use = (i < here) if sign > 0 else (i > here)
                 state = (nr, ni) if every else (jnp.where(use, nr, state[0]), jnp.where(use, ni, state[1]))
             return state
@@ -954,6 +964,7 @@
     for n, parts in enumerate(SCATTERS):
         phase = 0 if n < S_IN else 1
         m = {S_IN: IN, S_DOWN: DOWN}.get(n, n if phase == 0 else None)
+        first = sum(len(group) for group in scatter)
         scatter.append([])
         for i, (way, b, o, w, *rows) in enumerate(parts):
             ref, here = g[b], pl.ds(o, w)
@@ -962,7 +973,7 @@
             buf = ((k.s0a, k.s0b), (k.s1a, k.s1b))[phase][b]
             axis = 1 - way if phase == 0 else way
             scatter[n].append(
-                Scatter(r, ref, here, rows, pl.ds(o, w), phase, axis, buf, S.rs.at[n, i], R.rs.at[n, i])
+                Scatter(r, ref, here, rows, pl.ds(o, w), phase, axis, buf, S.rs.at[first + i], R.rs.at[first + i])
             )
 
     def finished(n, h):
@@ -1362,6 +1373,7 @@
 
 def results(*refs):
     sources, refs = refs[:5], refs[5:]
+    outs, refs = refs[:14], refs[14:]
     (bo, gt, g_gain_1, g_in, g_taps, g_decay, g_angle, g_re, g_im, g_out, g_gain_2, g_gate, g_up, g_down) = refs[:14]
     grad_w, small, gain, sems = refs[14:]
     c = lax.rem(lax.axis_index("seq"), 2)
@@ -1369,6 +1381,7 @@
         pltpu.make_async_copy(source, ref, sems.at[i])
         for i, (source, ref) in enumerate(zip(sources, (bo, gt, grad_w, small, gain)))
     ]
+    leaving = [pltpu.make_async_copy(ref, out, sems.at[5 + i]) for i, (ref, out) in enumerate(zip(refs, outs))]
     for copy in copies[::-1]:
         copy.start()
     for copy in copies[2:]:
@@ -1384,28 +1397,42 @@
             parts.append(grad_w[core, :, o + max(start - wa, 0):o + stop - wa])
         return jnp.concatenate(parts, 1).astype(F32)
 
-    for at, core in ((0, c), (1, 1 - c)):
+    cores = ((0, c), (1, 1 - c))
+    for at, core in cores:
         g_in[0, :, at * 256:at * 256 + 256] = cols(core, IN, 0, 256)
         for b in (1, 2):
             g_in[b, :, at * 256:at * 256 + 256] = cols(core, IN_2, b * 256 - 256, b * 256)
-        g_out[:, at * 256:at * 256 + 256] = cols(core, OUT, 0, 256)
+    leaving[3].start()
+    for at, core in cores:
         g_gate[:, at * 640:at * 640 + 640] = cols(core, GU, 0, 640)
         g_up[:, at * 640:at * 640 + 640] = cols(core, GU, 640, 1280)
+    first, second = cols(c, GU, 1280, 1408), cols(1 - c, GU, 1280, 1408)
+    g_gate[:, 1280:1408] = jnp.concatenate([first[:, 0:64], second[:, 0:64]], 1)
+    g_up[:, 1280:1408] = jnp.concatenate([first[:, 64:128], second[:, 64:128]], 1)
+    leaving[11].start()
+    leaving[12].start()
+    for copy in copies[:2]:
+        copy.wait()
+    leaving[0].start()
+    leaving[1].start()
+    for at, core in cores:
         g_down[:, at * 640:at * 640 + 640] = cols(core, DOWN, 0, 640)
+    first, second = cols(c, DOWN, 640, 768), cols(1 - c, DOWN, 640, 768)
+    g_down[:, 1280:1408] = jnp.concatenate([first[:, 0:64], second[:, 0:64]], 1)
+    leaving[13].start()
+    for at, core in cores:
         here = slice(at * 256, at * 256 + 256)
+        g_out[:, here] = cols(core, OUT, 0, 256)
         for i, ref in enumerate((g_decay, g_angle, g_re, g_im)):
             ref[:, here] = small[core, 16 * i:16 * i + 16, :]
         for i in range(3):
             g_taps[i, :, here] = small[core, 64 + 3 * i:67 + 3 * i, :]
-    first, second = cols(c, GU, 1280, 1408), cols(1 - c, GU, 1280, 1408)
-    g_gate[:, 1280:1408] = jnp.concatenate([first[:, 0:64], second[:, 0:64]], 1)
-    g_up[:, 1280:1408] = jnp.concatenate([first[:, 64:128], second[:, 64:128]], 1)
-    first, second = cols(c, DOWN, 640, 768), cols(1 - c, DOWN, 640, 768)
-    g_down[:, 1280:1408] = jnp.concatenate([first[:, 0:64], second[:, 0:64]], 1)
     for i, ref in enumerate((g_gain_1, g_gain_2)):
         a = gain[i:i + 1, :]
         ref[...] = jnp.where(c == 0, a[:, 0:64], a[:, 64:128])
-    for copy in copies[:2]:
+    for i in (9, 4, 5, 6, 7, 8, 2, 10):
+        leaving[i].start()
+    for copy in leaving:
         copy.wait()
 
 
@@ -1418,7 +1445,6 @@
         norm2_gain.reshape(1, 64), resets.reshape(1, 128), tokens, cotangent, conv_weight, pole_decay, pole_angle,
         residue_re, residue_im,
     )
-    vmem = pl.BlockSpec(memory_space=pltpu.VMEM)
     shapes = [
         ((128, 2048), BF16), ((128, 2048), BF16), ((1, 64), F32), ((3, 64, 512), F32), ((3, 3, 512), F32),
         ((16, 512), F32), ((16, 512), F32), ((16, 512), F32), ((16, 512), F32), ((64, 512), F32), ((1, 64), F32),
@@ -1428,8 +1454,9 @@
         results,
         out_shape=[jax.ShapeDtypeStruct(s, t) for s, t in shapes],
         in_specs=[pl.BlockSpec(memory_space=pl.ANY)] * len(raw),
-        out_specs=[vmem] * len(shapes),
-        scratch_shapes=[pltpu.VMEM(a.shape, a.dtype) for a in raw[2:]] + [pltpu.SemaphoreType.DMA((5,))],
+        out_specs=[pl.BlockSpec(memory_space=pl.ANY)] * len(shapes),
+        scratch_shapes=[pltpu.VMEM(*a) for a in shapes] + [pltpu.VMEM(a.shape, a.dtype) for a in raw[2:]]
+        + [pltpu.SemaphoreType.DMA((19,))],
         compiler_params=pltpu.CompilerParams(vmem_limit_bytes=60 * 2**20),
         name="results",
     )(*raw))

time: 166 us -> 161 us (0.970)
  Pallas kernels: 166 us -> 160 us
    pallas_call x1, Pallas kernels: 162 us -> 157 us  [block(): pl.pallas_call(kernel, out_shape=(jax.ShapeDtypeStruct((128, 2048), BF16)...]
where the time goes in v4:
time: 161 us
  Pallas kernels  160 us (99%)
    pallas_call x1, Pallas kernels, block(): pl.pallas_call(kernel, out_shape=(jax.ShapeDtypeStruct((128, 2048), BF16)...  157 us

profile of v4, /device:TPU:1, one launch (start us, length us, event | category | flops | bytes accessed | tf_op | source)
XLA Modules:
  0.0 161.0 jit_solution(6654729850076645717)
XLA Ops:
  0.7 157.4 %block.1 = (bf16[128,2048]{1,0:T(8,128)(2,1)}, bf16[128,2048]{1,0:T(8,128)(2,1)}, bf16[2,64,3200]{2,1,0:T(8,128)(2,1)}, f32[2,80,256]{2,1,0:T(8,128)}, f32[8,128]{1,0:T(8,128)}) custom-call(bf16[3,64,512]{2,1,0:T(8,128)(2,1)} %bitcast.7, bf16[64,512]{1,0:T(8,128)(2,1)} %refs_1_.1, bf16[64,1408]{1,0:T(8,128)(2,1)} %refs_2_.1, bf16[64,1408]{1,0:T(8,128)(2,1)} %refs_3_.1, ...), custom_call_target="tpu_custom_call" | custom-call | tf_op jit(solution)/shard_map/block/pallas_call | solution.py:1355
  158.0 3.0 %results.1 = (bf16[128,2048]{1,0:T(8,128)(2,1)}, bf16[128,2048]{1,0:T(8,128)(2,1)}, f32[1,64]{1,0:T(1,128)}, f32[3,64,512]{2,1,0:T(8,128)}, f32[3,3,512]{2,1,0:T...) custom-call(bf16[128,2048]{1,0:T(8,128)(2,1)} %get-tuple-element.33., ...), custom_call_target="tpu_custom_call" | custom-call | tf_op jit(solution)/shard_map/results/pallas_call | solution.py:1453

commit v5 on v4

--- a/solution.py
+++ b/solution.py
@@ -108,30 +108,31 @@
 PLAN = {
     START: ((AG, A_IN, 1),),
     GAIN_Y: ((AG, A_REST, 1), (AG, A_IN, 3),),
-    GAIN_Z: ((AG, A_REST, 3), (AG, A_IN, 4), (AG, B_IN, 1), (AG, B_IN, 2),),
-    EDGE: ((AG, B_IN, 3),),
-    PROJECT: ((AG, A_REST, 4), (AG, B_OUT, 1), (AG, B_GU_2, 1), (AG, B_IN, 4),),
-    ENDS_Y: ((AG, B_DOWN, 1),),
-    ENDS_Z: ((AG, B_OUT, 3), (AG, B_GU_2, 2), (AG, B_GU, 1), (AG, B_GU_2, 3),),
+    GAIN_Z: ((AG, A_REST, 3), (AG, A_IN, 4), (AG, B_IN, 1),),
+    NORM_1: ((AG, B_IN, 2),),
+    EDGE: ((AG, B_IN, 3), (AG, A_REST, 4), (AG, B_GU_2, 1), (AG, B_OUT, 1),),
+    PROJECT: ((AG, B_IN, 4),),
+    ENDS_Y: ((AG, B_GU, 1),),
+    ENDS_Z: ((AG, B_OUT, 3), (AG, B_DOWN, 1), (AG, B_GU, 2), (AG, B_GU, 3), (AG, B_GU_2, 2),),
     MIX: ((AG, B_OUT, 4),),
-    MIX_2: ((AG, B_GU, 2), (AG, B_GU, 3),),
-    N2_0: ((AG, B_DOWN, 2), (AG, B_DOWN, 3), (AG, B_GU_2, 4),),
-    FF: ((AG, B_GU, 4),),
+    MIX_0: ((AG, B_GU_2, 3),),
+    N2_0: ((AG, B_GU, 4), (AG, B_DOWN, 2), (AG, B_DOWN, 3),),
+    FF: ((AG, B_GU_2, 4),),
     ACT: ((WG, DOWN), (RS, DOWN, 0), (RS, DOWN, 1), (AG, B_DOWN, 4),),
     DN2_1: ((RS, DOWN, 2), (WG, GU),),
-    DN2_2: ((RS, GU, 0), (RS, GU_2, 0), (FFN, 0), (RS, GU, 1),),
-    DH_1: ((RS, GU_2, 1), (FFN, 1),),
-    BACKS_Y: ((RS, GU, 2), (RS, DOWN, 3), (SHORT_1,), (WG, IN),),
-    BACKS_Z: ((RS, IN, 0), (FFN, 2), (WG, OUT), (RS, GU_2, 2), (RS, OUT, 0), (FFN, 3), (RS, OUT, 1),),
-    DQ: ((RS, IN, 1), (RS, IN, 2), (RS, GU_2, 3), (RS, GU, 3), (RS, S_GU, 0), (RS, OUT, 2),),
-    DN1_0: ((WG, IN_2), (RS, IN_2, 0), (RS, IN_2, 1),),
-    DN1_1: ((SMALL, 0),),
-    DN1_2: ((RS, IN, 3), (RS, S_IN, 0), (RS, OUT, 3), (RS, IN_2, 2),),
-    GT_0: ((RS, S_DOWN, 0), (SMALL, 1), (FFN, 4),),
-    GT_2: ((RS, S_OUT, 0), (RS, IN_2, 3), (RS, S_IN_2, 0), (RS, S_GU, 1), (RS, S_DOWN, 1), (RS, S_IN, 1),),
-    GT_3: ((RS, S_IN_2, 1), (SMALL, 2),),
-    GT_4: ((RS, S_OUT, 1), (RS, S_GU, 2), (FFN, 5), (RS, S_DOWN, 2), (RS, S_IN_2, 2), (RS, S_IN, 2),
-        (RS, S_OUT, 2),),
+    DN2_2: ((RS, GU, 0), (RS, GU_2, 0), (FFN, 0), (RS, GU_2, 1),),
+    DH_1: ((RS, GU, 1),),
+    BACKS_Y: ((RS, GU_2, 2), (WG, OUT), (RS, OUT, 0), (FFN, 1), (SHORT_1,), (WG, IN),),
+    BACKS_Z: ((RS, IN, 0), (RS, GU, 2), (RS, GU_2, 3), (RS, IN, 1), (FFN, 2),),
+    DQ: ((RS, OUT, 1), (RS, OUT, 2), (RS, IN, 2), (RS, GU, 3), (RS, S_GU, 0),),
+    DN1_0: ((WG, IN_2), (RS, IN_2, 0),),
+    DN1_1: ((RS, IN_2, 1), (SMALL, 0),),
+    DN1_2: ((FFN, 3), (RS, IN, 3), (RS, OUT, 3), (RS, S_IN, 0), (RS, IN_2, 2),),
+    GT_0: ((RS, DOWN, 3), (RS, S_DOWN, 0), (FFN, 4), (SMALL, 1), (RS, S_OUT, 0),),
+    GT_1: ((RS, IN_2, 3), (RS, S_IN_2, 0), (RS, S_IN, 1),),
+    GT_2: ((RS, S_DOWN, 1), (RS, S_GU, 1), (SMALL, 2), (RS, S_IN_2, 1),),
+    GT_3: ((RS, S_OUT, 1), (RS, S_IN, 2), (RS, S_DOWN, 2), (FFN, 5),),
+    GT_4: ((RS, S_GU, 2), (RS, S_IN_2, 2), (RS, S_OUT, 2),),
 }
 
 

time: 161 us -> 160 us (level)
  no operation moved by 1% of the time
where the time goes in v5:
time: 160 us
  Pallas kernels  159 us (99%)
    pallas_call x1, Pallas kernels, block(): pl.pallas_call(kernel, out_shape=(jax.ShapeDtypeStruct((128, 2048), BF16)...  156 us

profile of v5, /device:TPU:1, one launch (start us, length us, event | category | flops | bytes accessed | tf_op | source)
XLA Modules:
  0.0 159.9 jit_solution(5019060934999819113)
XLA Ops:
  0.7 156.3 %block.1 = (bf16[128,2048]{1,0:T(8,128)(2,1)}, bf16[128,2048]{1,0:T(8,128)(2,1)}, bf16[2,64,3200]{2,1,0:T(8,128)(2,1)}, f32[2,80,256]{2,1,0:T(8,128)}, f32[8,128]{1,0:T(8,128)}) custom-call(bf16[3,64,512]{2,1,0:T(8,128)(2,1)} %bitcast.7, bf16[64,512]{1,0:T(8,128)(2,1)} %refs_1_.1, bf16[64,1408]{1,0:T(8,128)(2,1)} %refs_2_.1, bf16[64,1408]{1,0:T(8,128)(2,1)} %refs_3_.1, ...), custom_call_target="tpu_custom_call" | custom-call | tf_op jit(solution)/shard_map/block/pallas_call | solution.py:1356
  156.9 3.0 %results.1 = (bf16[128,2048]{1,0:T(8,128)(2,1)}, bf16[128,2048]{1,0:T(8,128)(2,1)}, f32[1,64]{1,0:T(1,128)}, f32[3,64,512]{2,1,0:T(8,128)}, f32[3,3,512]{2,1,0:T...) custom-call(bf16[128,2048]{1,0:T(8,128)(2,1)} %get-tuple-element.33., ...), custom_call_target="tpu_custom_call" | custom-call | tf_op jit(solution)/shard_map/results/pallas_call | solution.py:1454

commit v6 on v5

--- a/solution.py
+++ b/solution.py
@@ -497,6 +497,7 @@
     gain_in = ((8, 128), F32)
     taps = ((8, 768), F32)
     keep = ((256, 256), F32)
+    tok_here = ((128, 2048), BF16)
     gy = ((256, 2048), BF16)
     n1 = ((272, 2048), BF16)
     n2 = ((256, 2048), BF16)
@@ -606,6 +607,10 @@
 
     my64 = span(c * 64, 64)
     my128 = span(c * 128, 128)
+    tok_copy = pltpu.make_async_copy(k.tok, k.tok_here, local.at[5])
+    cot_copy = pltpu.make_async_copy(k.cot, k.gy.at[my128], local.at[6])
+    tok_copy.start()
+    cot_copy.start()
     gather = []
     for n, (phase, split, parts) in enumerate(GATHERS):
         first = sum(len(group) for group in gather)
@@ -678,7 +683,7 @@
 
     gain_sib = remote(k.gain_in, k.gain_pair.at[c], S.gain_sib, R.gain_sib, r.sib)
     keep_sib = remote(k.keep.at[my128], k.keep.at[my128], S.keep_s, R.keep_s, r.sib)
-    gy_sib = remote(k.cot, k.gy.at[my128], S.gy_s, R.gy_s, r.sib)
+    gy_sib = remote(k.gy.at[my128], k.gy.at[my128], S.gy_s, R.gy_s, r.sib)
     def share(n):
         for h in range(2):
             weight_sib(n, h).start()
@@ -716,7 +721,7 @@
     gain_z.begin()
     k.gains_all[z] = k.gains_y[...]
     at(GAIN_Z)
-    k.gy[my128] = k.cot[...]
+    cot_copy.wait()
 
     channels = pl.ds(pl.multiple_of(c * 256, 256), 256)
     decay, angle = k.decay[:, channels], k.angle[:, channels]
@@ -741,9 +746,10 @@
 
     def norm_one(i):
         rows = span(i * 16, 16)
-        a = k.tok[rows, :].astype(F32)
+        a = k.tok_here[rows, :].astype(F32)
         s = lax.rsqrt(jnp.mean(a * a, axis=-1, keepdims=True) + EPSILON)
         k.n1[pl.ds(pl.multiple_of(16 + c * 128 + i * 16, 16), 16), :] = (a * s * k.gains[0:1, :]).astype(BF16)
+    tok_copy.wait()
     loop(8, norm_one)
 
     def n1_rows(c):
@@ -893,7 +899,7 @@
 
     def norm_two(i):
         rows = pl.ds(pl.multiple_of(i * 16, 16), 16)
-        a = k.tok[pl.ds(pl.multiple_of(x * 32 + i * 16, 16), 16), :].astype(F32) + s_mix.result(rows)
+        a = k.tok_here[pl.ds(pl.multiple_of(x * 32 + i * 16, 16), 16), :].astype(F32) + s_mix.result(rows)
         k.h[rows, :] = a
         s = lax.rsqrt(jnp.mean(a * a, axis=-1, keepdims=True) + EPSILON)
         k.n2[pl.ds(pl.multiple_of(own + i * 16, 16), 16), :] = (a * s * k.gains[1:2, :]).astype(BF16)
@@ -1266,7 +1272,7 @@
     def d_norm_one(i):
         rows = pl.ds(pl.multiple_of(i * 16, 16), 16)
         here = pl.ds(pl.multiple_of(x * 32 + i * 16, 16), 16)
-        a = k.tok[here, :].astype(F32)
+        a = k.tok_here[here, :].astype(F32)
         s = lax.rsqrt(jnp.mean(a * a, axis=-1, keepdims=True) + EPSILON)
         hat = a * s
         dn = s_dn1.result(rows)
@@ -1362,9 +1368,9 @@
             jax.ShapeDtypeStruct((2, 80, 256), F32),
             jax.ShapeDtypeStruct((8, 128), F32),
         ),
-        in_specs=[vmem] * len(arrays),
+        in_specs=[vmem] * 8 + [pl.BlockSpec(memory_space=pl.ANY)] * 2 + [vmem] * 5,
         out_specs=[pl.BlockSpec(memory_space=pl.ANY)] * 5,
-        scratch_shapes=[pltpu.VMEM(*value) for _, value in fields(Scratch)] + sems + [pltpu.SemaphoreType.DMA((5,))],
+        scratch_shapes=[pltpu.VMEM(*value) for _, value in fields(Scratch)] + sems + [pltpu.SemaphoreType.DMA((7,))],
         compiler_params=pltpu.CompilerParams(
             collective_id=0, has_side_effects=True, vmem_limit_bytes=63 * 2**20
         ),

time: 160 us -> 160 us (level)
  no operation moved by 1% of the time
where the time goes in v6:
time: 160 us
  Pallas kernels  159 us (99%)
    pallas_call x1, Pallas kernels, block(): pl.pallas_call(kernel, out_shape=(jax.ShapeDtypeStruct((128, 2048), BF16)...  156 us

profile of v6, /device:TPU:1, one launch (start us, length us, event | category | flops | bytes accessed | tf_op | source)
XLA Modules:
  0.0 159.6 jit_solution(5879369712779183774)
XLA Ops:
  0.7 156.0 %block.1 = (bf16[128,2048]{1,0:T(8,128)(2,1)}, bf16[128,2048]{1,0:T(8,128)(2,1)}, bf16[2,64,3200]{2,1,0:T(8,128)(2,1)}, f32[2,80,256]{2,1,0:T(8,128)}, f32[8,128]{1,0:T(8,128)}) custom-call(bf16[3,64,512]{2,1,0:T(8,128)(2,1)} %bitcast.7, bf16[64,512]{1,0:T(8,128)(2,1)} %refs_1_.1, bf16[64,1408]{1,0:T(8,128)(2,1)} %refs_2_.1, bf16[64,1408]{1,0:T(8,128)(2,1)} %refs_3_.1, ...), custom_call_target="tpu_custom_call" | custom-call | tf_op jit(solution)/shard_map/block/pallas_call | solution.py:1362
  156.7 3.0 %results.1 = (bf16[128,2048]{1,0:T(8,128)(2,1)}, bf16[128,2048]{1,0:T(8,128)(2,1)}, f32[1,64]{1,0:T(1,128)}, f32[3,64,512]{2,1,0:T(8,128)}, f32[3,3,512]{2,1,0:T...) custom-call(bf16[128,2048]{1,0:T(8,128)(2,1)} %get-tuple-element.33., ...), custom_call_target="tpu_custom_call" | custom-call | tf_op jit(solution)/shard_map/results/pallas_call | solution.py:1460
